TPU v7x, 256 devices: a whole 4x4x8 slice. The times are simulated.
256 devices in a mesh: gx: 4 (over y), gy: 8 (over z), gz: 8 (over x, core).
Axes of the slice: x: 4, y: 4, z: 8, core: 2. Of those that a mesh axis runs over, the one named last changes fastest.
Arguments:
- source: float32 [32, 512, 1024], P('gx', 'gy', 'gz'), may hold values from -8 to 8
- coefficient: float32 [32, 512, 1024], P('gx', 'gy', 'gz'), may hold values from 0.05 to 4
Outputs:
- posterior_mean: float32 [32, 512, 1024], P('gx', 'gy', 'gz')
- residual: float32 [32, 512, 1024], P('gx', 'gy', 'gz')
All inputs are finite; a program needn't handle non-finite values.
Results may differ from a plain program's by a relative error of at most 0.000024.
Values sent between devices are 32-bit elements; how exact they have to be, the bound alone decides.
No kernel may reach another device: no remote copies, remote signals or barrier semaphores. Data moves between devices by JAX's collectives and lax.ppermute only.
A program may use at most 128 MiB of HBM per device.

v0:
```python
import jax
import jax.numpy as jnp
from jax import lax
from jax.sharding import PartitionSpec as P

SWEEPS = 3
COARSE_SWEEPS = 6


THETA = 1.25
DELTA = 0.75


def padded_2(array, sides, width):
    for axis, dim in sides:
        peers, length = (lax.axis_size(axis), array.shape[dim])
        up = [(i, (i + 1) % peers) for i in range(peers - 1)]
        down = [(j, i) for i, j in up]
        last = lax.slice_in_dim(array, length - width, length, axis=dim)
        first = lax.slice_in_dim(array, 0, width, axis=dim)
        before = lax.ppermute(last, axis, up)
        after = lax.ppermute(first, axis, down)
        array = jnp.concatenate([before, array, after], axis=dim)
    return array


def stencil(padded, field, diag, scale):
    beside = padded[2:, 1:-1, 1:-1] + padded[:-2, 1:-1, 1:-1]
    beside = beside + padded[1:-1, 2:, 1:-1] + padded[1:-1, :-2, 1:-1]
    beside = beside + padded[1:-1, 1:-1, 2:] + padded[1:-1, 1:-1, :-2]
    return (diag + 6.0 * scale) * field - scale * beside


def smooth(sol, res, diag, scale, sweeps, extend):
    sigma = THETA / DELTA
    rho = 1.0 / sigma
    inverse = 1.0 / (diag + 6.0 * scale)
    step_dir = res * inverse / THETA
    for sweep in range(sweeps):
        sol = sol + step_dir
        res = res - stencil(extend(step_dir), step_dir, diag, scale)
        rho_new = 1.0 / (2.0 * sigma - rho)
        step_dir = rho_new * rho * step_dir + 2.0 * rho_new / DELTA * res * inverse
        rho = rho_new
    return (sol, res)


def coarsen(field):
    a, b, c = field.shape
    return field.reshape(a // 2, 2, b // 2, 2, c // 2, 2).mean(axis=(1, 3, 5))


def refine(field):
    return jnp.repeat(jnp.repeat(jnp.repeat(field, 2, 0), 2, 1), 2, 2)


def fine_extend(field):
    return padded_2(field, (("gx", 0), ("gy", 1), ("gz", 2)), 1)


def middle_spread(field):
    return padded_2(field, (("gx", 0), ("gy", 1), ("gz", 2)), 1)


def bottom_spread(field):
    return padded_2(field, (("gx", 0), ("gy", 1), ("gz", 2)), 1)


def lower_levels(res1, coef_mid, middle_extend, bottom_extend):
    coef_low = coarsen(coef_mid)
    sol1, res1 = smooth(jnp.zeros_like(res1), res1, coef_mid, 0.25, SWEEPS, middle_extend)
    res2 = coarsen(res1)
    sol2, unused = smooth(
        jnp.zeros_like(res2), res2, coef_low, 0.0625, COARSE_SWEEPS, bottom_extend
    )
    lifted = refine(sol2)
    sol1 = sol1 + lifted
    res1 = res1 - stencil(middle_extend(lifted), lifted, coef_mid, 0.25)
    sol1, res1 = smooth(sol1, res1, coef_mid, 0.25, SWEEPS, middle_extend)
    return sol1


def per_device(source, coefficient):
    sol0, res0 = smooth(jnp.zeros_like(source), source, coefficient, 1.0, SWEEPS, fine_extend)
    res1 = coarsen(res0)
    coef_mid = coarsen(coefficient)
    sol1 = lower_levels(res1, coef_mid, middle_spread, bottom_spread)
    lifted = refine(sol1)
    sol0 = sol0 + lifted
    res0 = res0 - stencil(fine_extend(lifted), lifted, coefficient, 1.0)
    sol0, res0 = smooth(sol0, res0, coefficient, 1.0, SWEEPS, fine_extend)
    return (sol0, res0)


def solution(mesh):
    return jax.shard_map(
        per_device,
        mesh=mesh,
        in_specs=(P("gx", "gy", "gz"), P("gx", "gy", "gz")),
        out_specs=(P("gx", "gy", "gz"), P("gx", "gy", "gz")),
        check_vma=False,
    )
```

profile of v0, /device:TPU:71, one launch (start us, length us, event | category | flops | bytes accessed | tf_op | source)
XLA Modules:
  0.0 559.1 jit_solution(1794327661069840265)
XLA Ops:
  21.4 5.2 collective-permute-start.4
  41.7 4.9 collective-permute-start.9
  51.5 5.9 %collective-permute-start.10 = (f32[10,66,1]{1,0,2:T(8,128)S(1)}, f32[10,66,1]{1,0,2:T(8,128)S(1)}, u32[]{:S(2)}, u32[]{:S(2)}) collective-permute-start(f32[10,66,1]{1,0,2:T(8,128)S(1)} %get-tuple-element.47), channel_id=1, source_target_pairs={{1,0},{2,1},{3,2},{4,3},{5,4},{6,5},{7,6},{9,8},{10,9},{11,10},{12... | collective-permute-start | bytes 7928 | tf_op jit(solution)/shard_map/ppermute | solution.py:22
  77.6 18.9 %reshape.72 = f32[4,2,32,2,64,2]{5,4,3,2,1,0:T(8,128)} reshape(f32[8,64,128]{2,1,0:T(8,128)} %param.3) | data formatting | bytes 524288 | tf_op jit(solution)/shard_map/reshape | solution.py:50
  96.5 7.0 %reduce_sum.37 = f32[4,32,64]{2,1,0:T(8,128)S(1)} reduce(f32[4,2,32,2,64,2]{5,4,3,2,1,0:T(8,128)} %reshape.72, f32[]{:T(128)} %constant.26.clone.1), dimensions={1,3,5}, to_apply=%region_1.0 | reduce | flops 57344 | bytes 294916 | tf_op jit(solution)/shard_map/reduce_sum | solution.py:50
  106.5 5.6 %collective-permute-start.16 = (f32[10,66,1]{1,0,2:T(8,128)}, f32[10,66,1]{1,0,2:T(8,128)}, u32[]{:S(2)}, u32[]{:S(2)}) collective-permute-start(f32[10,66,1]{1,0,2:T(8,128)} %get-tuple-element.45), channel_id=1, source_target_pairs={{1,0},{2,1},{3,2},{4,3},{5,4},{6,5},{7,6},{9,8},{10,9},{11,10},{12... | collective-permute-start | bytes 7928 | tf_op jit(solution)/shard_map/ppermute | solution.py:22
  121.3 18.1 %reshape.71 = f32[4,2,32,2,64,2]{5,4,3,2,1,0:T(8,128)} reshape(f32[8,64,128]{2,1,0:T(8,128)S(1)} %copy.187) | data formatting | bytes 524288 | tf_op jit(solution)/shard_map/reshape | solution.py:50
  139.4 7.0 %reduce_sum.36 = f32[4,32,64]{2,1,0:T(8,128)S(1)} reduce(f32[4,2,32,2,64,2]{5,4,3,2,1,0:T(8,128)} %reshape.71, f32[]{:T(128)} %constant.26.clone.1), dimensions={1,3,5}, to_apply=%region_0.0 | reduce | flops 57344 | bytes 294916 | tf_op jit(solution)/shard_map/reduce_sum | solution.py:50
  159.9 5.9 %collective-permute-start.22 = (f32[6,34,1]{2,1,0:T(8,128)S(1)}, f32[6,34,1]{2,1,0:T(8,128)S(1)}, u32[]{:S(2)}, u32[]{:S(2)}) collective-permute-start(f32[6,34,1]{2,1,0:T(8,128)S(1)} %get-tuple-element.103), channel_id=1, source_target_pairs={{1,0},{2,1},{3,2},{4,3},{5,4},{6,5},{7,6},{9,8},{10,9},{11,10},{12... | collective-permute-start | bytes 2456 | tf_op jit(solution)/shard_map/ppermute | solution.py:22
  183.9 7.7 %collective-permute-start.28 = (f32[6,34,1]{2,1,0:T(8,128)S(1)}, f32[6,34,1]{2,1,0:T(8,128)S(1)}, u32[]{:S(2)}, u32[]{:S(2)}) collective-permute-start(f32[6,34,1]{2,1,0:T(8,128)S(1)} %get-tuple-element.101), channel_id=1, source_target_pairs={{1,0},{2,1},{3,2},{4,3},{5,4},{6,5},{7,6},{9,8},{10,9},{11,10},{12... | collective-permute-start | bytes 2456 | tf_op jit(solution)/shard_map/ppermute | solution.py:22
  209.1 7.7 %collective-permute-start.34 = (f32[6,34,1]{2,1,0:T(8,128)}, f32[6,34,1]{2,1,0:T(8,128)S(1)}, u32[]{:S(2)}, u32[]{:S(2)}) collective-permute-start(f32[6,34,1]{2,1,0:T(8,128)} %get-tuple-element.99), channel_id=1, source_target_pairs={{1,0},{2,1},{3,2},{4,3},{5,4},{6,5},{7,6},{9,8},{10,9},{11,10},{12... | collective-permute-start | bytes 2456 | tf_op jit(solution)/shard_map/ppermute | solution.py:22
  242.4 5.9 %collective-permute-start.40 = (f32[4,18,1]{2,1,0:T(8,128)S(1)}, f32[4,18,1]{2,1,0:T(8,128)S(1)}, u32[]{:S(2)}, u32[]{:S(2)}) collective-permute-start(f32[4,18,1]{2,1,0:T(8,128)S(1)} %get-tuple-element.137), channel_id=1, source_target_pairs={{1,0},{2,1},{3,2},{4,3},{5,4},{6,5},{7,6},{9,8},{10,9},{11,10},{12... | collective-permute-start | bytes 872 | tf_op jit(solution)/shard_map/ppermute | solution.py:22
  264.8 7.1 %collective-permute-start.46 = (f32[4,18,1]{2,1,0:T(8,128)S(1)}, f32[4,18,1]{2,1,0:T(8,128)S(1)}, u32[]{:S(2)}, u32[]{:S(2)}) collective-permute-start(f32[4,18,1]{2,1,0:T(8,128)S(1)} %get-tuple-element.135), channel_id=1, source_target_pairs={{1,0},{2,1},{3,2},{4,3},{5,4},{6,5},{7,6},{9,8},{10,9},{11,10},{12... | collective-permute-start | bytes 872 | tf_op jit(solution)/shard_map/ppermute | solution.py:22
  288.4 7.1 %collective-permute-start.52 = (f32[4,18,1]{2,1,0:T(8,128)S(1)}, f32[4,18,1]{2,1,0:T(8,128)S(1)}, u32[]{:S(2)}, u32[]{:S(2)}) collective-permute-start(f32[4,18,1]{2,1,0:T(8,128)S(1)} %get-tuple-element.133), channel_id=1, source_target_pairs={{1,0},{2,1},{3,2},{4,3},{5,4},{6,5},{7,6},{9,8},{10,9},{11,10},{12... | collective-permute-start | bytes 872 | tf_op jit(solution)/shard_map/ppermute | solution.py:22
  312.1 7.1 %collective-permute-start.58 = (f32[4,18,1]{2,1,0:T(8,128)S(1)}, f32[4,18,1]{2,1,0:T(8,128)S(1)}, u32[]{:S(2)}, u32[]{:S(2)}) collective-permute-start(f32[4,18,1]{2,1,0:T(8,128)S(1)} %get-tuple-element.131), channel_id=1, source_target_pairs={{1,0},{2,1},{3,2},{4,3},{5,4},{6,5},{7,6},{9,8},{10,9},{11,10},{12... | collective-permute-start | bytes 872 | tf_op jit(solution)/shard_map/ppermute | solution.py:22
  335.7 7.1 %collective-permute-start.64 = (f32[4,18,1]{2,1,0:T(8,128)S(1)}, f32[4,18,1]{2,1,0:T(8,128)S(1)}, u32[]{:S(2)}, u32[]{:S(2)}) collective-permute-start(f32[4,18,1]{2,1,0:T(8,128)S(1)} %get-tuple-element.129), channel_id=1, source_target_pairs={{1,0},{2,1},{3,2},{4,3},{5,4},{6,5},{7,6},{9,8},{10,9},{11,10},{12... | collective-permute-start | bytes 872 | tf_op jit(solution)/shard_map/ppermute | solution.py:22
  359.8 6.8 %collective-permute-start.70 = (f32[6,34,1]{2,1,0:T(8,128)S(1)}, f32[6,34,1]{2,1,0:T(8,128)S(1)}, u32[]{:S(2)}, u32[]{:S(2)}) collective-permute-start(f32[6,34,1]{2,1,0:T(8,128)S(1)} %get-tuple-element.97), channel_id=1, source_target_pairs={{1,0},{2,1},{3,2},{4,3},{5,4},{6,5},{7,6},{9,8},{10,9},{11,10},{12... | collective-permute-start | bytes 2456 | tf_op jit(solution)/shard_map/ppermute | solution.py:22
  385.8 8.0 %collective-permute-start.76 = (f32[6,34,1]{2,1,0:T(8,128)S(1)}, f32[6,34,1]{2,1,0:T(8,128)S(1)}, u32[]{:S(2)}, u32[]{:S(2)}) collective-permute-start(f32[6,34,1]{2,1,0:T(8,128)S(1)} %get-tuple-element.95), channel_id=1, source_target_pairs={{1,0},{2,1},{3,2},{4,3},{5,4},{6,5},{7,6},{9,8},{10,9},{11,10},{12... | collective-permute-start | bytes 2456 | tf_op jit(solution)/shard_map/ppermute | solution.py:22
  410.6 7.7 %collective-permute-start.82 = (f32[6,34,1]{2,1,0:T(8,128)S(1)}, f32[6,34,1]{2,1,0:T(8,128)S(1)}, u32[]{:S(2)}, u32[]{:S(2)}) collective-permute-start(f32[6,34,1]{2,1,0:T(8,128)S(1)} %get-tuple-element.93), channel_id=1, source_target_pairs={{1,0},{2,1},{3,2},{4,3},{5,4},{6,5},{7,6},{9,8},{10,9},{11,10},{12... | collective-permute-start | bytes 2456 | tf_op jit(solution)/shard_map/ppermute | solution.py:22
  424.1 4.6 collective-permute-start.85
  442.5 7.8 %collective-permute-start.88 = (f32[10,66,1]{1,0,2:T(8,128)}, f32[10,66,1]{1,0,2:T(8,128)}, u32[]{:S(2)}, u32[]{:S(2)}) collective-permute-start(f32[10,66,1]{1,0,2:T(8,128)} %get-tuple-element.43), channel_id=1, source_target_pairs={{1,0},{2,1},{3,2},{4,3},{5,4},{6,5},{7,6},{9,8},{10,9},{11,10},{12... | collective-permute-start | bytes 7928 | tf_op jit(solution)/shard_map/ppermute | solution.py:22
  479.4 6.5 %collective-permute-start.94 = (f32[10,66,1]{1,0,2:T(8,128)}, f32[10,66,1]{1,0,2:T(8,128)}, u32[]{:S(2)}, u32[]{:S(2)}) collective-permute-start(f32[10,66,1]{1,0,2:T(8,128)} %get-tuple-element.41), channel_id=1, source_target_pairs={{1,0},{2,1},{3,2},{4,3},{5,4},{6,5},{7,6},{9,8},{10,9},{11,10},{12... | collective-permute-start | bytes 7928 | tf_op jit(solution)/shard_map/ppermute | solution.py:22
  513.2 6.7 %collective-permute-start.100 = (f32[10,66,1]{1,0,2:T(8,128)}, f32[10,66,1]{1,0,2:T(8,128)}, u32[]{:S(2)}, u32[]{:S(2)}) collective-permute-start(f32[10,66,1]{1,0,2:T(8,128)} %get-tuple-element.39), channel_id=1, source_target_pairs={{1,0},{2,1},{3,2},{4,3},{5,4},{6,5},{7,6},{9,8},{10,9},{11,10},{12... | collective-permute-start | bytes 7928 | tf_op jit(solution)/shard_map/ppermute | solution.py:22
  545.7 5.9 %collective-permute-start.106 = (f32[10,66,1]{1,0,2:T(8,128)}, f32[10,66,1]{1,0,2:T(8,128)S(1)}, u32[]{:S(2)}, u32[]{:S(2)}) collective-permute-start(f32[10,66,1]{1,0,2:T(8,128)} %get-tuple-element.37), channel_id=1, source_target_pairs={{1,0},{2,1},{3,2},{4,3},{5,4},{6,5},{7,6},{9,8},{10,9},{11,10},{12... | collective-permute-start | bytes 7928 | tf_op jit(solution)/shard_map/ppermute | solution.py:22
  (401 shorter events, 374.6 us)
Async XLA Ops:
  21.4 9.3 %collective-permute-start.4 = (f32[10,66,1]{1,0,2:T(8,128)S(1)}, f32[10,66,1]{1,0,2:T(8,128)S(1)}, u32[]{:S(2)}, u32[]{:S(2)}) collective-permute-start(f32[10,66,1]{1,0,2:T(8,128)S(1)} %get-tuple-element.49), channel_id=1, source_target_pairs={{1,0},{2,1},{3,2},{4,3},{5,4},{6,5},{7,6},{9,8},{10,9},{11,10},{12... | collective-permute-start | bytes 7928 | tf_op jit(solution)/shard_map/ppermute | solution.py:22
  41.7 6.8 %collective-permute-start.9 = (f32[10,1,128]{2,1,0:T(1,128)S(1)}, f32[10,1,128]{2,1,0:T(1,128)S(1)}, u32[]{:S(2)}, u32[]{:S(2)}) collective-permute-start(f32[10,1,128]{2,1,0:T(1,128)S(1)} %get-tuple-element.85), channel_id=1, source_target_pairs={{0,8},{8,16},{16,24},{24,32},{32,40},{40,48},{48,56},{1,9},{9,17},... | collective-permute-start | bytes 15368 | tf_op jit(solution)/shard_map/ppermute | solution.py:21
  51.5 10.0 %collective-permute-start.10 = (f32[10,66,1]{1,0,2:T(8,128)S(1)}, f32[10,66,1]{1,0,2:T(8,128)S(1)}, u32[]{:S(2)}, u32[]{:S(2)}) collective-permute-start(f32[10,66,1]{1,0,2:T(8,128)S(1)} %get-tuple-element.47), channel_id=1, source_target_pairs={{1,0},{2,1},{3,2},{4,3},{5,4},{6,5},{7,6},{9,8},{10,9},{11,10},{12... | collective-permute-start | bytes 7928 | tf_op jit(solution)/shard_map/ppermute | solution.py:22
  72.3 31.2 %collective-permute-start.15 = (f32[10,1,128]{2,1,0:T(1,128)S(1)}, f32[10,1,128]{2,1,0:T(1,128)S(1)}, u32[]{:S(2)}, u32[]{:S(2)}) collective-permute-start(f32[10,1,128]{2,1,0:T(1,128)S(1)} %get-tuple-element.81), channel_id=1, source_target_pairs={{0,8},{8,16},{16,24},{24,32},{32,40},{40,48},{48,56},{1,9},{9,17},... | collective-permute-start | bytes 15368 | tf_op jit(solution)/shard_map/ppermute | solution.py:21
  75.2 28.3 %collective-permute-start.14 = (f32[10,1,128]{2,1,0:T(1,128)S(1)}, f32[10,1,128]{2,1,0:T(1,128)S(1)}, u32[]{:S(2)}, u32[]{:S(2)}) collective-permute-start(f32[10,1,128]{2,1,0:T(1,128)S(1)} %get-tuple-element.82), channel_id=1, source_target_pairs={{8,0},{16,8},{24,16},{32,24},{40,32},{48,40},{56,48},{9,1},{17,9},... | collective-permute-start | bytes 15368 | tf_op jit(solution)/shard_map/ppermute | solution.py:22
  106.5 11.8 %collective-permute-start.16 = (f32[10,66,1]{1,0,2:T(8,128)}, f32[10,66,1]{1,0,2:T(8,128)}, u32[]{:S(2)}, u32[]{:S(2)}) collective-permute-start(f32[10,66,1]{1,0,2:T(8,128)} %get-tuple-element.45), channel_id=1, source_target_pairs={{1,0},{2,1},{3,2},{4,3},{5,4},{6,5},{7,6},{9,8},{10,9},{11,10},{12... | collective-permute-start | bytes 7928 | tf_op jit(solution)/shard_map/ppermute | solution.py:22
  159.9 7.2 %collective-permute-start.22 = (f32[6,34,1]{2,1,0:T(8,128)S(1)}, f32[6,34,1]{2,1,0:T(8,128)S(1)}, u32[]{:S(2)}, u32[]{:S(2)}) collective-permute-start(f32[6,34,1]{2,1,0:T(8,128)S(1)} %get-tuple-element.103), channel_id=1, source_target_pairs={{1,0},{2,1},{3,2},{4,3},{5,4},{6,5},{7,6},{9,8},{10,9},{11,10},{12... | collective-permute-start | bytes 2456 | tf_op jit(solution)/shard_map/ppermute | solution.py:22
  183.9 9.1 %collective-permute-start.28 = (f32[6,34,1]{2,1,0:T(8,128)S(1)}, f32[6,34,1]{2,1,0:T(8,128)S(1)}, u32[]{:S(2)}, u32[]{:S(2)}) collective-permute-start(f32[6,34,1]{2,1,0:T(8,128)S(1)} %get-tuple-element.101), channel_id=1, source_target_pairs={{1,0},{2,1},{3,2},{4,3},{5,4},{6,5},{7,6},{9,8},{10,9},{11,10},{12... | collective-permute-start | bytes 2456 | tf_op jit(solution)/shard_map/ppermute | solution.py:22
  209.1 14.4 %collective-permute-start.34 = (f32[6,34,1]{2,1,0:T(8,128)}, f32[6,34,1]{2,1,0:T(8,128)S(1)}, u32[]{:S(2)}, u32[]{:S(2)}) collective-permute-start(f32[6,34,1]{2,1,0:T(8,128)} %get-tuple-element.99), channel_id=1, source_target_pairs={{1,0},{2,1},{3,2},{4,3},{5,4},{6,5},{7,6},{9,8},{10,9},{11,10},{12... | collective-permute-start | bytes 2456 | tf_op jit(solution)/shard_map/ppermute | solution.py:22
  216.9 6.7 %collective-permute-start.35 = (f32[6,34,1]{2,1,0:T(8,128)S(1)}, f32[6,34,1]{2,1,0:T(8,128)S(1)}, u32[]{:S(2)}, u32[]{:S(2)}) collective-permute-start(f32[6,34,1]{2,1,0:T(8,128)S(1)} %get-tuple-element.100), channel_id=1, source_target_pairs={{0,1},{1,2},{2,3},{3,4},{4,5},{5,6},{6,7},{8,9},{9,10},{10,11},{11... | collective-permute-start | bytes 2456 | tf_op jit(solution)/shard_map/ppermute | solution.py:21
  242.4 7.2 %collective-permute-start.40 = (f32[4,18,1]{2,1,0:T(8,128)S(1)}, f32[4,18,1]{2,1,0:T(8,128)S(1)}, u32[]{:S(2)}, u32[]{:S(2)}) collective-permute-start(f32[4,18,1]{2,1,0:T(8,128)S(1)} %get-tuple-element.137), channel_id=1, source_target_pairs={{1,0},{2,1},{3,2},{4,3},{5,4},{6,5},{7,6},{9,8},{10,9},{11,10},{12... | collective-permute-start | bytes 872 | tf_op jit(solution)/shard_map/ppermute | solution.py:22
  264.8 8.4 %collective-permute-start.46 = (f32[4,18,1]{2,1,0:T(8,128)S(1)}, f32[4,18,1]{2,1,0:T(8,128)S(1)}, u32[]{:S(2)}, u32[]{:S(2)}) collective-permute-start(f32[4,18,1]{2,1,0:T(8,128)S(1)} %get-tuple-element.135), channel_id=1, source_target_pairs={{1,0},{2,1},{3,2},{4,3},{5,4},{6,5},{7,6},{9,8},{10,9},{11,10},{12... | collective-permute-start | bytes 872 | tf_op jit(solution)/shard_map/ppermute | solution.py:22
  288.4 8.4 %collective-permute-start.52 = (f32[4,18,1]{2,1,0:T(8,128)S(1)}, f32[4,18,1]{2,1,0:T(8,128)S(1)}, u32[]{:S(2)}, u32[]{:S(2)}) collective-permute-start(f32[4,18,1]{2,1,0:T(8,128)S(1)} %get-tuple-element.133), channel_id=1, source_target_pairs={{1,0},{2,1},{3,2},{4,3},{5,4},{6,5},{7,6},{9,8},{10,9},{11,10},{12... | collective-permute-start | bytes 872 | tf_op jit(solution)/shard_map/ppermute | solution.py:22
  312.1 8.4 %collective-permute-start.58 = (f32[4,18,1]{2,1,0:T(8,128)S(1)}, f32[4,18,1]{2,1,0:T(8,128)S(1)}, u32[]{:S(2)}, u32[]{:S(2)}) collective-permute-start(f32[4,18,1]{2,1,0:T(8,128)S(1)} %get-tuple-element.131), channel_id=1, source_target_pairs={{1,0},{2,1},{3,2},{4,3},{5,4},{6,5},{7,6},{9,8},{10,9},{11,10},{12... | collective-permute-start | bytes 872 | tf_op jit(solution)/shard_map/ppermute | solution.py:22
  335.7 8.4 %collective-permute-start.64 = (f32[4,18,1]{2,1,0:T(8,128)S(1)}, f32[4,18,1]{2,1,0:T(8,128)S(1)}, u32[]{:S(2)}, u32[]{:S(2)}) collective-permute-start(f32[4,18,1]{2,1,0:T(8,128)S(1)} %get-tuple-element.129), channel_id=1, source_target_pairs={{1,0},{2,1},{3,2},{4,3},{5,4},{6,5},{7,6},{9,8},{10,9},{11,10},{12... | collective-permute-start | bytes 872 | tf_op jit(solution)/shard_map/ppermute | solution.py:22
  359.8 8.1 %collective-permute-start.70 = (f32[6,34,1]{2,1,0:T(8,128)S(1)}, f32[6,34,1]{2,1,0:T(8,128)S(1)}, u32[]{:S(2)}, u32[]{:S(2)}) collective-permute-start(f32[6,34,1]{2,1,0:T(8,128)S(1)} %get-tuple-element.97), channel_id=1, source_target_pairs={{1,0},{2,1},{3,2},{4,3},{5,4},{6,5},{7,6},{9,8},{10,9},{11,10},{12... | collective-permute-start | bytes 2456 | tf_op jit(solution)/shard_map/ppermute | solution.py:22
  385.8 9.3 %collective-permute-start.76 = (f32[6,34,1]{2,1,0:T(8,128)S(1)}, f32[6,34,1]{2,1,0:T(8,128)S(1)}, u32[]{:S(2)}, u32[]{:S(2)}) collective-permute-start(f32[6,34,1]{2,1,0:T(8,128)S(1)} %get-tuple-element.95), channel_id=1, source_target_pairs={{1,0},{2,1},{3,2},{4,3},{5,4},{6,5},{7,6},{9,8},{10,9},{11,10},{12... | collective-permute-start | bytes 2456 | tf_op jit(solution)/shard_map/ppermute | solution.py:22
  410.6 9.1 %collective-permute-start.82 = (f32[6,34,1]{2,1,0:T(8,128)S(1)}, f32[6,34,1]{2,1,0:T(8,128)S(1)}, u32[]{:S(2)}, u32[]{:S(2)}) collective-permute-start(f32[6,34,1]{2,1,0:T(8,128)S(1)} %get-tuple-element.93), channel_id=1, source_target_pairs={{1,0},{2,1},{3,2},{4,3},{5,4},{6,5},{7,6},{9,8},{10,9},{11,10},{12... | collective-permute-start | bytes 2456 | tf_op jit(solution)/shard_map/ppermute | solution.py:22
  422.1 7.7 %collective-permute-start.84 = (f32[1,64,128]{1,0,2:T(1,128)S(1)}, f32[1,64,128]{1,0,2:T(1,128)S(1)}, u32[]{:S(2)}, u32[]{:S(2)}) collective-permute-start(f32[1,64,128]{1,0,2:T(1,128)S(1)} %bitcast.48), channel_id=1, source_target_pairs={{64,0},{128,64},{192,128},{65,1},{129,65},{193,129},{66,2},{130,66... | collective-permute-start | bytes 98312 | tf_op jit(solution)/shard_map/ppermute | solution.py:22
  442.5 13.9 %collective-permute-start.88 = (f32[10,66,1]{1,0,2:T(8,128)}, f32[10,66,1]{1,0,2:T(8,128)}, u32[]{:S(2)}, u32[]{:S(2)}) collective-permute-start(f32[10,66,1]{1,0,2:T(8,128)} %get-tuple-element.43), channel_id=1, source_target_pairs={{1,0},{2,1},{3,2},{4,3},{5,4},{6,5},{7,6},{9,8},{10,9},{11,10},{12... | collective-permute-start | bytes 7928 | tf_op jit(solution)/shard_map/ppermute | solution.py:22
  479.4 9.8 %collective-permute-start.94 = (f32[10,66,1]{1,0,2:T(8,128)}, f32[10,66,1]{1,0,2:T(8,128)}, u32[]{:S(2)}, u32[]{:S(2)}) collective-permute-start(f32[10,66,1]{1,0,2:T(8,128)} %get-tuple-element.41), channel_id=1, source_target_pairs={{1,0},{2,1},{3,2},{4,3},{5,4},{6,5},{7,6},{9,8},{10,9},{11,10},{12... | collective-permute-start | bytes 7928 | tf_op jit(solution)/shard_map/ppermute | solution.py:22
  513.2 12.7 %collective-permute-start.100 = (f32[10,66,1]{1,0,2:T(8,128)}, f32[10,66,1]{1,0,2:T(8,128)}, u32[]{:S(2)}, u32[]{:S(2)}) collective-permute-start(f32[10,66,1]{1,0,2:T(8,128)} %get-tuple-element.39), channel_id=1, source_target_pairs={{1,0},{2,1},{3,2},{4,3},{5,4},{6,5},{7,6},{9,8},{10,9},{11,10},{12... | collective-permute-start | bytes 7928 | tf_op jit(solution)/shard_map/ppermute | solution.py:22
  537.3 7.2 %collective-permute-start.105 = (f32[10,1,128]{2,1,0:T(1,128)S(1)}, f32[10,1,128]{2,1,0:T(1,128)S(1)}, u32[]{:S(2)}, u32[]{:S(2)}) collective-permute-start(f32[10,1,128]{2,1,0:T(1,128)S(1)} %get-tuple-element.65), channel_id=1, source_target_pairs={{0,8},{8,16},{16,24},{24,32},{32,40},{40,48},{48,56},{1,9},{9,17},... | collective-permute-start | bytes 15368 | tf_op jit(solution)/shard_map/ppermute | solution.py:21
  545.7 7.7 %collective-permute-start.106 = (f32[10,66,1]{1,0,2:T(8,128)}, f32[10,66,1]{1,0,2:T(8,128)S(1)}, u32[]{:S(2)}, u32[]{:S(2)}) collective-permute-start(f32[10,66,1]{1,0,2:T(8,128)} %get-tuple-element.37), channel_id=1, source_target_pairs={{1,0},{2,1},{3,2},{4,3},{5,4},{6,5},{7,6},{9,8},{10,9},{11,10},{12... | collective-permute-start | bytes 7928 | tf_op jit(solution)/shard_map/ppermute | solution.py:22
  (99 other events, 589.0 us)
where the time goes:
time: 566 us; the launch traced here: 559 us
  starting transfers between devices  309 us (55%)
  waiting for transfers between devices  105 us (19%)
  local copies, waits for them, and re-layouts  93.4 us (17%)
  other arithmetic  48.5 us (9%)
    ppermute x54, starting transfers between devices, padded_2(): after = lax.ppermute(first, axis, down)  187 us
    ppermute x54, starting transfers between devices, padded_2(): before = lax.ppermute(last, axis, up)  122 us
    ppermute x54, waiting for transfers between devices, padded_2(): after = lax.ppermute(first, axis, down)  84.3 us
    reshape x3, local copies, waits for them, and re-layouts, coarsen(): return field.reshape(a // 2, 2, b // 2, 2, c // 2, 2).mean(axis=(1, 3, 5))  40.5 us
    unnamed x48, local copies, waits for them, and re-layouts  26.3 us
    ppermute x54, waiting for transfers between devices, padded_2(): before = lax.ppermute(last, axis, up)  20.9 us
    reduce_sum x4, other arithmetic, coarsen(): return field.reshape(a // 2, 2, b // 2, 2, c // 2, 2).mean(axis=(1, 3, 5))  17.6 us
  transfers between devices with their start and end apart: 108, of which 44 were waited for; matrix products, arithmetic and copies ran while one was open for 10% of the time, Pallas kernels for 0%

commit v1 on v0

v1 whole, which is shorter than its diff:
```python
import jax
import jax.numpy as jnp
from jax import lax
from jax.experimental import pallas as pl
from jax.experimental.pallas import tpu as pltpu
from jax.sharding import PartitionSpec as P

SWEEPS = 3
COARSE_SWEEPS = 6
THETA = 1.25
DELTA = 0.75
F32 = jnp.float32
EXACT = lax.Precision.HIGHEST

XH = 3
NX0, NY0, NZ0 = 8, 64, 128
NXE = NX0 + 2 * XH
W = 9
R0 = 88
Q0 = 72
R1 = 40
Q1 = 48
R2 = 32
VM = 60 * 1024 * 1024


def coefficients(count):
    sigma = THETA / DELTA
    rho = 1.0 / sigma
    pairs = []
    for _ in range(count):
        rho_new = 1.0 / (2.0 * sigma - rho)
        pairs.append((rho_new * rho, 2.0 * rho_new / DELTA))
        rho = rho_new
    return pairs


def turn(value, shift, axis):
    return pltpu.roll(value, shift % value.shape[axis], axis)


def beside(value):
    return (turn(value, 1, 0) + turn(value, -1, 0)) + (turn(value, 1, 1) + turn(value, -1, 1))


def rows_of(shape):
    return lax.broadcasted_iota(jnp.int32, shape, 0)


def lanes_of(shape):
    return lax.broadcasted_iota(jnp.int32, shape, 1)


def inside_yz(shape, own_rows, split_row, own_lanes, split_lane):
    gy, gz = lax.axis_index("gy"), lax.axis_index("gz")
    last_y, last_z = lax.axis_size("gy") - 1, lax.axis_size("gz") - 1
    row, lane = rows_of(shape), lanes_of(shape)
    up_y, down_y = (gy < last_y).astype(jnp.int32), (gy > 0).astype(jnp.int32)
    up_z, down_z = (gz < last_z).astype(jnp.int32), (gz > 0).astype(jnp.int32)
    in_y = jnp.where(row < own_rows, 1, jnp.where(row < split_row, up_y, down_y))
    in_z = jnp.where(lane < own_lanes, 1, jnp.where(lane < split_lane, up_z, down_z))
    return (in_y * in_z) > 0


def dot(a, b):
    return jnp.dot(a, b, precision=EXACT, preferred_element_type=F32)


def call(body, outs, scratch, *args):
    vmem = pl.BlockSpec(memory_space=pltpu.VMEM)
    return pl.pallas_call(
        body,
        out_shape=[jax.ShapeDtypeStruct(s, F32) for s in outs],
        in_specs=[vmem] * len(args),
        out_specs=[vmem] * len(outs),
        scratch_shapes=[pltpu.VMEM(s, F32) for s in scratch],
        compiler_params=pltpu.CompilerParams(vmem_limit_bytes=VM),
    )(*args)


def ring(value, axis, shift):
    size = lax.axis_size(axis)
    return lax.ppermute(value, axis, [(i, (i + shift) % size) for i in range(size)])


def plane_of(own, low, high, which, x):
    if x < XH:
        return low.at[which * XH + x]
    if x < XH + NX0:
        return own[which].at[x - XH]
    return high.at[which * XH + x - XH - NX0]


def pack_y(s, c, low, high, up, down):
    for a in range(2):
        for x in range(NXE):
            src = plane_of((s, c), low, high, a, x)
            at = a * NXE + x
            up[at * 8 : at * 8 + 8, :] = src[56:64, :]
            down[at * 8 : at * 8 + 8, :] = src[0:8, :]
            up[224 + at : 225 + at, :] = src[55:56, :]
            down[224 + at : 225 + at, :] = src[8:9, :]
    up[252:256, :] = jnp.zeros((4, 128), F32)
    down[252:256, :] = jnp.zeros((4, 128), F32)


def pack_z(s, c, low, high, below, above, main, up, down):
    lane = lanes_of((R0, 128))
    for a in range(2):
        ups = jnp.zeros((R0, 128), F32)
        downs = jnp.zeros((R0, 128), F32)
        for x in range(NXE):
            src = plane_of((s, c), low, high, a, x)
            at = a * NXE + x
            main[a, x, 0:64, :] = src[...]
            main[a, x, 64:72, :] = above[at * 8 : at * 8 + 8, :]
            main[a, x, 72:80, :] = jnp.zeros((8, 128), F32)
            main[a, x, 72:73, :] = above[224 + at : 225 + at, :]
            main[a, x, 79:80, :] = below[224 + at : 225 + at, :]
            main[a, x, 80:88, :] = below[at * 8 : at * 8 + 8, :]
            plane = main[a, x]
            here = (lane >= W * x) & (lane < W * x + W)
            ups = jnp.where(here, turn(plane, W * x - (128 - W), 1), ups)
            downs = jnp.where(here, turn(plane, W * x, 1), downs)
        up[a] = ups
        down[a] = downs


def fine_sweep(src, dst, res, diag, inverse, first, stop, pair, also):
    def body(x, carry):
        d = src[x]
        near = beside(d) + (src[x - 1] + src[x + 1])
        r = res[x] - (diag[x] * d - near)
        res[x] = r
        also(x, d)
        if pair is not None:
            dst[x] = pair[0] * d + (pair[1] * inverse[x]) * r
        return carry

    lax.fori_loop(first, stop, body, 0)


def to_q0(ref, x):
    tail = jnp.where(rows_of((8, 256)) < 4, ref[x, 64:72, :], ref[x, 80:88, :])
    return ref[x, 0:64, :], tail


def fine_before(
    main, below, above, sol, res_q, diag_q, inv_q, msg2, msg_up, msg_down, res, diag, inv, da, db
):
    lane = lanes_of((R0, 128))
    for a in range(2):
        left, right = below[a], above[a]
        for x in range(NXE):
            side = jnp.where(lane < W, turn(right, -W * x, 1), 0.0)
            side = jnp.where(lane >= 128 - W, turn(left, 128 - W - W * x, 1), side)
            ref = (res, diag)[a]
            ref[x, :, 0:128] = main[a, x]
            ref[x, :, 128:256] = side
    row40, row88 = rows_of((R1, R0)), lanes_of((R1, R0))
    fold_y = jnp.where(row88 // 2 == jnp.where(row40 < 36, row40, row40 + 4), 0.125, 0.0).astype(F32)
    fold_z = jnp.where(rows_of((256, 128)) // 2 == lanes_of((256, 128)), 1.0, 0.0).astype(F32)

    def fold(ref, i):
        both = ref[XH + 2 * i] + ref[XH + 2 * i + 1]
        return dot(fold_y, dot(both, fold_z))

    coef1 = [fold(diag, i) for i in range(4)]

    gx = lax.axis_index("gx")
    in_yz = inside_yz((R0, 256), 64, 76, 128, 192)
    low_x, high_x = gx > 0, gx < lax.axis_size("gx") - 1

    def start(x, carry):
        g = diag[x] + 6.0
        diag[x] = g
        here = ((x >= XH) | low_x) & ((x < XH + NX0) | high_x)
        inverse = jnp.where(in_yz & here, 1.0 / g, 0.0)
        inv[x] = inverse
        da[x] = res[x] * inverse * (1.0 / THETA)
        top, tail = to_q0(diag, x)
        diag_q[x, 0:64, :] = top
        diag_q[x, 64:72, :] = tail
        top, tail = to_q0(inv, x)
        inv_q[x, 0:64, :] = top
        inv_q[x, 64:72, :] = tail
        return carry

    lax.fori_loop(0, NXE, start, 0)

    def add(first):
        def put(x, d):
            own = d[0:64, 0:128]
            at = jnp.clip(x - XH, 0, NX0 - 1)
            if first:
                sol[at] = own
            else:
                inside = ((x >= XH) & (x < XH + NX0)).astype(F32)
                sol[at] += inside * own

        return put

    pairs = coefficients(SWEEPS)
    buffers = (da, db)
    for k in range(SWEEPS):
        src, dst = buffers[k % 2], buffers[(k + 1) % 2]
        last = k == SWEEPS - 1

        def nothing(x, d):
            return None

        fine_sweep(src, dst, res, diag, inv, k + 1, NXE - 1 - k, None if last else pairs[k], nothing)

        def gather(x, carry):
            own = src[XH + x, 0:64, 0:128]
            sol[x] = own if k == 0 else sol[x] + own
            return carry

        lax.fori_loop(0, NX0, gather, 0)

    def keep(x, carry):
        top, tail = to_q0(res, XH + x)
        res_q[x, 0:64, :] = top
        res_q[x, 64:72, :] = tail
        return carry

    lax.fori_loop(0, NX0, keep, 0)

    lane40 = lanes_of((R1, 128))
    halo = jnp.zeros((R1, 128), F32)
    for i in range(4):
        r1, c1 = fold(res, i), coef1[i]
        both = jnp.where(lane40 < 64, r1, turn(c1, 64, 1))
        for msg in (msg2, msg_up, msg_down):
            msg[i * R1 : i * R1 + R1, :] = both
        for a, v in ((0, r1), (1, c1)):
            base = (a * 4 + i) * 8
            halo = jnp.where((lane40 >= base) & (lane40 < base + 4), turn(v, base - 64, 1), halo)
            halo = jnp.where((lane40 >= base + 4) & (lane40 < base + 8), turn(v, base + 4 - 124, 1), halo)
    msg2[160:200, :] = halo
    lane72 = lanes_of((Q0, 128))
    for msg, first in ((msg_up, NX0 - XH), (msg_down, 0)):
        side = jnp.zeros((Q0, 128), F32)
        for i in range(XH):
            msg[160 + i * Q0 : 160 + i * Q0 + Q0, :] = res_q[first + i, :, 0:128]
            v = res_q[first + i, :, 128:256]
            base = 64 + 6 * i
            side = jnp.where((lane72 >= base) & (lane72 < base + 3), turn(v, base, 1), side)
            side = jnp.where((lane72 >= base + 3) & (lane72 < base + 6), turn(v, base + 3 - 125, 1), side)
        at = 160 + XH * Q0
        msg[at : at + R1, :] = jnp.where(lane40 < 64, halo, side[0:R1])
        msg[at + R1 : at + Q0, :] = side[R1:Q0]


def line_sweep(src, dst, res, diag, inverse, planes, scale, pair):
    def body(x, carry):
        d = src[x + 1]
        near = beside(d) + (src[x] + src[x + 2])
        r = res[x] - (diag[x] * d - scale * near)
        res[x] = r
        if pair is not None:
            dst[x + 1] = pair[0] * d + (pair[1] * inverse[x]) * r
        return carry

    lax.fori_loop(0, planes, body, 0, unroll=2)


def middle_before(own, low, high, far, res, sol, coef, low_res, low_coef, up, down, diag, inv, da, db):
    gx = lax.axis_index("gx")
    size = lax.axis_size("gx")
    lane40 = lanes_of((R1, 128))
    for msg, shift, side_at in ((own, 0, 160), (low, 3, 160 + XH * Q0), (high, 1, 160 + XH * Q0), (far, 2, 160)):
        place = lax.rem(gx + shift, size) * 4
        side = msg[side_at : side_at + R1, :]
        for i in range(4):
            both = msg[i * R1 : i * R1 + R1, :]
            for a, ref in ((0, res), (1, coef)):
                base = (a * 4 + i) * 8
                v = both if a == 0 else turn(both, 64, 1)
                v = jnp.where(lane40 < 64, v, turn(side, 64 - base, 1))
                v = jnp.where(lane40 < 68, v, 0.0)
                v = jnp.where(lane40 < 124, v, turn(side, 124 - base - 4, 1))
                ref[place + i] = v
    in_yz = inside_yz((R1, 128), 32, 36, 64, 96)
    empty = jnp.zeros((R1, 128), F32)
    for buffer in (da, db):
        buffer[0] = empty
        buffer[17] = empty

    def start(x, carry):
        g = coef[x] + 1.5
        diag[x] = g
        inverse = jnp.where(in_yz, 1.0 / g, 0.0)
        inv[x] = inverse
        d = res[x] * inverse * (1.0 / THETA)
        da[x + 1] = d
        sol[x] = d
        return carry

    lax.fori_loop(0, 16, start, 0)
    pairs = coefficients(SWEEPS)
    buffers = (da, db)
    for k in range(SWEEPS):
        src, dst = buffers[k % 2], buffers[(k + 1) % 2]
        line_sweep(src, dst, res, diag, inv, 16, 0.25, pairs[k] if k < SWEEPS - 1 else None)
        if k < SWEEPS - 1:

            def gather(x, carry):
                sol[x] += dst[x + 1]
                return carry

            lax.fori_loop(0, 16, gather, 0, unroll=2)
    fold_y = jnp.where(lanes_of((16, R1)) // 2 == rows_of((16, R1)), 0.125, 0.0).astype(F32)
    fold_z = jnp.where(
        (rows_of((128, 128)) // 2 == lanes_of((128, 128))) & (lanes_of((128, 128)) < 32), 1.0, 0.0
    ).astype(F32)
    lane8 = lanes_of((8, 128))
    for i in range(8):
        r2 = dot(fold_y, dot(res[2 * i] + res[2 * i + 1], fold_z))
        c2 = dot(fold_y, dot(coef[2 * i] + coef[2 * i + 1], fold_z))
        low_res[i] = r2
        low_coef[i] = c2
        both = r2 + turn(c2, 32, 1)
        up[i * 8 : i * 8 + 8, :] = both[8:16]
        down[i * 8 : i * 8 + 8, :] = both[0:8]
    for x in range(16):
        at = 64 + x * 8
        up[at : at + 8, :] = jnp.where(lane8 < 64, res[x, 24:32, :], turn(sol[x, 24:32, :], 64, 1))
        down[at : at + 8, :] = jnp.where(lane8 < 64, res[x, 0:8, :], turn(sol[x, 0:8, :], 64, 1))


def pack_low_z(low_res, low_coef, res, sol, below, above, res2, coef2, res1, sol1, up, down):
    lane2 = lanes_of((R2, 128))
    lane1 = lanes_of((Q1, 128))
    lane8 = lanes_of((8, 128))
    ups = jnp.zeros((R2, 128), F32)
    downs = jnp.zeros((R2, 128), F32)
    for i in range(8):
        res2[i, 0:16, :] = low_res[i]
        coef2[i, 0:16, :] = low_coef[i]
        for msg, at in ((above, 16), (below, 24)):
            both = msg[i * 8 : i * 8 + 8, :]
            res2[i, at : at + 8, :] = jnp.where(lane8 < 32, both, 0.0)
            coef2[i, at : at + 8, :] = jnp.where(lane8 < 32, turn(both, -32, 1), 0.0)
        for a, ref in ((0, res2), (1, coef2)):
            v = ref[i]
            base = a * 64 + i * 8
            here = (lane2 >= base) & (lane2 < base + 8)
            ups = jnp.where(here, turn(v, base - 24, 1), ups)
            downs = jnp.where(here, turn(v, base, 1), downs)
    up[0:R2, :] = ups
    down[0:R2, :] = downs
    ups = jnp.zeros((Q1, 128), F32)
    downs = jnp.zeros((Q1, 128), F32)
    for x in range(16):
        res1[x, 0:32, :] = jnp.where(lanes_of((32, 128)) < 64, res[x, 0:32, :], 0.0)
        sol1[x, 0:32, :] = jnp.where(lanes_of((32, 128)) < 64, sol[x, 0:32, :], 0.0)
        for msg, at in ((above, 32), (below, 40)):
            both = msg[64 + x * 8 : 72 + x * 8, :]
            res1[x, at : at + 8, :] = jnp.where(lane8 < 64, both, 0.0)
            sol1[x, at : at + 8, :] = jnp.where(lane8 < 64, turn(both, 64, 1), 0.0)
        base = 4 * x
        here = (lane1 >= base) & (lane1 < base + 4)
        ups = jnp.where(here, turn(res1[x], base - 60, 1), ups)
        downs = jnp.where(here, turn(res1[x], base, 1), downs)
        base = 64 + 2 * x
        here = (lane1 >= base) & (lane1 < base + 2)
        ups = jnp.where(here, turn(sol1[x], base - 62, 1), ups)
        downs = jnp.where(here, turn(sol1[x], base, 1), downs)
    up[R2 : R2 + Q1, :] = ups
    down[R2 : R2 + Q1, :] = downs


def finish(
    res2_in, coef2_in, res1_in, sol1_in, coef1, left, right, sol0, res_q, diag_q, inv_q, low, high,
    out_sol, out_res,
    res2, diag2, inv2, sol2, da2, db2, res1, diag1, inv1, sol1, da1, db1, p0, res0, da0, db0,
):
    gx = lax.axis_index("gx")
    lane2 = lanes_of((R2, 128))
    in_yz = inside_yz((R2, 128), 16, 24, 32, 64)
    empty = jnp.zeros((R2, 128), F32)
    for buffer in (da2, db2):
        buffer[0] = empty
        buffer[9] = empty
    from_left, from_right = left[0:R2, :], right[0:R2, :]
    for i in range(8):
        parts = []
        for a, ref in ((0, res2_in), (1, coef2_in)):
            base = a * 64 + i * 8
            v = jnp.where(lane2 < 32, ref[i], turn(from_right, 32 - base, 1))
            v = jnp.where(lane2 < 40, v, 0.0)
            parts.append(jnp.where(lane2 < 120, v, turn(from_left, 120 - base, 1)))
        g = parts[1] + 0.375
        inverse = jnp.where(in_yz, 1.0 / g, 0.0)
        res2[i] = parts[0]
        diag2[i] = g
        inv2[i] = inverse
        d = parts[0] * inverse * (1.0 / THETA)
        da2[i + 1] = d
        sol2[i] = d
    pairs = coefficients(COARSE_SWEEPS)
    buffers = (da2, db2)
    for k in range(COARSE_SWEEPS - 1):
        src, dst = buffers[k % 2], buffers[(k + 1) % 2]
        line_sweep(src, dst, res2, diag2, inv2, 8, 0.0625, pairs[k])

        def gather(x, carry):
            sol2[x] += dst[x + 1]
            return carry

        lax.fori_loop(0, 8, gather, 0, unroll=2)

    lane1 = lanes_of((Q1, 128))
    in_yz1 = inside_yz((Q1, 128), 32, 40, 64, 96)
    empty = jnp.zeros((Q1, 128), F32)
    for buffer in (da1, db1):
        buffer[0] = empty
        buffer[17] = empty
    for x in (0, 1, 18, 19):
        sol1[x] = empty
    from_left, from_right = left[R2 : R2 + Q1, :], right[R2 : R2 + Q1, :]
    row, col = rows_of((Q1, R2)), lanes_of((Q1, R2))
    lift_y = jnp.where(col == row // 2 + jnp.where(row >= 40, 8, 0), 1.0, 0.0).astype(F32)
    row, col = rows_of((128, 128)), lanes_of((128, 128))
    lift_z = jnp.where(row == col // 2 + jnp.where(col >= 96, 64, 0), 1.0, 0.0).astype(F32)
    for i in range(8):
        lifted = dot(lift_y, dot(sol2[i], lift_z))
        for x in (2 * i, 2 * i + 1):
            db1[x + 1] = lifted
            base = 4 * x
            v = jnp.where(lane1 < 64, res1_in[x], turn(from_right, 64 - base, 1))
            v = jnp.where(lane1 < 68, v, 0.0)
            res1[x] = jnp.where(lane1 < 124, v, turn(from_left, 124 - base, 1))
            base = 64 + 2 * x
            v = jnp.where(lane1 < 64, sol1_in[x], turn(from_right, 64 - base, 1))
            v = jnp.where(lane1 < 66, v, 0.0)
            v = jnp.where(lane1 < 126, v, turn(from_left, 126 - base, 1))
            sol1[x + 2] = jnp.where(in_yz1, v, 0.0) + lifted

    def correct1(x, carry):
        g = jnp.concatenate([coef1[x], coef1[x, 32:40, :]], 0) + 1.5
        inverse = jnp.where(in_yz1, 1.0 / g, 0.0)
        diag1[x] = g
        inv1[x] = inverse
        p = db1[x + 1]
        near = beside(p) + (db1[x] + db1[x + 2])
        r = res1[x] - (g * p - 0.25 * near)
        res1[x] = r
        d = r * inverse * (1.0 / THETA)
        da1[x + 1] = d
        sol1[x + 2] += d
        return carry

    lax.fori_loop(0, 16, correct1, 0)
    pairs = coefficients(SWEEPS)
    buffers = (da1, db1)
    for k in range(SWEEPS - 1):
        src, dst = buffers[k % 2], buffers[(k + 1) % 2]
        line_sweep(src, dst, res1, diag1, inv1, 16, 0.25, pairs[k])

        def gather1(x, carry):
            sol1[x + 2] += dst[x + 1]
            return carry

        lax.fori_loop(0, 16, gather1, 0, unroll=2)

    row, col = rows_of((Q0, Q1)), lanes_of((Q0, Q1))
    lift_y = jnp.where(col == row // 2 + jnp.where(row >= 68, 12, 0), 1.0, 0.0).astype(F32)
    lift_z = jnp.where(rows_of((128, 256)) == lanes_of((128, 256)) // 2, 1.0, 0.0).astype(F32)
    for i in range(8):
        lifted = dot(lift_y, dot(sol1[gx * 4 + i], lift_z))
        p0[2 * i] = lifted
        p0[2 * i + 1] = lifted
    lane72 = lanes_of((Q0, 128))
    at = 160 + XH * Q0
    for msg, first in ((low, 0), (high, XH + NX0)):
        side = msg[at : at + Q0, :]
        for i in range(XH):
            base = 64 + 6 * i
            v = jnp.where(lane72 < 3, turn(side, -base, 1), 0.0)
            v = jnp.where(lane72 < 125, v, turn(side, 125 - base - 3, 1))
            res0[first + i, :, 0:128] = msg[160 + i * Q0 : 160 + i * Q0 + Q0, :]
            res0[first + i, :, 128:256] = v

    def fetch(x, carry):
        res0[x + XH] = res_q[x]
        return carry

    lax.fori_loop(0, NX0, fetch, 0)

    def correct0(x, carry):
        p = p0[x + 1]
        near = beside(p) + (p0[x] + p0[x + 2])
        r = res0[x] - (diag_q[x] * p - near)
        res0[x] = r
        da0[x] = r * inv_q[x] * (1.0 / THETA)
        return carry

    lax.fori_loop(0, NXE, correct0, 0)

    def begin(x, carry):
        out_sol[x] = sol0[x] + p0[x + XH + 1, 0:64, 0:128]
        return carry

    lax.fori_loop(0, NX0, begin, 0)
    buffers = (da0, db0)
    for k in range(SWEEPS):
        src, dst = buffers[k % 2], buffers[(k + 1) % 2]

        def gather0(x, carry):
            out_sol[x] += src[x + XH, 0:64, 0:128]
            return carry

        lax.fori_loop(0, NX0, gather0, 0)
        fine_sweep(
            src, dst, res0, diag_q, inv_q, k + 1, NXE - 1 - k, pairs[k] if k < SWEEPS - 1 else None,
            lambda x, d: None,
        )

    def put(x, carry):
        out_res[x] = res0[x + XH, 0:64, 0:128]
        return carry

    lax.fori_loop(0, NX0, put, 0)


def per_device(s, c):
    up = jnp.concatenate([s[NX0 - XH :], c[NX0 - XH :]], 0)
    down = jnp.concatenate([s[:XH], c[:XH]], 0)
    low, high = ring(up, "gx", 1), ring(down, "gx", -1)
    up, down = call(pack_y, [(256, 128)] * 2, [], s, c, low, high)
    below, above = ring(up, "gy", 1), ring(down, "gy", -1)
    main, up, down = call(
        pack_z, [(2, NXE, R0, 128), (2, R0, 128), (2, R0, 128)], [], s, c, low, high, below, above
    )
    below, above = ring(up, "gz", 1), ring(down, "gz", -1)
    big = (NXE, R0, 256)
    sol0, res_q, diag_q, inv_q, msg2, msg_up, msg_down = call(
        fine_before,
        [(NX0, 64, 128), (NX0, Q0, 256), (NXE, Q0, 256), (NXE, Q0, 256), (200, 128), (448, 128), (448, 128)],
        [big] * 5,
        main, below, above,
    )
    low, high, far = ring(msg_up, "gx", 1), ring(msg_down, "gx", -1), ring(msg2, "gx", 2)
    mid = (16, R1, 128)
    res1, sol1, coef1, res2, coef2, up, down = call(
        middle_before,
        [mid, mid, mid, (8, 16, 128), (8, 16, 128), (192, 128), (192, 128)],
        [mid, mid, (18, R1, 128), (18, R1, 128)],
        msg2, low, high, far,
    )
    below, above = ring(up, "gy", 1), ring(down, "gy", -1)
    bot, mid = (8, R2, 128), (16, Q1, 128)
    res2, coef2, res1, sol1, up, down = call(
        pack_low_z,
        [bot, bot, mid, mid, (R2 + Q1, 128), (R2 + Q1, 128)],
        [],
        res2, coef2, res1, sol1, below, above,
    )
    left, right = ring(up, "gz", 1), ring(down, "gz", -1)
    big = (NXE, Q0, 256)
    own = (NX0, NY0, NZ0)
    return tuple(
        call(
            finish,
            [own, own],
            [bot] * 4 + [(10, R2, 128)] * 2 + [mid] * 3 + [(20, Q1, 128)] + [(18, Q1, 128)] * 2
            + [(16, Q0, 256)] + [big] * 3,
            res2, coef2, res1, sol1, coef1, left, right, sol0, res_q, diag_q, inv_q, low, high,
        )
    )


def solution(mesh):
    return jax.shard_map(
        per_device,
        mesh=mesh,
        in_specs=(P("gx", "gy", "gz"), P("gx", "gy", "gz")),
        out_specs=(P("gx", "gy", "gz"), P("gx", "gy", "gz")),
        check_vma=False,
    )
```

time: 566 us -> 98.6 us (0.17); the launches traced: 559 us -> 98.3 us
  starting transfers between devices: 309 us -> 15.8 us
  local copies, waits for them, and re-layouts: 93.4 us -> 6.35 us
  waiting for transfers between devices: 105 us -> 31.5 us
  other arithmetic: 48.5 us -> 0.03 us
  Pallas kernels: 0 us -> 43.9 us
    ppermute x108 -> x13, starting transfers between devices: 309 us -> 15.8 us  [ring(): lax.ppermute(value, axis, [(i, (i + shift) % size) for i in range(size)])]
    ppermute x108 -> x13, waiting for transfers between devices: 105 us -> 31.5 us  [ring(): lax.ppermute(value, axis, [(i, (i + shift) % size) for i in range(size)])]
    pallas_call x0 -> x6, Pallas kernels: none -> 43.9 us  [call(): pl.pallas_call(body, out_shape=[jax.ShapeDtypeStruct(s, F32) for s in out...]
    reshape x7 -> x0, local copies, waits for them, and re-layouts: 41 us -> none  [the longest x3 40.5 us: coarsen(): return field.reshape(a // 2, 2, b // 2, 2, c // 2, 2).mean(axis=(1, 3, 5))]
    unnamed x48 -> x26, local copies, waits for them, and re-layouts: 26.3 us -> 5.28 us
    reduce_sum x4 -> x0, other arithmetic: 17.6 us -> none  [coarsen(): return field.reshape(a // 2, 2, b // 2, 2, c // 2, 2).mean(axis=(1, 3, 5))]
    add x13 -> x0, other arithmetic: 14.5 us -> none  [the longest x10 9.7 us: smooth(): step_dir = rho_new * rho * step_dir + 2.0 * rho_new / DELTA * res * inverse]
    concatenate x7 -> x0, local copies, waits for them, and re-layouts: 9.18 us -> none  [padded_2(): array = jnp.concatenate([before, array, after], axis=dim)]
  transfers between devices with their start and end apart: 108 -> 13, of which waited for: 44 -> 10; matrix products, arithmetic and copies ran while one was open for 10% -> 0% of each run, Pallas kernels for 0% -> 0%
where the time goes in v1:
time: 98.6 us; the launch traced here: 98.3 us
  Pallas kernels  43.9 us (45%)
  waiting for transfers between devices  31.5 us (32%)
  starting transfers between devices  15.8 us (16%)
  local copies, waits for them, and re-layouts  6.35 us (6%)
    pallas_call x6, Pallas kernels, call(): pl.pallas_call(body, out_shape=[jax.ShapeDtypeStruct(s, F32) for s in out...  43.9 us
    ppermute x13, waiting for transfers between devices, ring(): lax.ppermute(value, axis, [(i, (i + shift) % size) for i in range(size)])  31.5 us
    ppermute x13, starting transfers between devices, ring(): lax.ppermute(value, axis, [(i, (i + shift) % size) for i in range(size)])  15.8 us
    unnamed x26, local copies, waits for them, and re-layouts  5.28 us
  transfers between devices with their start and end apart: 13, of which 10 were waited for; matrix products, arithmetic and copies ran while one was open for 0% of the time, Pallas kernels for 0%

profile of v1, /device:TPU:71, one launch (start us, length us, event | category | flops | bytes accessed | tf_op | source)
XLA Modules:
  0.0 98.3 jit_solution(16393397487943818046)
XLA Ops:
  0.6 1.1 %fusion = (f32[3,64,128]{2,1,0:T(8,128)S(1)}, f32[3,64,128]{2,1,0:T(8,128)S(1)}, f32[3,64,128]{2,1,0:T(8,128)S(1)}, f32[3,64,128]{2,1,0:T(8,128)S(1)}) fusion(f32[8,64,128]{2,1,0:T(8,128)} %s.3, f32[8,64,128]{2,1,0:T(8,128)} %c.3), kind=kLoop, calls=%fused_computation.2 | loop fusion | bytes 786432 | tf_op jit(solution)/shard_map/slice | solution.py:530
  1.7 1.4 %collective-permute-start = (f32[6,64,128]{2,1,0:T(8,128)S(1)}, f32[6,64,128]{2,1,0:T(8,128)S(1)}, u32[]{:S(2)}, u32[]{:S(2)}) collective-permute-start(f32[6,64,128]{2,1,0:T(8,128)S(1)} %pad_maximum_fusion), channel_id=1, source_target_pairs={{0,64},{64,128},{128,192},{192,0},{1,65},{65,129},{129,193},{193,1... | collective-permute-start | bytes 589832 | tf_op jit(solution)/shard_map/ppermute | solution.py:83
  3.1 1.5 %collective-permute-start.1 = (f32[6,64,128]{2,1,0:T(8,128)S(1)}, f32[6,64,128]{2,1,0:T(8,128)S(1)}, u32[]{:S(2)}, u32[]{:S(2)}) collective-permute-start(f32[6,64,128]{2,1,0:T(8,128)S(1)} %pad_maximum_fusion.1), channel_id=1, source_target_pairs={{0,192},{64,0},{128,64},{192,128},{1,193},{65,1},{129,65},{193,129... | collective-permute-start | bytes 589832 | tf_op jit(solution)/shard_map/ppermute | solution.py:83
  4.6 4.3 %collective-permute-done.low = f32[6,64,128]{2,1,0:T(8,128)S(1)} collective-permute-done((f32[6,64,128]{2,1,0:T(8,128)S(1)}, f32[6,64,128]{2,1,0:T(8,128)S(1)}, u32[]{:S(2)}, u32[]{:S(2)}) %collective-permute-start) | collective-permute-done | bytes 196640 | tf_op jit(solution)/shard_map/ppermute | solution.py:83
  10.3 1.9 %shard_map.41 = (f32[256,128]{1,0:T(8,128)}, f32[256,128]{1,0:T(8,128)}) custom-call(f32[8,64,128]{2,1,0:T(8,128)} %s.3, f32[8,64,128]{2,1,0:T(8,128)} %c.3, f32[6,64,128]{2,1,0:T(8,128)} %copy-done.2, f32[6,64,128]{2,1,0:T(8,128)} %copy-done.3), custom_call_target="tpu_custom_call" | custom-call | tf_op jit(solution)/shard_map/pallas_call | solution.py:71
  12.1 1.6 %collective-permute-start.2 = (f32[256,128]{1,0:T(8,128)}, f32[256,128]{1,0:T(8,128)S(1)}, u32[]{:S(2)}, u32[]{:S(2)}) collective-permute-start(f32[256,128]{1,0:T(8,128)} %get-tuple-element.27), channel_id=1, source_target_pairs={{0,8},{8,16},{16,24},{24,32},{32,40},{40,48},{48,56},{56,0},{1,9},... | collective-permute-start | bytes 393224 | tf_op jit(solution)/shard_map/ppermute | solution.py:83
  13.8 2.4 %collective-permute-done.2.below = f32[256,128]{1,0:T(8,128)S(1)} collective-permute-done((f32[256,128]{1,0:T(8,128)}, f32[256,128]{1,0:T(8,128)S(1)}, u32[]{:S(2)}, u32[]{:S(2)}) %collective-permute-start.2) | collective-permute-done | bytes 131104 | tf_op jit(solution)/shard_map/ppermute | solution.py:83
  16.2 3.0 %collective-permute-done.3.above = f32[256,128]{1,0:T(8,128)S(1)} collective-permute-done((f32[256,128]{1,0:T(8,128)}, f32[256,128]{1,0:T(8,128)S(1)}, u32[]{:S(2)}, u32[]{:S(2)}) %collective-permute-start.3) | collective-permute-done | bytes 131104 | tf_op jit(solution)/shard_map/ppermute | solution.py:83
  19.8 2.9 %shard_map.42 = (f32[2,14,88,128]{3,2,1,0:T(8,128)}, f32[2,88,128]{2,1,0:T(8,128)}, f32[2,88,128]{2,1,0:T(8,128)}) custom-call(f32[8,64,128]{2,1,0:T(8,128)} %s.3, f32[8,64,128]{2,1,0:T(8,128)} %c.3, f32[6,64,128]{2,1,0:T(8,128)} %copy-done.2, f32[6,64,128]{2,1,0:T(8,128)} %copy-done.3, f32[256,128]{1,0:T(8,128)} %copy-done.4, f32[256,128]{1,0:T(8,128)} %copy-done.5), custom_call_target="tpu_custom_call" | custom-call | tf_op jit(solution)/shard_map/pallas_call | solution.py:71
  22.8 2.7 %collective-permute-start.4 = (f32[2,88,128]{2,1,0:T(8,128)}, f32[2,88,128]{2,1,0:T(8,128)S(1)}, u32[]{:S(2)}, u32[]{:S(2)}) collective-permute-start(f32[2,88,128]{2,1,0:T(8,128)} %get-tuple-element.30), channel_id=1, source_target_pairs={{0,1},{1,2},{2,3},{3,4},{4,5},{5,6},{6,7},{7,0},{8,9},{9,10},{10,1... | collective-permute-start | bytes 270344 | tf_op jit(solution)/shard_map/ppermute | solution.py:83
  25.5 1.9 %collective-permute-done.4.below = f32[2,88,128]{2,1,0:T(8,128)S(1)} collective-permute-done((f32[2,88,128]{2,1,0:T(8,128)}, f32[2,88,128]{2,1,0:T(8,128)S(1)}, u32[]{:S(2)}, u32[]{:S(2)}) %collective-permute-start.4) | collective-permute-done | bytes 90144 | tf_op jit(solution)/shard_map/ppermute | solution.py:83
  27.4 3.5 %collective-permute-done.5.above = f32[2,88,128]{2,1,0:T(8,128)S(1)} collective-permute-done((f32[2,88,128]{2,1,0:T(8,128)}, f32[2,88,128]{2,1,0:T(8,128)S(1)}, u32[]{:S(2)}, u32[]{:S(2)}) %collective-permute-start.5) | collective-permute-done | bytes 90144 | tf_op jit(solution)/shard_map/ppermute | solution.py:83
  31.5 9.3 %shard_map.43 = (f32[8,64,128]{2,1,0:T(8,128)}, f32[8,72,256]{2,1,0:T(8,128)}, f32[14,72,256]{2,1,0:T(8,128)}, f32[14,72,256]{2,1,0:T(8,128)}, f32[200,128]{1,0:...) custom-call(f32[2,14,88,128]{3,2,1,0:T(8,128)} %get-tuple-element.29.main, f32[2,88,128]{2,1,0:T(8,128)} %copy-done.9, ...), custom_call_target="tpu_custom_call" | custom-call | tf_op jit(solution)/shard_map/pallas_call | solution.py:71
  41.5 1.9 %collective-permute-start.7 = (f32[448,128]{1,0:T(8,128)}, f32[448,128]{1,0:T(8,128)S(1)}, u32[]{:S(2)}, u32[]{:S(2)}) collective-permute-start(f32[448,128]{1,0:T(8,128)} %get-tuple-element.34), channel_id=1, source_target_pairs={{0,192},{64,0},{128,64},{192,128},{1,193},{65,1},{129,65},{193,129... | collective-permute-start | bytes 688136 | tf_op jit(solution)/shard_map/ppermute | solution.py:83
  44.3 7.3 %collective-permute-done.8.far = f32[200,128]{1,0:T(8,128)S(1)} collective-permute-done((f32[200,128]{1,0:T(8,128)}, f32[200,128]{1,0:T(8,128)S(1)}, u32[]{:S(2)}, u32[]{:S(2)}) %collective-permute-start.8) | collective-permute-done | bytes 102432 | tf_op jit(solution)/shard_map/ppermute | solution.py:83
  53.0 8.2 %shard_map.44 = (f32[16,40,128]{2,1,0:T(8,128)}, f32[16,40,128]{2,1,0:T(8,128)}, f32[16,40,128]{2,1,0:T(8,128)}, f32[8,16,128]{2,1,0:T(8,128)}, f32[8,16,128]{2,...) custom-call(f32[200,128]{1,0:T(8,128)} %get-tuple-element.32.own, f32[448,128]{1,0:T(8,128)} %copy-done, ...), custom_call_target="tpu_custom_call" | custom-call | tf_op jit(solution)/shard_map/pallas_call | solution.py:71
  61.1 3.0 %collective-permute-start.9 = (f32[192,128]{1,0:T(8,128)}, f32[192,128]{1,0:T(8,128)S(1)}, u32[]{:S(2)}, u32[]{:S(2)}) collective-permute-start(f32[192,128]{1,0:T(8,128)} %get-tuple-element.39), channel_id=1, source_target_pairs={{0,8},{8,16},{16,24},{24,32},{32,40},{40,48},{48,56},{56,0},{1,9},... | collective-permute-start | bytes 294920 | tf_op jit(solution)/shard_map/ppermute | solution.py:83
  64.1 2.6 %collective-permute-done.9.below = f32[192,128]{1,0:T(8,128)S(1)} collective-permute-done((f32[192,128]{1,0:T(8,128)}, f32[192,128]{1,0:T(8,128)S(1)}, u32[]{:S(2)}, u32[]{:S(2)}) %collective-permute-start.9) | collective-permute-done | bytes 98336 | tf_op jit(solution)/shard_map/ppermute | solution.py:83
  66.7 1.8 %collective-permute-done.10.above = f32[192,128]{1,0:T(8,128)S(1)} collective-permute-done((f32[192,128]{1,0:T(8,128)}, f32[192,128]{1,0:T(8,128)S(1)}, u32[]{:S(2)}, u32[]{:S(2)}) %collective-permute-start.10) | collective-permute-done | bytes 98336 | tf_op jit(solution)/shard_map/ppermute | solution.py:83
  69.1 3.5 %shard_map.45 = (f32[8,32,128]{2,1,0:T(8,128)}, f32[8,32,128]{2,1,0:T(8,128)}, f32[16,48,128]{2,1,0:T(8,128)}, f32[16,48,128]{2,1,0:T(8,128)}, f32[80,128]{1,0:T(8,128)}, /*index=5*/f32[80,128]{1,0:T(8,128)}) custom-call(f32[8,16,128]{2,1,0:T(8,128)} %get-tuple-element.35.low_res, f32[8,16,128]{2,1,0:T(8,128)} %get-tuple-element.36.low_coef, ...), custom_call_target="tpu_custom_call" | custom-call | tf_op jit(solution)/shard_map/pallas_call | solution.py:71
  72.6 2.1 %collective-permute-start.11 = (f32[80,128]{1,0:T(8,128)}, f32[80,128]{1,0:T(8,128)S(1)}, u32[]{:S(2)}, u32[]{:S(2)}) collective-permute-start(f32[80,128]{1,0:T(8,128)} %get-tuple-element.46), channel_id=1, source_target_pairs={{0,1},{1,2},{2,3},{3,4},{4,5},{5,6},{6,7},{7,0},{8,9},{9,10},{10,1... | collective-permute-start | bytes 122888 | tf_op jit(solution)/shard_map/ppermute | solution.py:83
  74.7 1.4 %collective-permute-done.11.left = f32[80,128]{1,0:T(8,128)S(1)} collective-permute-done((f32[80,128]{1,0:T(8,128)}, f32[80,128]{1,0:T(8,128)S(1)}, u32[]{:S(2)}, u32[]{:S(2)}) %collective-permute-start.11) | collective-permute-done | bytes 40992 | tf_op jit(solution)/shard_map/ppermute | solution.py:83
  76.1 3.4 %collective-permute-done.12.right = f32[80,128]{1,0:T(8,128)S(1)} collective-permute-done((f32[80,128]{1,0:T(8,128)}, f32[80,128]{1,0:T(8,128)S(1)}, u32[]{:S(2)}, u32[]{:S(2)}) %collective-permute-start.12) | collective-permute-done | bytes 40992 | tf_op jit(solution)/shard_map/ppermute | solution.py:83
  80.1 18.2 %shard_map.46 = (f32[8,64,128]{2,1,0:T(8,128)}, f32[8,64,128]{2,1,0:T(8,128)}) custom-call(f32[8,32,128]{2,1,0:T(8,128)} %get-tuple-element.41.res2_in, f32[8,32,128]{2,1,0:T(8,128)} %get-tuple-element.42.coef2_in, f32[16,48,128]{2,1,0:T(8,128)} %get-tuple-element.43.res1_in, f32[16,48,128]{2,1,0:T(8,128)} %get-tuple-element.44.sol1_in, ...), custom_call_target="tpu_custom_call" | custom-call | tf_op jit(solution)/shard_map/pallas_call | solution.py:71
  (37 shorter events, 6.9 us)
Async XLA Ops:
  1.7 7.2 %collective-permute-start = (f32[6,64,128]{2,1,0:T(8,128)S(1)}, f32[6,64,128]{2,1,0:T(8,128)S(1)}, u32[]{:S(2)}, u32[]{:S(2)}) collective-permute-start(f32[6,64,128]{2,1,0:T(8,128)S(1)} %pad_maximum_fusion), channel_id=1, source_target_pairs={{0,64},{64,128},{128,192},{192,0},{1,65},{65,129},{129,193},{193,1... | collective-permute-start | bytes 589832 | tf_op jit(solution)/shard_map/ppermute | solution.py:83
  3.1 5.8 %collective-permute-start.1 = (f32[6,64,128]{2,1,0:T(8,128)S(1)}, f32[6,64,128]{2,1,0:T(8,128)S(1)}, u32[]{:S(2)}, u32[]{:S(2)}) collective-permute-start(f32[6,64,128]{2,1,0:T(8,128)S(1)} %pad_maximum_fusion.1), channel_id=1, source_target_pairs={{0,192},{64,0},{128,64},{192,128},{1,193},{65,1},{129,65},{193,129... | collective-permute-start | bytes 589832 | tf_op jit(solution)/shard_map/ppermute | solution.py:83
  8.9 0.7 copy-start.2
  9.6 0.7 copy-start.3
  12.1 4.0 %collective-permute-start.2 = (f32[256,128]{1,0:T(8,128)}, f32[256,128]{1,0:T(8,128)S(1)}, u32[]{:S(2)}, u32[]{:S(2)}) collective-permute-start(f32[256,128]{1,0:T(8,128)} %get-tuple-element.27), channel_id=1, source_target_pairs={{0,8},{8,16},{16,24},{24,32},{32,40},{40,48},{48,56},{56,0},{1,9},... | collective-permute-start | bytes 393224 | tf_op jit(solution)/shard_map/ppermute | solution.py:83
  13.8 5.4 %collective-permute-start.3 = (f32[256,128]{1,0:T(8,128)}, f32[256,128]{1,0:T(8,128)S(1)}, u32[]{:S(2)}, u32[]{:S(2)}) collective-permute-start(f32[256,128]{1,0:T(8,128)} %get-tuple-element.28), channel_id=1, source_target_pairs={{0,56},{8,0},{16,8},{24,16},{32,24},{40,32},{48,40},{56,48},{1,57}... | collective-permute-start | bytes 393224 | tf_op jit(solution)/shard_map/ppermute | solution.py:83
  16.2 3.0 %copy-start.4 = (f32[256,128]{1,0:T(8,128)}, f32[256,128]{1,0:T(8,128)S(1)}, u32[]{:S(2)}) copy-start(f32[256,128]{1,0:T(8,128)S(1)} %collective-permute-done.2.below) | copy-start | bytes 393220
  19.2 0.6 copy-start.5
  22.8 4.6 %collective-permute-start.4 = (f32[2,88,128]{2,1,0:T(8,128)}, f32[2,88,128]{2,1,0:T(8,128)S(1)}, u32[]{:S(2)}, u32[]{:S(2)}) collective-permute-start(f32[2,88,128]{2,1,0:T(8,128)} %get-tuple-element.30), channel_id=1, source_target_pairs={{0,1},{1,2},{2,3},{3,4},{4,5},{5,6},{6,7},{7,0},{8,9},{9,10},{10,1... | collective-permute-start | bytes 270344 | tf_op jit(solution)/shard_map/ppermute | solution.py:83
  25.5 5.4 %collective-permute-start.5 = (f32[2,88,128]{2,1,0:T(8,128)}, f32[2,88,128]{2,1,0:T(8,128)S(1)}, u32[]{:S(2)}, u32[]{:S(2)}) collective-permute-start(f32[2,88,128]{2,1,0:T(8,128)} %get-tuple-element.31), channel_id=1, source_target_pairs={{0,7},{1,0},{2,1},{3,2},{4,3},{5,4},{6,5},{7,6},{8,15},{9,8},{10,9... | collective-permute-start | bytes 270344 | tf_op jit(solution)/shard_map/ppermute | solution.py:83
  27.4 3.5 %copy-start.9 = (f32[2,88,128]{2,1,0:T(8,128)}, f32[2,88,128]{2,1,0:T(8,128)S(1)}, u32[]{:S(2)}) copy-start(f32[2,88,128]{2,1,0:T(8,128)S(1)} %collective-permute-done.4.below) | copy-start | bytes 270340
  40.8 10.8 %collective-permute-start.6 = (f32[448,128]{1,0:T(8,128)}, f32[448,128]{1,0:T(8,128)S(1)}, u32[]{:S(2)}, u32[]{:S(2)}) collective-permute-start(f32[448,128]{1,0:T(8,128)} %get-tuple-element.33), channel_id=1, source_target_pairs={{0,64},{64,128},{128,192},{192,0},{1,65},{65,129},{129,193},{193,1... | collective-permute-start | bytes 688136 | tf_op jit(solution)/shard_map/ppermute | solution.py:83
  41.5 10.1 %collective-permute-start.7 = (f32[448,128]{1,0:T(8,128)}, f32[448,128]{1,0:T(8,128)S(1)}, u32[]{:S(2)}, u32[]{:S(2)}) collective-permute-start(f32[448,128]{1,0:T(8,128)} %get-tuple-element.34), channel_id=1, source_target_pairs={{0,192},{64,0},{128,64},{192,128},{1,193},{65,1},{129,65},{193,129... | collective-permute-start | bytes 688136 | tf_op jit(solution)/shard_map/ppermute | solution.py:83
  43.5 8.1 %collective-permute-start.8 = (f32[200,128]{1,0:T(8,128)}, f32[200,128]{1,0:T(8,128)S(1)}, u32[]{:S(2)}, u32[]{:S(2)}) collective-permute-start(f32[200,128]{1,0:T(8,128)} %get-tuple-element.32.own), channel_id=1, source_target_pairs={{0,128},{64,192},{128,0},{192,64},{1,129},{65,193},{129,1},{193,65... | collective-permute-start | bytes 307208 | tf_op jit(solution)/shard_map/ppermute | solution.py:83
  51.6 0.6 copy-start.6
  51.6 0.7 copy-start
  52.3 0.7 copy-start.1
  61.1 5.6 %collective-permute-start.9 = (f32[192,128]{1,0:T(8,128)}, f32[192,128]{1,0:T(8,128)S(1)}, u32[]{:S(2)}, u32[]{:S(2)}) collective-permute-start(f32[192,128]{1,0:T(8,128)} %get-tuple-element.39), channel_id=1, source_target_pairs={{0,8},{8,16},{16,24},{24,32},{32,40},{40,48},{48,56},{56,0},{1,9},... | collective-permute-start | bytes 294920 | tf_op jit(solution)/shard_map/ppermute | solution.py:83
  64.1 4.4 %collective-permute-start.10 = (f32[192,128]{1,0:T(8,128)}, f32[192,128]{1,0:T(8,128)S(1)}, u32[]{:S(2)}, u32[]{:S(2)}) collective-permute-start(f32[192,128]{1,0:T(8,128)} %get-tuple-element.40), channel_id=1, source_target_pairs={{0,56},{8,0},{16,8},{24,16},{32,24},{40,32},{48,40},{56,48},{1,57}... | collective-permute-start | bytes 294920 | tf_op jit(solution)/shard_map/ppermute | solution.py:83
  66.7 1.8 %copy-start.7 = (f32[192,128]{1,0:T(8,128)}, f32[192,128]{1,0:T(8,128)S(1)}, u32[]{:S(2)}) copy-start(f32[192,128]{1,0:T(8,128)S(1)} %collective-permute-done.9.below) | copy-start | bytes 294916
  68.5 0.6 copy-start.8
  72.6 3.5 %collective-permute-start.11 = (f32[80,128]{1,0:T(8,128)}, f32[80,128]{1,0:T(8,128)S(1)}, u32[]{:S(2)}, u32[]{:S(2)}) collective-permute-start(f32[80,128]{1,0:T(8,128)} %get-tuple-element.46), channel_id=1, source_target_pairs={{0,1},{1,2},{2,3},{3,4},{4,5},{5,6},{6,7},{7,0},{8,9},{9,10},{10,1... | collective-permute-start | bytes 122888 | tf_op jit(solution)/shard_map/ppermute | solution.py:83
  74.7 4.8 %collective-permute-start.12 = (f32[80,128]{1,0:T(8,128)}, f32[80,128]{1,0:T(8,128)S(1)}, u32[]{:S(2)}, u32[]{:S(2)}) collective-permute-start(f32[80,128]{1,0:T(8,128)} %get-tuple-element.47), channel_id=1, source_target_pairs={{0,7},{1,0},{2,1},{3,2},{4,3},{5,4},{6,5},{7,6},{8,15},{9,8},{10,9... | collective-permute-start | bytes 122888 | tf_op jit(solution)/shard_map/ppermute | solution.py:83
  76.1 3.4 %copy-start.11 = (f32[80,128]{1,0:T(8,128)}, f32[80,128]{1,0:T(8,128)S(1)}, u32[]{:S(2)}) copy-start(f32[80,128]{1,0:T(8,128)S(1)} %collective-permute-done.11.left) | copy-start | bytes 122884
  (2 other events, 1.2 us)

commit v2 on v1

--- a/solution.py
+++ b/solution.py
@@ -21,7 +21,7 @@
 R1 = 40
 Q1 = 48
 R2 = 32
-VM = 60 * 1024 * 1024
+MIB = 1024 * 1024
 
 
 def coefficients(count):
@@ -66,7 +66,7 @@
     return jnp.dot(a, b, precision=EXACT, preferred_element_type=F32)
 
 
-def call(body, outs, scratch, *args):
+def call(body, limit, outs, scratch, *args):
     vmem = pl.BlockSpec(memory_space=pltpu.VMEM)
     return pl.pallas_call(
         body,
@@ -74,7 +74,7 @@
         in_specs=[vmem] * len(args),
         out_specs=[vmem] * len(outs),
         scratch_shapes=[pltpu.VMEM(s, F32) for s in scratch],
-        compiler_params=pltpu.CompilerParams(vmem_limit_bytes=VM),
+        compiler_params=pltpu.CompilerParams(vmem_limit_bytes=limit * MIB),
     )(*args)
 
 
@@ -187,18 +187,6 @@
         return carry
 
     lax.fori_loop(0, NXE, start, 0)
-
-    def add(first):
-        def put(x, d):
-            own = d[0:64, 0:128]
-            at = jnp.clip(x - XH, 0, NX0 - 1)
-            if first:
-                sol[at] = own
-            else:
-                inside = ((x >= XH) & (x < XH + NX0)).astype(F32)
-                sol[at] += inside * own
-
-        return put
 
     pairs = coefficients(SWEEPS)
     buffers = (da, db)
@@ -252,17 +240,19 @@
         msg[at + R1 : at + Q0, :] = side[R1:Q0]
 
 
-def line_sweep(src, dst, res, diag, inverse, planes, scale, pair):
+def line_sweep(src, dst, res, diag, inverse, planes, scale, pair, sol, ahead=0):
     def body(x, carry):
         d = src[x + 1]
         near = beside(d) + (src[x] + src[x + 2])
         r = res[x] - (diag[x] * d - scale * near)
         res[x] = r
         if pair is not None:
-            dst[x + 1] = pair[0] * d + (pair[1] * inverse[x]) * r
-        return carry
-
-    lax.fori_loop(0, planes, body, 0, unroll=2)
+            step = pair[0] * d + (pair[1] * inverse[x]) * r
+            dst[x + 1] = step
+            sol[x + ahead] += step
+        return carry
+
+    lax.fori_loop(0, planes, body, 0, unroll=True)
 
 
 def middle_before(own, low, high, far, res, sol, coef, low_res, low_coef, up, down, diag, inv, da, db):
@@ -302,14 +292,7 @@
     buffers = (da, db)
     for k in range(SWEEPS):
         src, dst = buffers[k % 2], buffers[(k + 1) % 2]
-        line_sweep(src, dst, res, diag, inv, 16, 0.25, pairs[k] if k < SWEEPS - 1 else None)
-        if k < SWEEPS - 1:
-
-            def gather(x, carry):
-                sol[x] += dst[x + 1]
-                return carry
-
-            lax.fori_loop(0, 16, gather, 0, unroll=2)
+        line_sweep(src, dst, res, diag, inv, 16, 0.25, pairs[k] if k < SWEEPS - 1 else None, sol)
     fold_y = jnp.where(lanes_of((16, R1)) // 2 == rows_of((16, R1)), 0.125, 0.0).astype(F32)
     fold_z = jnp.where(
         (rows_of((128, 128)) // 2 == lanes_of((128, 128))) & (lanes_of((128, 128)) < 32), 1.0, 0.0
@@ -371,12 +354,7 @@
     down[R2 : R2 + Q1, :] = downs
 
 
-def finish(
-    res2_in, coef2_in, res1_in, sol1_in, coef1, left, right, sol0, res_q, diag_q, inv_q, low, high,
-    out_sol, out_res,
-    res2, diag2, inv2, sol2, da2, db2, res1, diag1, inv1, sol1, da1, db1, p0, res0, da0, db0,
-):
-    gx = lax.axis_index("gx")
+def bottom(res2_in, coef2_in, left, right, sol2, res2, diag2, inv2, da2, db2):
     lane2 = lanes_of((R2, 128))
     in_yz = inside_yz((R2, 128), 16, 24, 32, 64)
     empty = jnp.zeros((R2, 128), F32)
@@ -403,14 +381,10 @@
     buffers = (da2, db2)
     for k in range(COARSE_SWEEPS - 1):
         src, dst = buffers[k % 2], buffers[(k + 1) % 2]
-        line_sweep(src, dst, res2, diag2, inv2, 8, 0.0625, pairs[k])
-
-        def gather(x, carry):
-            sol2[x] += dst[x + 1]
-            return carry
-
-        lax.fori_loop(0, 8, gather, 0, unroll=2)
-
+        line_sweep(src, dst, res2, diag2, inv2, 8, 0.0625, pairs[k], sol2)
+
+
+def middle_after(sol2, res1_in, sol1_in, coef1, left, right, sol1, res1, diag1, inv1, da1, db1):
     lane1 = lanes_of((Q1, 128))
     in_yz1 = inside_yz((Q1, 128), 32, 40, 64, 96)
     empty = jnp.zeros((Q1, 128), F32)
@@ -457,14 +431,13 @@
     buffers = (da1, db1)
     for k in range(SWEEPS - 1):
         src, dst = buffers[k % 2], buffers[(k + 1) % 2]
-        line_sweep(src, dst, res1, diag1, inv1, 16, 0.25, pairs[k])
-
-        def gather1(x, carry):
-            sol1[x + 2] += dst[x + 1]
-            return carry
-
-        lax.fori_loop(0, 16, gather1, 0, unroll=2)
-
+        line_sweep(src, dst, res1, diag1, inv1, 16, 0.25, pairs[k], sol1, 2)
+
+
+def fine_after(
+    sol1, sol0, res_q, diag_q, inv_q, low, high, out_sol, out_res, p0, res0, da0, db0
+):
+    gx = lax.axis_index("gx")
     row, col = rows_of((Q0, Q1)), lanes_of((Q0, Q1))
     lift_y = jnp.where(col == row // 2 + jnp.where(row >= 68, 12, 0), 1.0, 0.0).astype(F32)
     lift_z = jnp.where(rows_of((128, 256)) == lanes_of((128, 256)) // 2, 1.0, 0.0).astype(F32)
@@ -504,6 +477,7 @@
         return carry
 
     lax.fori_loop(0, NX0, begin, 0)
+    pairs = coefficients(SWEEPS)
     buffers = (da0, db0)
     for k in range(SWEEPS):
         src, dst = buffers[k % 2], buffers[(k + 1) % 2]
@@ -529,15 +503,16 @@
     up = jnp.concatenate([s[NX0 - XH :], c[NX0 - XH :]], 0)
     down = jnp.concatenate([s[:XH], c[:XH]], 0)
     low, high = ring(up, "gx", 1), ring(down, "gx", -1)
-    up, down = call(pack_y, [(256, 128)] * 2, [], s, c, low, high)
+    up, down = call(pack_y, 4, [(256, 128)] * 2, [], s, c, low, high)
     below, above = ring(up, "gy", 1), ring(down, "gy", -1)
     main, up, down = call(
-        pack_z, [(2, NXE, R0, 128), (2, R0, 128), (2, R0, 128)], [], s, c, low, high, below, above
+        pack_z, 8, [(2, NXE, R0, 128), (2, R0, 128), (2, R0, 128)], [], s, c, low, high, below, above
     )
     below, above = ring(up, "gz", 1), ring(down, "gz", -1)
     big = (NXE, R0, 256)
     sol0, res_q, diag_q, inv_q, msg2, msg_up, msg_down = call(
         fine_before,
+        16,
         [(NX0, 64, 128), (NX0, Q0, 256), (NXE, Q0, 256), (NXE, Q0, 256), (200, 128), (448, 128), (448, 128)],
         [big] * 5,
         main, below, above,
@@ -546,6 +521,7 @@
     mid = (16, R1, 128)
     res1, sol1, coef1, res2, coef2, up, down = call(
         middle_before,
+        8,
         [mid, mid, mid, (8, 16, 128), (8, 16, 128), (192, 128), (192, 128)],
         [mid, mid, (18, R1, 128), (18, R1, 128)],
         msg2, low, high, far,
@@ -554,6 +530,7 @@
     bot, mid = (8, R2, 128), (16, Q1, 128)
     res2, coef2, res1, sol1, up, down = call(
         pack_low_z,
+        4,
         [bot, bot, mid, mid, (R2 + Q1, 128), (R2 + Q1, 128)],
         [],
         res2, coef2, res1, sol1, below, above,
@@ -561,13 +538,23 @@
     left, right = ring(up, "gz", 1), ring(down, "gz", -1)
     big = (NXE, Q0, 256)
     own = (NX0, NY0, NZ0)
+    (sol2,) = call(
+        bottom, 4, [bot], [bot] * 3 + [(10, R2, 128)] * 2, res2, coef2, left, right
+    )
+    (sol1,) = call(
+        middle_after,
+        8,
+        [(20, Q1, 128)],
+        [mid] * 3 + [(18, Q1, 128)] * 2,
+        sol2, res1, sol1, coef1, left, right,
+    )
     return tuple(
         call(
-            finish,
+            fine_after,
+            16,
             [own, own],
-            [bot] * 4 + [(10, R2, 128)] * 2 + [mid] * 3 + [(20, Q1, 128)] + [(18, Q1, 128)] * 2
-            + [(16, Q0, 256)] + [big] * 3,
-            res2, coef2, res1, sol1, coef1, left, right, sol0, res_q, diag_q, inv_q, low, high,
+            [(16, Q0, 256)] + [big] * 3,
+            sol1, sol0, res_q, diag_q, inv_q, low, high,
         )
     )
 

time: 98.6 us -> 75.8 us (0.77)
  Pallas kernels: 43.9 us -> 26.7 us
  local copies, waits for them, and re-layouts: 6.35 us -> 1.13 us
  waiting for transfers between devices: 31.5 us -> 30.5 us
    pallas_call x6 -> x8, Pallas kernels: 43.9 us -> 26.7 us  [call(): pl.pallas_call(body, out_shape=[jax.ShapeDtypeStruct(s, F32) for s in out...]
    unnamed x26 -> x4, local copies, waits for them, and re-layouts: 5.28 us -> 0.01 us
    ppermute x13, waiting for transfers between devices: 31.5 us -> 30.5 us  [ring(): lax.ppermute(value, axis, [(i, (i + shift) % size) for i in range(size)])]
where the time goes in v2:
time: 75.8 us; the launch traced here: 75.7 us
  waiting for transfers between devices  30.5 us (40%)
  Pallas kernels  26.7 us (35%)
  starting transfers between devices  16.7 us (22%)
  local copies, waits for them, and re-layouts  1.13 us (1%)
    ppermute x13, waiting for transfers between devices, ring(): lax.ppermute(value, axis, [(i, (i + shift) % size) for i in range(size)])  30.5 us
    pallas_call x8, Pallas kernels, call(): pl.pallas_call(body, out_shape=[jax.ShapeDtypeStruct(s, F32) for s in out...  26.7 us
    ppermute x13, starting transfers between devices, ring(): lax.ppermute(value, axis, [(i, (i + shift) % size) for i in range(size)])  16.7 us
  transfers between devices with their start and end apart: 13, of which 10 were waited for; matrix products, arithmetic and copies ran while one was open for 0% of the time, Pallas kernels for 0%

profile of v2, /device:TPU:71, one launch (start us, length us, event | category | flops | bytes accessed | tf_op | source)
XLA Modules:
  0.0 75.7 jit_solution(8050522619442816754)
XLA Ops:
  0.6 1.1 %fusion = (f32[3,64,128]{2,1,0:T(8,128)S(1)}, f32[3,64,128]{2,1,0:T(8,128)S(1)}, f32[3,64,128]{2,1,0:T(8,128)S(1)}, f32[3,64,128]{2,1,0:T(8,128)S(1)}) fusion(f32[8,64,128]{2,1,0:T(8,128)} %s.3, f32[8,64,128]{2,1,0:T(8,128)} %c.3), kind=kLoop, calls=%fused_computation.2 | loop fusion | bytes 786432 | tf_op jit(solution)/shard_map/slice | solution.py:504
  1.8 1.4 %collective-permute-start = (f32[6,64,128]{2,1,0:T(8,128)S(1)}, f32[6,64,128]{2,1,0:T(8,128)S(1)}, u32[]{:S(2)}, u32[]{:S(2)}) collective-permute-start(f32[6,64,128]{2,1,0:T(8,128)S(1)} %pad_maximum_fusion), channel_id=1, source_target_pairs={{0,64},{64,128},{128,192},{192,0},{1,65},{65,129},{129,193},{193,1... | collective-permute-start | bytes 589832 | tf_op jit(solution)/shard_map/ppermute | solution.py:83
  3.2 1.5 %collective-permute-start.1 = (f32[6,64,128]{2,1,0:T(8,128)S(1)}, f32[6,64,128]{2,1,0:T(8,128)S(1)}, u32[]{:S(2)}, u32[]{:S(2)}) collective-permute-start(f32[6,64,128]{2,1,0:T(8,128)S(1)} %pad_maximum_fusion.1), channel_id=1, source_target_pairs={{0,192},{64,0},{128,64},{192,128},{1,193},{65,1},{129,65},{193,129... | collective-permute-start | bytes 589832 | tf_op jit(solution)/shard_map/ppermute | solution.py:83
  4.7 4.3 %collective-permute-done.low = f32[6,64,128]{2,1,0:T(8,128)S(1)} collective-permute-done((f32[6,64,128]{2,1,0:T(8,128)S(1)}, f32[6,64,128]{2,1,0:T(8,128)S(1)}, u32[]{:S(2)}, u32[]{:S(2)}) %collective-permute-start) | collective-permute-done | bytes 196640 | tf_op jit(solution)/shard_map/ppermute | solution.py:83
  9.0 1.7 %collective-permute-start.2 = (f32[256,128]{1,0:T(8,128)S(1)}, f32[256,128]{1,0:T(8,128)S(1)}, u32[]{:S(2)}, u32[]{:S(2)}) collective-permute-start(f32[256,128]{1,0:T(8,128)S(1)} %get-tuple-element.27), channel_id=1, source_target_pairs={{0,8},{8,16},{16,24},{24,32},{32,40},{40,48},{48,56},{56,0},{1,9},... | collective-permute-start | bytes 393224 | tf_op jit(solution)/shard_map/ppermute | solution.py:83
  10.8 2.2 %collective-permute-done.2.below = f32[256,128]{1,0:T(8,128)S(1)} collective-permute-done((f32[256,128]{1,0:T(8,128)S(1)}, f32[256,128]{1,0:T(8,128)S(1)}, u32[]{:S(2)}, u32[]{:S(2)}) %collective-permute-start.2) | collective-permute-done | bytes 131104 | tf_op jit(solution)/shard_map/ppermute | solution.py:83
  12.9 3.0 %collective-permute-done.3.above = f32[256,128]{1,0:T(8,128)S(1)} collective-permute-done((f32[256,128]{1,0:T(8,128)S(1)}, f32[256,128]{1,0:T(8,128)S(1)}, u32[]{:S(2)}, u32[]{:S(2)}) %collective-permute-start.3) | collective-permute-done | bytes 131104 | tf_op jit(solution)/shard_map/ppermute | solution.py:83
  16.7 2.8 %collective-permute-start.4 = (f32[2,88,128]{2,1,0:T(8,128)S(1)}, f32[2,88,128]{2,1,0:T(8,128)S(1)}, u32[]{:S(2)}, u32[]{:S(2)}) collective-permute-start(f32[2,88,128]{2,1,0:T(8,128)S(1)} %get-tuple-element.30), channel_id=1, source_target_pairs={{0,1},{1,2},{2,3},{3,4},{4,5},{5,6},{6,7},{7,0},{8,9},{9,10},{10,1... | collective-permute-start | bytes 270344 | tf_op jit(solution)/shard_map/ppermute | solution.py:83
  19.5 1.6 %collective-permute-done.4.below = f32[2,88,128]{2,1,0:T(8,128)S(1)} collective-permute-done((f32[2,88,128]{2,1,0:T(8,128)S(1)}, f32[2,88,128]{2,1,0:T(8,128)S(1)}, u32[]{:S(2)}, u32[]{:S(2)}) %collective-permute-start.4) | collective-permute-done | bytes 90144 | tf_op jit(solution)/shard_map/ppermute | solution.py:83
  21.1 3.6 %collective-permute-done.5.above = f32[2,88,128]{2,1,0:T(8,128)S(1)} collective-permute-done((f32[2,88,128]{2,1,0:T(8,128)S(1)}, f32[2,88,128]{2,1,0:T(8,128)S(1)}, u32[]{:S(2)}, u32[]{:S(2)}) %collective-permute-start.5) | collective-permute-done | bytes 90144 | tf_op jit(solution)/shard_map/ppermute | solution.py:83
  24.7 7.1 %shard_map.43 = (f32[8,64,128]{2,1,0:T(8,128)S(1)}, f32[8,72,256]{2,1,0:T(8,128)S(1)}, f32[14,72,256]{2,1,0:T(8,128)S(1)}, f32[14,72,256]{2,1,0:T(8,128)S(1)}, f...) custom-call(f32[2,14,88,128]{3,2,1,0:T(8,128)S(1)} %get-tuple-element.29.main, ...), custom_call_target="tpu_custom_call" | custom-call | tf_op jit(solution)/shard_map/pallas_call | solution.py:71
  31.8 1.4 %collective-permute-start.6 = (f32[448,128]{1,0:T(8,128)S(1)}, f32[448,128]{1,0:T(8,128)S(1)}, u32[]{:S(2)}, u32[]{:S(2)}) collective-permute-start(f32[448,128]{1,0:T(8,128)S(1)} %get-tuple-element.33), channel_id=1, source_target_pairs={{0,64},{64,128},{128,192},{192,0},{1,65},{65,129},{129,193},{193,1... | collective-permute-start | bytes 688136 | tf_op jit(solution)/shard_map/ppermute | solution.py:83
  33.2 1.5 %collective-permute-start.7 = (f32[448,128]{1,0:T(8,128)S(1)}, f32[448,128]{1,0:T(8,128)S(1)}, u32[]{:S(2)}, u32[]{:S(2)}) collective-permute-start(f32[448,128]{1,0:T(8,128)S(1)} %get-tuple-element.34), channel_id=1, source_target_pairs={{0,192},{64,0},{128,64},{192,128},{1,193},{65,1},{129,65},{193,129... | collective-permute-start | bytes 688136 | tf_op jit(solution)/shard_map/ppermute | solution.py:83
  34.6 1.3 %collective-permute-start.8 = (f32[200,128]{1,0:T(8,128)S(1)}, f32[200,128]{1,0:T(8,128)S(1)}, u32[]{:S(2)}, u32[]{:S(2)}) collective-permute-start(f32[200,128]{1,0:T(8,128)S(1)} %get-tuple-element.32.own), channel_id=1, source_target_pairs={{0,128},{64,192},{128,0},{192,64},{1,129},{65,193},{129,1},{193,65... | collective-permute-start | bytes 307208 | tf_op jit(solution)/shard_map/ppermute | solution.py:83
  36.0 7.0 %collective-permute-done.8.far = f32[200,128]{1,0:T(8,128)S(1)} collective-permute-done((f32[200,128]{1,0:T(8,128)S(1)}, f32[200,128]{1,0:T(8,128)S(1)}, u32[]{:S(2)}, u32[]{:S(2)}) %collective-permute-start.8) | collective-permute-done | bytes 102432 | tf_op jit(solution)/shard_map/ppermute | solution.py:83
  43.0 4.1 %shard_map.44 = (f32[16,40,128]{2,1,0:T(8,128)S(1)}, f32[16,40,128]{2,1,0:T(8,128)S(1)}, f32[16,40,128]{2,1,0:T(8,128)S(1)}, f32[8,16,128]{2,1,0:T(8,128)S(1)}, ...) custom-call(f32[200,128]{1,0:T(8,128)S(1)} %get-tuple-element.32.own, ...), custom_call_target="tpu_custom_call" | custom-call | tf_op jit(solution)/shard_map/pallas_call | solution.py:71
  47.1 3.0 %collective-permute-start.9 = (f32[192,128]{1,0:T(8,128)S(1)}, f32[192,128]{1,0:T(8,128)S(1)}, u32[]{:S(2)}, u32[]{:S(2)}) collective-permute-start(f32[192,128]{1,0:T(8,128)S(1)} %get-tuple-element.39), channel_id=1, source_target_pairs={{0,8},{8,16},{16,24},{24,32},{32,40},{40,48},{48,56},{56,0},{1,9},... | collective-permute-start | bytes 294920 | tf_op jit(solution)/shard_map/ppermute | solution.py:83
  50.0 2.3 %collective-permute-done.9.below = f32[192,128]{1,0:T(8,128)S(1)} collective-permute-done((f32[192,128]{1,0:T(8,128)S(1)}, f32[192,128]{1,0:T(8,128)S(1)}, u32[]{:S(2)}, u32[]{:S(2)}) %collective-permute-start.9) | collective-permute-done | bytes 98336 | tf_op jit(solution)/shard_map/ppermute | solution.py:83
  52.3 2.0 %collective-permute-done.10.above = f32[192,128]{1,0:T(8,128)S(1)} collective-permute-done((f32[192,128]{1,0:T(8,128)S(1)}, f32[192,128]{1,0:T(8,128)S(1)}, u32[]{:S(2)}, u32[]{:S(2)}) %collective-permute-start.10) | collective-permute-done | bytes 98336 | tf_op jit(solution)/shard_map/ppermute | solution.py:83
  54.3 1.5 %shard_map.45 = (f32[8,32,128]{2,1,0:T(8,128)S(1)}, f32[8,32,128]{2,1,0:T(8,128)S(1)}, f32[16,48,128]{2,1,0:T(8,128)S(1)}, f32[16,48,128]{2,1,0:T(8,128)S(1)}, f...) custom-call(f32[8,16,128]{2,1,0:T(8,128)S(1)} %get-tuple-element.35.low_res, f32[8,16,128]{2,1,0:T(8,128)S(1)} %get-tuple-element.36.low_coef, ...), custom_call_target="tpu_custom_call" | custom-call | tf_op jit(solution)/shard_map/pallas_call | solution.py:71
  55.8 2.1 %collective-permute-start.11 = (f32[80,128]{1,0:T(8,128)S(1)}, f32[80,128]{1,0:T(8,128)S(1)}, u32[]{:S(2)}, u32[]{:S(2)}) collective-permute-start(f32[80,128]{1,0:T(8,128)S(1)} %get-tuple-element.43), channel_id=1, source_target_pairs={{0,1},{1,2},{2,3},{3,4},{4,5},{5,6},{6,7},{7,0},{8,9},{9,10},{10,1... | collective-permute-start | bytes 122888 | tf_op jit(solution)/shard_map/ppermute | solution.py:83
  59.0 3.5 %collective-permute-done.12.right = f32[80,128]{1,0:T(8,128)S(1)} collective-permute-done((f32[80,128]{1,0:T(8,128)S(1)}, f32[80,128]{1,0:T(8,128)S(1)}, u32[]{:S(2)}, u32[]{:S(2)}) %collective-permute-start.12) | collective-permute-done | bytes 40992 | tf_op jit(solution)/shard_map/ppermute | solution.py:83
  63.2 4.2 %shard_map.47.sol1 = f32[20,48,128]{2,1,0:T(8,128)S(1)} custom-call(f32[8,32,128]{2,1,0:T(8,128)S(1)} %shard_map.46.sol2, f32[16,48,128]{2,1,0:T(8,128)S(1)} %get-tuple-element.45.res1_in, f32[16,48,128]{2,1,0:T(8,128)S(1)} %get-tuple-element.46.sol1_in, f32[16,40,128]{2,1,0:T(8,128)S(1)} %get-tuple-element.47.coef1, ...), custom_call_target="tpu_custom_call" | custom-call | tf_op jit(solution)/shard_map/pallas_call | solution.py:71
  67.4 8.3 %shard_map.48 = (f32[8,64,128]{2,1,0:T(8,128)}, f32[8,64,128]{2,1,0:T(8,128)}) custom-call(f32[20,48,128]{2,1,0:T(8,128)S(1)} %shard_map.47.sol1, f32[8,64,128]{2,1,0:T(8,128)S(1)} %get-tuple-element.48.sol0, f32[8,72,256]{2,1,0:T(8,128)S(1)} %get-tuple-element.49.res_q, f32[14,72,256]{2,1,0:T(8,128)S(1)} %get-tuple-element.50.diag_q, ...), custom_call_target="tpu_custom_call" | custom-call | tf_op jit(solution)/shard_map/pallas_call | solution.py:71
  (17 shorter events, 2.5 us)
Async XLA Ops:
  0.6 8.4 %copy-start.1 = (f32[8,64,128]{2,1,0:T(8,128)S(1)}, f32[8,64,128]{2,1,0:T(8,128)}, u32[]{:S(2)}) copy-start(f32[8,64,128]{2,1,0:T(8,128)} %c.3) | copy-start | bytes 786436
  0.6 8.4 %copy-start = (f32[8,64,128]{2,1,0:T(8,128)S(1)}, f32[8,64,128]{2,1,0:T(8,128)}, u32[]{:S(2)}) copy-start(f32[8,64,128]{2,1,0:T(8,128)} %s.3) | copy-start | bytes 786436
  1.8 7.2 %collective-permute-start = (f32[6,64,128]{2,1,0:T(8,128)S(1)}, f32[6,64,128]{2,1,0:T(8,128)S(1)}, u32[]{:S(2)}, u32[]{:S(2)}) collective-permute-start(f32[6,64,128]{2,1,0:T(8,128)S(1)} %pad_maximum_fusion), channel_id=1, source_target_pairs={{0,64},{64,128},{128,192},{192,0},{1,65},{65,129},{129,193},{193,1... | collective-permute-start | bytes 589832 | tf_op jit(solution)/shard_map/ppermute | solution.py:83
  3.2 5.8 %collective-permute-start.1 = (f32[6,64,128]{2,1,0:T(8,128)S(1)}, f32[6,64,128]{2,1,0:T(8,128)S(1)}, u32[]{:S(2)}, u32[]{:S(2)}) collective-permute-start(f32[6,64,128]{2,1,0:T(8,128)S(1)} %pad_maximum_fusion.1), channel_id=1, source_target_pairs={{0,192},{64,0},{128,64},{192,128},{1,193},{65,1},{129,65},{193,129... | collective-permute-start | bytes 589832 | tf_op jit(solution)/shard_map/ppermute | solution.py:83
  9.0 3.9 %collective-permute-start.2 = (f32[256,128]{1,0:T(8,128)S(1)}, f32[256,128]{1,0:T(8,128)S(1)}, u32[]{:S(2)}, u32[]{:S(2)}) collective-permute-start(f32[256,128]{1,0:T(8,128)S(1)} %get-tuple-element.27), channel_id=1, source_target_pairs={{0,8},{8,16},{16,24},{24,32},{32,40},{40,48},{48,56},{56,0},{1,9},... | collective-permute-start | bytes 393224 | tf_op jit(solution)/shard_map/ppermute | solution.py:83
  10.8 5.2 %collective-permute-start.3 = (f32[256,128]{1,0:T(8,128)S(1)}, f32[256,128]{1,0:T(8,128)S(1)}, u32[]{:S(2)}, u32[]{:S(2)}) collective-permute-start(f32[256,128]{1,0:T(8,128)S(1)} %get-tuple-element.28), channel_id=1, source_target_pairs={{0,56},{8,0},{16,8},{24,16},{32,24},{40,32},{48,40},{56,48},{1,57}... | collective-permute-start | bytes 393224 | tf_op jit(solution)/shard_map/ppermute | solution.py:83
  16.7 4.4 %collective-permute-start.4 = (f32[2,88,128]{2,1,0:T(8,128)S(1)}, f32[2,88,128]{2,1,0:T(8,128)S(1)}, u32[]{:S(2)}, u32[]{:S(2)}) collective-permute-start(f32[2,88,128]{2,1,0:T(8,128)S(1)} %get-tuple-element.30), channel_id=1, source_target_pairs={{0,1},{1,2},{2,3},{3,4},{4,5},{5,6},{6,7},{7,0},{8,9},{9,10},{10,1... | collective-permute-start | bytes 270344 | tf_op jit(solution)/shard_map/ppermute | solution.py:83
  19.5 5.2 %collective-permute-start.5 = (f32[2,88,128]{2,1,0:T(8,128)S(1)}, f32[2,88,128]{2,1,0:T(8,128)S(1)}, u32[]{:S(2)}, u32[]{:S(2)}) collective-permute-start(f32[2,88,128]{2,1,0:T(8,128)S(1)} %get-tuple-element.31), channel_id=1, source_target_pairs={{0,7},{1,0},{2,1},{3,2},{4,3},{5,4},{6,5},{7,6},{8,15},{9,8},{10,9... | collective-permute-start | bytes 270344 | tf_op jit(solution)/shard_map/ppermute | solution.py:83
  31.8 11.2 %collective-permute-start.6 = (f32[448,128]{1,0:T(8,128)S(1)}, f32[448,128]{1,0:T(8,128)S(1)}, u32[]{:S(2)}, u32[]{:S(2)}) collective-permute-start(f32[448,128]{1,0:T(8,128)S(1)} %get-tuple-element.33), channel_id=1, source_target_pairs={{0,64},{64,128},{128,192},{192,0},{1,65},{65,129},{129,193},{193,1... | collective-permute-start | bytes 688136 | tf_op jit(solution)/shard_map/ppermute | solution.py:83
  33.2 9.8 %collective-permute-start.7 = (f32[448,128]{1,0:T(8,128)S(1)}, f32[448,128]{1,0:T(8,128)S(1)}, u32[]{:S(2)}, u32[]{:S(2)}) collective-permute-start(f32[448,128]{1,0:T(8,128)S(1)} %get-tuple-element.34), channel_id=1, source_target_pairs={{0,192},{64,0},{128,64},{192,128},{1,193},{65,1},{129,65},{193,129... | collective-permute-start | bytes 688136 | tf_op jit(solution)/shard_map/ppermute | solution.py:83
  34.6 8.3 %collective-permute-start.8 = (f32[200,128]{1,0:T(8,128)S(1)}, f32[200,128]{1,0:T(8,128)S(1)}, u32[]{:S(2)}, u32[]{:S(2)}) collective-permute-start(f32[200,128]{1,0:T(8,128)S(1)} %get-tuple-element.32.own), channel_id=1, source_target_pairs={{0,128},{64,192},{128,0},{192,64},{1,129},{65,193},{129,1},{193,65... | collective-permute-start | bytes 307208 | tf_op jit(solution)/shard_map/ppermute | solution.py:83
  47.1 5.2 %collective-permute-start.9 = (f32[192,128]{1,0:T(8,128)S(1)}, f32[192,128]{1,0:T(8,128)S(1)}, u32[]{:S(2)}, u32[]{:S(2)}) collective-permute-start(f32[192,128]{1,0:T(8,128)S(1)} %get-tuple-element.39), channel_id=1, source_target_pairs={{0,8},{8,16},{16,24},{24,32},{32,40},{40,48},{48,56},{56,0},{1,9},... | collective-permute-start | bytes 294920 | tf_op jit(solution)/shard_map/ppermute | solution.py:83
  50.0 4.2 %collective-permute-start.10 = (f32[192,128]{1,0:T(8,128)S(1)}, f32[192,128]{1,0:T(8,128)S(1)}, u32[]{:S(2)}, u32[]{:S(2)}) collective-permute-start(f32[192,128]{1,0:T(8,128)S(1)} %get-tuple-element.40), channel_id=1, source_target_pairs={{0,56},{8,0},{16,8},{24,16},{32,24},{40,32},{48,40},{56,48},{1,57}... | collective-permute-start | bytes 294920 | tf_op jit(solution)/shard_map/ppermute | solution.py:83
  55.8 3.2 %collective-permute-start.11 = (f32[80,128]{1,0:T(8,128)S(1)}, f32[80,128]{1,0:T(8,128)S(1)}, u32[]{:S(2)}, u32[]{:S(2)}) collective-permute-start(f32[80,128]{1,0:T(8,128)S(1)} %get-tuple-element.43), channel_id=1, source_target_pairs={{0,1},{1,2},{2,3},{3,4},{4,5},{5,6},{6,7},{7,0},{8,9},{9,10},{10,1... | collective-permute-start | bytes 122888 | tf_op jit(solution)/shard_map/ppermute | solution.py:83
  57.9 4.6 %collective-permute-start.12 = (f32[80,128]{1,0:T(8,128)S(1)}, f32[80,128]{1,0:T(8,128)S(1)}, u32[]{:S(2)}, u32[]{:S(2)}) collective-permute-start(f32[80,128]{1,0:T(8,128)S(1)} %get-tuple-element.44), channel_id=1, source_target_pairs={{0,7},{1,0},{2,1},{3,2},{4,3},{5,4},{6,5},{7,6},{8,15},{9,8},{10,9... | collective-permute-start | bytes 122888 | tf_op jit(solution)/shard_map/ppermute | solution.py:83

commit v3 on v2

--- a/solution.py
+++ b/solution.py
@@ -137,7 +137,7 @@
             dst[x] = pair[0] * d + (pair[1] * inverse[x]) * r
         return carry
 
-    lax.fori_loop(first, stop, body, 0)
+    lax.fori_loop(first, stop, body, 0, unroll=True)
 
 
 def to_q0(ref, x):
@@ -186,7 +186,7 @@
         inv_q[x, 64:72, :] = tail
         return carry
 
-    lax.fori_loop(0, NXE, start, 0)
+    lax.fori_loop(0, NXE, start, 0, unroll=True)
 
     pairs = coefficients(SWEEPS)
     buffers = (da, db)
@@ -204,7 +204,7 @@
             sol[x] = own if k == 0 else sol[x] + own
             return carry
 
-        lax.fori_loop(0, NX0, gather, 0)
+        lax.fori_loop(0, NX0, gather, 0, unroll=True)
 
     def keep(x, carry):
         top, tail = to_q0(res, XH + x)
@@ -212,7 +212,7 @@
         res_q[x, 64:72, :] = tail
         return carry
 
-    lax.fori_loop(0, NX0, keep, 0)
+    lax.fori_loop(0, NX0, keep, 0, unroll=True)
 
     lane40 = lanes_of((R1, 128))
     halo = jnp.zeros((R1, 128), F32)
@@ -287,7 +287,7 @@
         sol[x] = d
         return carry
 
-    lax.fori_loop(0, 16, start, 0)
+    lax.fori_loop(0, 16, start, 0, unroll=True)
     pairs = coefficients(SWEEPS)
     buffers = (da, db)
     for k in range(SWEEPS):
@@ -426,7 +426,7 @@
         sol1[x + 2] += d
         return carry
 
-    lax.fori_loop(0, 16, correct1, 0)
+    lax.fori_loop(0, 16, correct1, 0, unroll=True)
     pairs = coefficients(SWEEPS)
     buffers = (da1, db1)
     for k in range(SWEEPS - 1):
@@ -460,7 +460,7 @@
         res0[x + XH] = res_q[x]
         return carry
 
-    lax.fori_loop(0, NX0, fetch, 0)
+    lax.fori_loop(0, NX0, fetch, 0, unroll=True)
 
     def correct0(x, carry):
         p = p0[x + 1]
@@ -470,13 +470,13 @@
         da0[x] = r * inv_q[x] * (1.0 / THETA)
         return carry
 
-    lax.fori_loop(0, NXE, correct0, 0)
+    lax.fori_loop(0, NXE, correct0, 0, unroll=True)
 
     def begin(x, carry):
         out_sol[x] = sol0[x] + p0[x + XH + 1, 0:64, 0:128]
         return carry
 
-    lax.fori_loop(0, NX0, begin, 0)
+    lax.fori_loop(0, NX0, begin, 0, unroll=True)
     pairs = coefficients(SWEEPS)
     buffers = (da0, db0)
     for k in range(SWEEPS):
@@ -486,7 +486,7 @@
             out_sol[x] += src[x + XH, 0:64, 0:128]
             return carry
 
-        lax.fori_loop(0, NX0, gather0, 0)
+        lax.fori_loop(0, NX0, gather0, 0, unroll=True)
         fine_sweep(
             src, dst, res0, diag_q, inv_q, k + 1, NXE - 1 - k, pairs[k] if k < SWEEPS - 1 else None,
             lambda x, d: None,
@@ -496,7 +496,7 @@
         out_res[x] = res0[x + XH, 0:64, 0:128]
         return carry
 
-    lax.fori_loop(0, NX0, put, 0)
+    lax.fori_loop(0, NX0, put, 0, unroll=True)
 
 
 def per_device(s, c):

time: 75.8 us -> 66.2 us (0.87)
  Pallas kernels: 26.7 us -> 17.1 us
    pallas_call x8, Pallas kernels: 26.7 us -> 17.1 us  [call(): pl.pallas_call(body, out_shape=[jax.ShapeDtypeStruct(s, F32) for s in out...]
where the time goes in v3:
time: 66.2 us; the launch traced here: 66.1 us
  waiting for transfers between devices  30.5 us (46%)
  Pallas kernels  17.1 us (26%)
  starting transfers between devices  16.7 us (25%)
  local copies, waits for them, and re-layouts  1.13 us (2%)
  between operations  0.73 us (1%)
    ppermute x13, waiting for transfers between devices, ring(): lax.ppermute(value, axis, [(i, (i + shift) % size) for i in range(size)])  30.5 us
    pallas_call x8, Pallas kernels, call(): pl.pallas_call(body, out_shape=[jax.ShapeDtypeStruct(s, F32) for s in out...  17.1 us
    ppermute x13, starting transfers between devices, ring(): lax.ppermute(value, axis, [(i, (i + shift) % size) for i in range(size)])  16.7 us
  transfers between devices with their start and end apart: 13, of which 10 were waited for; matrix products, arithmetic and copies ran while one was open for 0% of the time, Pallas kernels for 0%

profile of v3, /device:TPU:71, one launch (start us, length us, event | category | flops | bytes accessed | tf_op | source)
XLA Modules:
  0.0 66.1 jit_solution(7374893677347167858)
XLA Ops:
  0.6 1.1 %fusion = (f32[3,64,128]{2,1,0:T(8,128)S(1)}, f32[3,64,128]{2,1,0:T(8,128)S(1)}, f32[3,64,128]{2,1,0:T(8,128)S(1)}, f32[3,64,128]{2,1,0:T(8,128)S(1)}) fusion(f32[8,64,128]{2,1,0:T(8,128)} %s.3, f32[8,64,128]{2,1,0:T(8,128)} %c.3), kind=kLoop, calls=%fused_computation.2 | loop fusion | bytes 786432 | tf_op jit(solution)/shard_map/slice | solution.py:504
  1.8 1.4 %collective-permute-start = (f32[6,64,128]{2,1,0:T(8,128)S(1)}, f32[6,64,128]{2,1,0:T(8,128)S(1)}, u32[]{:S(2)}, u32[]{:S(2)}) collective-permute-start(f32[6,64,128]{2,1,0:T(8,128)S(1)} %pad_maximum_fusion), channel_id=1, source_target_pairs={{0,64},{64,128},{128,192},{192,0},{1,65},{65,129},{129,193},{193,1... | collective-permute-start | bytes 589832 | tf_op jit(solution)/shard_map/ppermute | solution.py:83
  3.2 1.5 %collective-permute-start.1 = (f32[6,64,128]{2,1,0:T(8,128)S(1)}, f32[6,64,128]{2,1,0:T(8,128)S(1)}, u32[]{:S(2)}, u32[]{:S(2)}) collective-permute-start(f32[6,64,128]{2,1,0:T(8,128)S(1)} %pad_maximum_fusion.1), channel_id=1, source_target_pairs={{0,192},{64,0},{128,64},{192,128},{1,193},{65,1},{129,65},{193,129... | collective-permute-start | bytes 589832 | tf_op jit(solution)/shard_map/ppermute | solution.py:83
  4.7 4.3 %collective-permute-done.low = f32[6,64,128]{2,1,0:T(8,128)S(1)} collective-permute-done((f32[6,64,128]{2,1,0:T(8,128)S(1)}, f32[6,64,128]{2,1,0:T(8,128)S(1)}, u32[]{:S(2)}, u32[]{:S(2)}) %collective-permute-start) | collective-permute-done | bytes 196640 | tf_op jit(solution)/shard_map/ppermute | solution.py:83
  9.0 1.7 %collective-permute-start.2 = (f32[256,128]{1,0:T(8,128)S(1)}, f32[256,128]{1,0:T(8,128)S(1)}, u32[]{:S(2)}, u32[]{:S(2)}) collective-permute-start(f32[256,128]{1,0:T(8,128)S(1)} %get-tuple-element.27), channel_id=1, source_target_pairs={{0,8},{8,16},{16,24},{24,32},{32,40},{40,48},{48,56},{56,0},{1,9},... | collective-permute-start | bytes 393224 | tf_op jit(solution)/shard_map/ppermute | solution.py:83
  10.8 2.2 %collective-permute-done.2.below = f32[256,128]{1,0:T(8,128)S(1)} collective-permute-done((f32[256,128]{1,0:T(8,128)S(1)}, f32[256,128]{1,0:T(8,128)S(1)}, u32[]{:S(2)}, u32[]{:S(2)}) %collective-permute-start.2) | collective-permute-done | bytes 131104 | tf_op jit(solution)/shard_map/ppermute | solution.py:83
  12.9 3.0 %collective-permute-done.3.above = f32[256,128]{1,0:T(8,128)S(1)} collective-permute-done((f32[256,128]{1,0:T(8,128)S(1)}, f32[256,128]{1,0:T(8,128)S(1)}, u32[]{:S(2)}, u32[]{:S(2)}) %collective-permute-start.3) | collective-permute-done | bytes 131104 | tf_op jit(solution)/shard_map/ppermute | solution.py:83
  16.7 2.8 %collective-permute-start.4 = (f32[2,88,128]{2,1,0:T(8,128)S(1)}, f32[2,88,128]{2,1,0:T(8,128)S(1)}, u32[]{:S(2)}, u32[]{:S(2)}) collective-permute-start(f32[2,88,128]{2,1,0:T(8,128)S(1)} %get-tuple-element.30), channel_id=1, source_target_pairs={{0,1},{1,2},{2,3},{3,4},{4,5},{5,6},{6,7},{7,0},{8,9},{9,10},{10,1... | collective-permute-start | bytes 270344 | tf_op jit(solution)/shard_map/ppermute | solution.py:83
  19.5 1.6 %collective-permute-done.4.below = f32[2,88,128]{2,1,0:T(8,128)S(1)} collective-permute-done((f32[2,88,128]{2,1,0:T(8,128)S(1)}, f32[2,88,128]{2,1,0:T(8,128)S(1)}, u32[]{:S(2)}, u32[]{:S(2)}) %collective-permute-start.4) | collective-permute-done | bytes 90144 | tf_op jit(solution)/shard_map/ppermute | solution.py:83
  21.1 3.6 %collective-permute-done.5.above = f32[2,88,128]{2,1,0:T(8,128)S(1)} collective-permute-done((f32[2,88,128]{2,1,0:T(8,128)S(1)}, f32[2,88,128]{2,1,0:T(8,128)S(1)}, u32[]{:S(2)}, u32[]{:S(2)}) %collective-permute-start.5) | collective-permute-done | bytes 90144 | tf_op jit(solution)/shard_map/ppermute | solution.py:83
  24.7 4.1 %shard_map.43 = (f32[8,64,128]{2,1,0:T(8,128)S(1)}, f32[8,72,256]{2,1,0:T(8,128)S(1)}, f32[14,72,256]{2,1,0:T(8,128)S(1)}, f32[14,72,256]{2,1,0:T(8,128)S(1)}, f...) custom-call(f32[2,14,88,128]{3,2,1,0:T(8,128)S(1)} %get-tuple-element.29.main, ...), custom_call_target="tpu_custom_call" | custom-call | tf_op jit(solution)/shard_map/pallas_call | solution.py:71
  28.7 1.4 %collective-permute-start.6 = (f32[448,128]{1,0:T(8,128)S(1)}, f32[448,128]{1,0:T(8,128)S(1)}, u32[]{:S(2)}, u32[]{:S(2)}) collective-permute-start(f32[448,128]{1,0:T(8,128)S(1)} %get-tuple-element.33), channel_id=1, source_target_pairs={{0,64},{64,128},{128,192},{192,0},{1,65},{65,129},{129,193},{193,1... | collective-permute-start | bytes 688136 | tf_op jit(solution)/shard_map/ppermute | solution.py:83
  30.1 1.5 %collective-permute-start.7 = (f32[448,128]{1,0:T(8,128)S(1)}, f32[448,128]{1,0:T(8,128)S(1)}, u32[]{:S(2)}, u32[]{:S(2)}) collective-permute-start(f32[448,128]{1,0:T(8,128)S(1)} %get-tuple-element.34), channel_id=1, source_target_pairs={{0,192},{64,0},{128,64},{192,128},{1,193},{65,1},{129,65},{193,129... | collective-permute-start | bytes 688136 | tf_op jit(solution)/shard_map/ppermute | solution.py:83
  31.6 1.3 %collective-permute-start.8 = (f32[200,128]{1,0:T(8,128)S(1)}, f32[200,128]{1,0:T(8,128)S(1)}, u32[]{:S(2)}, u32[]{:S(2)}) collective-permute-start(f32[200,128]{1,0:T(8,128)S(1)} %get-tuple-element.32.own), channel_id=1, source_target_pairs={{0,128},{64,192},{128,0},{192,64},{1,129},{65,193},{129,1},{193,65... | collective-permute-start | bytes 307208 | tf_op jit(solution)/shard_map/ppermute | solution.py:83
  32.9 7.0 %collective-permute-done.8.far = f32[200,128]{1,0:T(8,128)S(1)} collective-permute-done((f32[200,128]{1,0:T(8,128)S(1)}, f32[200,128]{1,0:T(8,128)S(1)}, u32[]{:S(2)}, u32[]{:S(2)}) %collective-permute-start.8) | collective-permute-done | bytes 102432 | tf_op jit(solution)/shard_map/ppermute | solution.py:83
  39.9 3.8 %shard_map.44 = (f32[16,40,128]{2,1,0:T(8,128)S(1)}, f32[16,40,128]{2,1,0:T(8,128)S(1)}, f32[16,40,128]{2,1,0:T(8,128)S(1)}, f32[8,16,128]{2,1,0:T(8,128)S(1)}, ...) custom-call(f32[200,128]{1,0:T(8,128)S(1)} %get-tuple-element.32.own, ...), custom_call_target="tpu_custom_call" | custom-call | tf_op jit(solution)/shard_map/pallas_call | solution.py:71
  43.7 3.0 %collective-permute-start.9 = (f32[192,128]{1,0:T(8,128)S(1)}, f32[192,128]{1,0:T(8,128)S(1)}, u32[]{:S(2)}, u32[]{:S(2)}) collective-permute-start(f32[192,128]{1,0:T(8,128)S(1)} %get-tuple-element.39), channel_id=1, source_target_pairs={{0,8},{8,16},{16,24},{24,32},{32,40},{40,48},{48,56},{56,0},{1,9},... | collective-permute-start | bytes 294920 | tf_op jit(solution)/shard_map/ppermute | solution.py:83
  46.7 2.3 %collective-permute-done.9.below = f32[192,128]{1,0:T(8,128)S(1)} collective-permute-done((f32[192,128]{1,0:T(8,128)S(1)}, f32[192,128]{1,0:T(8,128)S(1)}, u32[]{:S(2)}, u32[]{:S(2)}) %collective-permute-start.9) | collective-permute-done | bytes 98336 | tf_op jit(solution)/shard_map/ppermute | solution.py:83
  49.0 2.0 %collective-permute-done.10.above = f32[192,128]{1,0:T(8,128)S(1)} collective-permute-done((f32[192,128]{1,0:T(8,128)S(1)}, f32[192,128]{1,0:T(8,128)S(1)}, u32[]{:S(2)}, u32[]{:S(2)}) %collective-permute-start.10) | collective-permute-done | bytes 98336 | tf_op jit(solution)/shard_map/ppermute | solution.py:83
  51.0 1.5 %shard_map.45 = (f32[8,32,128]{2,1,0:T(8,128)S(1)}, f32[8,32,128]{2,1,0:T(8,128)S(1)}, f32[16,48,128]{2,1,0:T(8,128)S(1)}, f32[16,48,128]{2,1,0:T(8,128)S(1)}, f...) custom-call(f32[8,16,128]{2,1,0:T(8,128)S(1)} %get-tuple-element.35.low_res, f32[8,16,128]{2,1,0:T(8,128)S(1)} %get-tuple-element.36.low_coef, ...), custom_call_target="tpu_custom_call" | custom-call | tf_op jit(solution)/shard_map/pallas_call | solution.py:71
  52.5 2.1 %collective-permute-start.11 = (f32[80,128]{1,0:T(8,128)S(1)}, f32[80,128]{1,0:T(8,128)S(1)}, u32[]{:S(2)}, u32[]{:S(2)}) collective-permute-start(f32[80,128]{1,0:T(8,128)S(1)} %get-tuple-element.43), channel_id=1, source_target_pairs={{0,1},{1,2},{2,3},{3,4},{4,5},{5,6},{6,7},{7,0},{8,9},{9,10},{10,1... | collective-permute-start | bytes 122888 | tf_op jit(solution)/shard_map/ppermute | solution.py:83
  55.7 3.5 %collective-permute-done.12.right = f32[80,128]{1,0:T(8,128)S(1)} collective-permute-done((f32[80,128]{1,0:T(8,128)S(1)}, f32[80,128]{1,0:T(8,128)S(1)}, u32[]{:S(2)}, u32[]{:S(2)}) %collective-permute-start.12) | collective-permute-done | bytes 40992 | tf_op jit(solution)/shard_map/ppermute | solution.py:83
  59.8 2.5 %shard_map.47.sol1 = f32[20,48,128]{2,1,0:T(8,128)S(1)} custom-call(f32[8,32,128]{2,1,0:T(8,128)S(1)} %shard_map.46.sol2, f32[16,48,128]{2,1,0:T(8,128)S(1)} %get-tuple-element.45.res1_in, f32[16,48,128]{2,1,0:T(8,128)S(1)} %get-tuple-element.46.sol1_in, f32[16,40,128]{2,1,0:T(8,128)S(1)} %get-tuple-element.47.coef1, ...), custom_call_target="tpu_custom_call" | custom-call | tf_op jit(solution)/shard_map/pallas_call | solution.py:71
  62.4 3.7 %shard_map.48 = (f32[8,64,128]{2,1,0:T(8,128)}, f32[8,64,128]{2,1,0:T(8,128)}) custom-call(f32[20,48,128]{2,1,0:T(8,128)S(1)} %shard_map.47.sol1, f32[8,64,128]{2,1,0:T(8,128)S(1)} %get-tuple-element.48.sol0, f32[8,72,256]{2,1,0:T(8,128)S(1)} %get-tuple-element.49.res_q, f32[14,72,256]{2,1,0:T(8,128)S(1)} %get-tuple-element.50.diag_q, ...), custom_call_target="tpu_custom_call" | custom-call | tf_op jit(solution)/shard_map/pallas_call | solution.py:71
  (17 shorter events, 2.5 us)
Async XLA Ops:
  0.6 8.4 %copy-start.1 = (f32[8,64,128]{2,1,0:T(8,128)S(1)}, f32[8,64,128]{2,1,0:T(8,128)}, u32[]{:S(2)}) copy-start(f32[8,64,128]{2,1,0:T(8,128)} %c.3) | copy-start | bytes 786436
  0.6 8.4 %copy-start = (f32[8,64,128]{2,1,0:T(8,128)S(1)}, f32[8,64,128]{2,1,0:T(8,128)}, u32[]{:S(2)}) copy-start(f32[8,64,128]{2,1,0:T(8,128)} %s.3) | copy-start | bytes 786436
  1.8 7.2 %collective-permute-start = (f32[6,64,128]{2,1,0:T(8,128)S(1)}, f32[6,64,128]{2,1,0:T(8,128)S(1)}, u32[]{:S(2)}, u32[]{:S(2)}) collective-permute-start(f32[6,64,128]{2,1,0:T(8,128)S(1)} %pad_maximum_fusion), channel_id=1, source_target_pairs={{0,64},{64,128},{128,192},{192,0},{1,65},{65,129},{129,193},{193,1... | collective-permute-start | bytes 589832 | tf_op jit(solution)/shard_map/ppermute | solution.py:83
  3.2 5.8 %collective-permute-start.1 = (f32[6,64,128]{2,1,0:T(8,128)S(1)}, f32[6,64,128]{2,1,0:T(8,128)S(1)}, u32[]{:S(2)}, u32[]{:S(2)}) collective-permute-start(f32[6,64,128]{2,1,0:T(8,128)S(1)} %pad_maximum_fusion.1), channel_id=1, source_target_pairs={{0,192},{64,0},{128,64},{192,128},{1,193},{65,1},{129,65},{193,129... | collective-permute-start | bytes 589832 | tf_op jit(solution)/shard_map/ppermute | solution.py:83
  9.0 3.9 %collective-permute-start.2 = (f32[256,128]{1,0:T(8,128)S(1)}, f32[256,128]{1,0:T(8,128)S(1)}, u32[]{:S(2)}, u32[]{:S(2)}) collective-permute-start(f32[256,128]{1,0:T(8,128)S(1)} %get-tuple-element.27), channel_id=1, source_target_pairs={{0,8},{8,16},{16,24},{24,32},{32,40},{40,48},{48,56},{56,0},{1,9},... | collective-permute-start | bytes 393224 | tf_op jit(solution)/shard_map/ppermute | solution.py:83
  10.8 5.2 %collective-permute-start.3 = (f32[256,128]{1,0:T(8,128)S(1)}, f32[256,128]{1,0:T(8,128)S(1)}, u32[]{:S(2)}, u32[]{:S(2)}) collective-permute-start(f32[256,128]{1,0:T(8,128)S(1)} %get-tuple-element.28), channel_id=1, source_target_pairs={{0,56},{8,0},{16,8},{24,16},{32,24},{40,32},{48,40},{56,48},{1,57}... | collective-permute-start | bytes 393224 | tf_op jit(solution)/shard_map/ppermute | solution.py:83
  16.7 4.4 %collective-permute-start.4 = (f32[2,88,128]{2,1,0:T(8,128)S(1)}, f32[2,88,128]{2,1,0:T(8,128)S(1)}, u32[]{:S(2)}, u32[]{:S(2)}) collective-permute-start(f32[2,88,128]{2,1,0:T(8,128)S(1)} %get-tuple-element.30), channel_id=1, source_target_pairs={{0,1},{1,2},{2,3},{3,4},{4,5},{5,6},{6,7},{7,0},{8,9},{9,10},{10,1... | collective-permute-start | bytes 270344 | tf_op jit(solution)/shard_map/ppermute | solution.py:83
  19.5 5.2 %collective-permute-start.5 = (f32[2,88,128]{2,1,0:T(8,128)S(1)}, f32[2,88,128]{2,1,0:T(8,128)S(1)}, u32[]{:S(2)}, u32[]{:S(2)}) collective-permute-start(f32[2,88,128]{2,1,0:T(8,128)S(1)} %get-tuple-element.31), channel_id=1, source_target_pairs={{0,7},{1,0},{2,1},{3,2},{4,3},{5,4},{6,5},{7,6},{8,15},{9,8},{10,9... | collective-permute-start | bytes 270344 | tf_op jit(solution)/shard_map/ppermute | solution.py:83
  28.7 11.2 %collective-permute-start.6 = (f32[448,128]{1,0:T(8,128)S(1)}, f32[448,128]{1,0:T(8,128)S(1)}, u32[]{:S(2)}, u32[]{:S(2)}) collective-permute-start(f32[448,128]{1,0:T(8,128)S(1)} %get-tuple-element.33), channel_id=1, source_target_pairs={{0,64},{64,128},{128,192},{192,0},{1,65},{65,129},{129,193},{193,1... | collective-permute-start | bytes 688136 | tf_op jit(solution)/shard_map/ppermute | solution.py:83
  30.1 9.8 %collective-permute-start.7 = (f32[448,128]{1,0:T(8,128)S(1)}, f32[448,128]{1,0:T(8,128)S(1)}, u32[]{:S(2)}, u32[]{:S(2)}) collective-permute-start(f32[448,128]{1,0:T(8,128)S(1)} %get-tuple-element.34), channel_id=1, source_target_pairs={{0,192},{64,0},{128,64},{192,128},{1,193},{65,1},{129,65},{193,129... | collective-permute-start | bytes 688136 | tf_op jit(solution)/shard_map/ppermute | solution.py:83
  31.6 8.3 %collective-permute-start.8 = (f32[200,128]{1,0:T(8,128)S(1)}, f32[200,128]{1,0:T(8,128)S(1)}, u32[]{:S(2)}, u32[]{:S(2)}) collective-permute-start(f32[200,128]{1,0:T(8,128)S(1)} %get-tuple-element.32.own), channel_id=1, source_target_pairs={{0,128},{64,192},{128,0},{192,64},{1,129},{65,193},{129,1},{193,65... | collective-permute-start | bytes 307208 | tf_op jit(solution)/shard_map/ppermute | solution.py:83
  43.7 5.2 %collective-permute-start.9 = (f32[192,128]{1,0:T(8,128)S(1)}, f32[192,128]{1,0:T(8,128)S(1)}, u32[]{:S(2)}, u32[]{:S(2)}) collective-permute-start(f32[192,128]{1,0:T(8,128)S(1)} %get-tuple-element.39), channel_id=1, source_target_pairs={{0,8},{8,16},{16,24},{24,32},{32,40},{40,48},{48,56},{56,0},{1,9},... | collective-permute-start | bytes 294920 | tf_op jit(solution)/shard_map/ppermute | solution.py:83
  46.7 4.2 %collective-permute-start.10 = (f32[192,128]{1,0:T(8,128)S(1)}, f32[192,128]{1,0:T(8,128)S(1)}, u32[]{:S(2)}, u32[]{:S(2)}) collective-permute-start(f32[192,128]{1,0:T(8,128)S(1)} %get-tuple-element.40), channel_id=1, source_target_pairs={{0,56},{8,0},{16,8},{24,16},{32,24},{40,32},{48,40},{56,48},{1,57}... | collective-permute-start | bytes 294920 | tf_op jit(solution)/shard_map/ppermute | solution.py:83
  52.5 3.2 %collective-permute-start.11 = (f32[80,128]{1,0:T(8,128)S(1)}, f32[80,128]{1,0:T(8,128)S(1)}, u32[]{:S(2)}, u32[]{:S(2)}) collective-permute-start(f32[80,128]{1,0:T(8,128)S(1)} %get-tuple-element.43), channel_id=1, source_target_pairs={{0,1},{1,2},{2,3},{3,4},{4,5},{5,6},{6,7},{7,0},{8,9},{9,10},{10,1... | collective-permute-start | bytes 122888 | tf_op jit(solution)/shard_map/ppermute | solution.py:83
  54.6 4.6 %collective-permute-start.12 = (f32[80,128]{1,0:T(8,128)S(1)}, f32[80,128]{1,0:T(8,128)S(1)}, u32[]{:S(2)}, u32[]{:S(2)}) collective-permute-start(f32[80,128]{1,0:T(8,128)S(1)} %get-tuple-element.44), channel_id=1, source_target_pairs={{0,7},{1,0},{2,1},{3,2},{4,3},{5,4},{6,5},{7,6},{8,15},{9,8},{10,9... | collective-permute-start | bytes 122888 | tf_op jit(solution)/shard_map/ppermute | solution.py:83

commit v4 on v3

v4 whole, which is shorter than its diff:
```python
import jax
import jax.numpy as jnp
from jax import lax
from jax.experimental import pallas as pl
from jax.experimental.pallas import tpu as pltpu
from jax.sharding import PartitionSpec as P

SWEEPS = 3
COARSE_SWEEPS = 6
THETA = 1.25
DELTA = 0.75
F32 = jnp.float32

XH = 3
NX0, NY0, NZ0 = 8, 64, 128
NXE = NX0 + 2 * XH
W = 9
R0 = 88
Q0 = 72
R1 = 40
Q1 = 48
R2 = 32
MIB = 1024 * 1024


def coefficients(count):
    sigma = THETA / DELTA
    rho = 1.0 / sigma
    pairs = []
    for _ in range(count):
        rho_new = 1.0 / (2.0 * sigma - rho)
        pairs.append((rho_new * rho, 2.0 * rho_new / DELTA))
        rho = rho_new
    return pairs


def turn(value, shift, axis):
    return pltpu.roll(value, shift % value.shape[axis], axis)


def beside(value):
    return (turn(value, 1, 0) + turn(value, -1, 0)) + (turn(value, 1, 1) + turn(value, -1, 1))


def rows_of(shape):
    return lax.broadcasted_iota(jnp.int32, shape, 0)


def lanes_of(shape):
    return lax.broadcasted_iota(jnp.int32, shape, 1)


def inside_yz(shape, own_rows, split_row, own_lanes, split_lane):
    gy, gz = lax.axis_index("gy"), lax.axis_index("gz")
    last_y, last_z = lax.axis_size("gy") - 1, lax.axis_size("gz") - 1
    row, lane = rows_of(shape), lanes_of(shape)
    up_y, down_y = (gy < last_y).astype(jnp.int32), (gy > 0).astype(jnp.int32)
    up_z, down_z = (gz < last_z).astype(jnp.int32), (gz > 0).astype(jnp.int32)
    in_y = jnp.where(row < own_rows, 1, jnp.where(row < split_row, up_y, down_y))
    in_z = jnp.where(lane < own_lanes, 1, jnp.where(lane < split_lane, up_z, down_z))
    return (in_y * in_z) > 0


def pick(value, lane):
    return jnp.take_along_axis(value, lane, axis=1, mode="promise_in_bounds")


def pairs_of_lanes(value):
    lane = lanes_of(value.shape)
    return pick(value + turn(value, -1, 1), 2 * lane - jnp.where(lane < 64, 0, 128))


def call(body, limit, outs, scratch, *args, micros=1.0):
    vmem = pl.BlockSpec(memory_space=pltpu.VMEM)
    return pl.pallas_call(
        body,
        out_shape=[jax.ShapeDtypeStruct(s, F32) for s in outs],
        in_specs=[vmem] * len(args),
        out_specs=[vmem] * len(outs),
        scratch_shapes=[pltpu.VMEM(s, F32) for s in scratch],
        compiler_params=pltpu.CompilerParams(vmem_limit_bytes=limit * MIB),
        cost_estimate=pl.CostEstimate(flops=0, bytes_accessed=int(micros * 3690000), transcendentals=0),
    )(*args)


def ring(value, axis, shift):
    size = lax.axis_size(axis)
    return lax.ppermute(value, axis, [(i, (i + shift) % size) for i in range(size)])


def plane_of(own, low, high, which, x):
    if x < XH:
        return low.at[which * XH + x]
    if x < XH + NX0:
        return own[which].at[x - XH]
    return high.at[which * XH + x - XH - NX0]


def pack_y(s, c, low, high, up, down):
    for a in range(2):
        for x in range(NXE):
            src = plane_of((s, c), low, high, a, x)
            at = a * NXE + x
            up[at * 8 : at * 8 + 8, :] = src[56:64, :]
            down[at * 8 : at * 8 + 8, :] = src[0:8, :]
            up[224 + at : 225 + at, :] = src[55:56, :]
            down[224 + at : 225 + at, :] = src[8:9, :]
    up[252:256, :] = jnp.zeros((4, 128), F32)
    down[252:256, :] = jnp.zeros((4, 128), F32)


def pack_wide(up, down, row, count, plane):
    lane = lanes_of((count, 128))
    for a in range(2):
        ups = jnp.zeros((count, 128), F32)
        downs = jnp.zeros((count, 128), F32)
        for x in range(NXE):
            v = plane(a, x)
            here = (lane >= W * x) & (lane < W * x + W)
            ups = jnp.where(here, turn(v, W * x - (128 - W), 1), ups)
            downs = jnp.where(here, turn(v, W * x, 1), downs)
        up[a, row : row + count, :] = ups
        down[a, row : row + count, :] = downs


def halo_rows(below, above, a, x):
    at = a * NXE + x
    row = rows_of((8, 128))
    middle = jnp.where(row == 0, above[224 + at : 225 + at, :], 0.0)
    middle = jnp.where(row == 7, below[224 + at : 225 + at, :], middle)
    return jnp.concatenate([above[at * 8 : at * 8 + 8, :], middle, below[at * 8 : at * 8 + 8, :]], 0)


def pack_z_own(s, c, low, high, up, down):
    pack_wide(up, down, 0, 64, lambda a, x: plane_of((s, c), low, high, a, x)[...])


def pack_z_halo(own_up, own_down, below, above, up, down):
    up[:, 0:64, :] = own_up[...]
    down[:, 0:64, :] = own_down[...]
    pack_wide(up, down, 64, 24, lambda a, x: halo_rows(below, above, a, x))


def fine_sweep(src, dst, res, diag, inverse, first, stop, pair, also):
    def body(x, carry):
        d = src[x]
        near = beside(d) + (src[x - 1] + src[x + 1])
        r = res[x] - (diag[x] * d - near)
        res[x] = r
        also(x, d)
        if pair is not None:
            dst[x] = pair[0] * d + (pair[1] * inverse[x]) * r
        return carry

    lax.fori_loop(first, stop, body, 0, unroll=True)


def to_q0(ref, x):
    tail = jnp.where(rows_of((8, 256)) < 4, ref[x, 64:72, :], ref[x, 80:88, :])
    return ref[x, 0:64, :], tail


def fine_before(
    s, c, low, high, below_y, above_y, below, above, sol, res, diag, inv, msg, da, db, rows
):
    lane = lanes_of((R0, 128))
    for a in range(2):
        left, right = below[a], above[a]
        for x in range(NXE):
            side = jnp.where(lane < W, turn(right, -W * x, 1), 0.0)
            side = jnp.where(lane >= 128 - W, turn(left, 128 - W - W * x, 1), side)
            ref = (res, diag)[a]
            ref[x, 0:64, 0:128] = plane_of((s, c), low, high, a, x)[...]
            ref[x, 64:88, 0:128] = halo_rows(below_y, above_y, a, x)
            ref[x, :, 128:256] = side
    lane40 = lanes_of((R1, 128))

    def fold(ref, i, at):
        both = ref[XH + 2 * i] + ref[XH + 2 * i + 1]
        sides = []
        for side in range(2):
            part = both[:, 128 * side : 128 * side + 128]
            rows[at, side, 0:72, :] = part[0:72]
            rows[at, side, 72:80, :] = part[80:88]
            sides.append(rows.at[at, side][pl.ds(0, R1, stride=2), :] + rows.at[at, side][pl.ds(1, R1, stride=2), :])
        return 0.125 * jnp.where(lane40 < 64, pairs_of_lanes(sides[0]), pairs_of_lanes(sides[1]))

    coef1 = [fold(diag, i, i) for i in range(4)]

    gx = lax.axis_index("gx")
    in_yz = inside_yz((R0, 256), 64, 76, 128, 192)
    low_x, high_x = gx > 0, gx < lax.axis_size("gx") - 1

    def start(x, carry):
        g = diag[x] + 6.0
        diag[x] = g
        here = ((x >= XH) | low_x) & ((x < XH + NX0) | high_x)
        inverse = jnp.where(in_yz & here, 1.0 / g, 0.0)
        inv[x] = inverse
        da[x] = res[x] * inverse * (1.0 / THETA)
        return carry

    lax.fori_loop(0, NXE, start, 0, unroll=True)

    pairs = coefficients(SWEEPS)
    buffers = (da, db)
    for k in range(SWEEPS):
        src, dst = buffers[k % 2], buffers[(k + 1) % 2]
        last = k == SWEEPS - 1

        def nothing(x, d):
            return None

        fine_sweep(src, dst, res, diag, inv, k + 1, NXE - 1 - k, None if last else pairs[k], nothing)

        def gather(x, carry):
            own = src[XH + x, 0:64, 0:128]
            sol[x] = own if k == 0 else sol[x] + own
            return carry

        lax.fori_loop(0, NX0, gather, 0, unroll=True)

    halo = jnp.zeros((R1, 128), F32)
    for i in range(4):
        r1, c1 = fold(res, i, 4 + i), coef1[i]
        both = jnp.where(lane40 < 64, r1, turn(c1, 64, 1))
        msg[i * R1 : i * R1 + R1, :] = both
        for a, v in ((0, r1), (1, c1)):
            base = (a * 4 + i) * 8
            halo = jnp.where((lane40 >= base) & (lane40 < base + 4), turn(v, base - 64, 1), halo)
            halo = jnp.where((lane40 >= base + 4) & (lane40 < base + 8), turn(v, base + 4 - 124, 1), halo)
    msg[160:200, :] = halo


def line_sweep(src, dst, res, diag, inverse, planes, scale, pair, sol, ahead=0):
    def body(x, carry):
        d = src[x + 1]
        near = beside(d) + (src[x] + src[x + 2])
        r = res[x] - (diag[x] * d - scale * near)
        res[x] = r
        if pair is not None:
            step = pair[0] * d + (pair[1] * inverse[x]) * r
            dst[x + 1] = step
            sol[x + ahead] += step
        return carry

    lax.fori_loop(0, planes, body, 0, unroll=True)


def middle_before(own, low, high, far, res, sol, coef, low_res, low_coef, up, down, diag, inv, da, db, rows):
    gx = lax.axis_index("gx")
    size = lax.axis_size("gx")
    lane40 = lanes_of((R1, 128))
    for msg, shift in ((own, 0), (low, 3), (high, 1), (far, 2)):
        place = lax.rem(gx + shift, size) * 4
        side = msg[160:200, :]
        for i in range(4):
            both = msg[i * R1 : i * R1 + R1, :]
            for a, ref in ((0, res), (1, coef)):
                base = (a * 4 + i) * 8
                v = both if a == 0 else turn(both, 64, 1)
                v = jnp.where(lane40 < 64, v, turn(side, 64 - base, 1))
                v = jnp.where(lane40 < 68, v, 0.0)
                v = jnp.where(lane40 < 124, v, turn(side, 124 - base - 4, 1))
                ref[place + i] = v
    in_yz = inside_yz((R1, 128), 32, 36, 64, 96)
    empty = jnp.zeros((R1, 128), F32)
    for buffer in (da, db):
        buffer[0] = empty
        buffer[17] = empty

    def start(x, carry):
        g = coef[x] + 1.5
        diag[x] = g
        inverse = jnp.where(in_yz, 1.0 / g, 0.0)
        inv[x] = inverse
        d = res[x] * inverse * (1.0 / THETA)
        da[x + 1] = d
        sol[x] = d
        return carry

    lax.fori_loop(0, 16, start, 0, unroll=True)
    pairs = coefficients(SWEEPS)
    buffers = (da, db)
    for k in range(SWEEPS):
        src, dst = buffers[k % 2], buffers[(k + 1) % 2]
        line_sweep(src, dst, res, diag, inv, 16, 0.25, pairs[k] if k < SWEEPS - 1 else None, sol)
    lane8, row8 = lanes_of((8, 128)), rows_of((8, 128))

    def fold(ref, i, at):
        rows[at] = ref[2 * i, 0:32, :] + ref[2 * i + 1, 0:32, :]
        part = rows.at[at]
        return 0.125 * pairs_of_lanes(part[pl.ds(0, 16, stride=2), :] + part[pl.ds(1, 16, stride=2), :])

    lows = []
    for i in range(8):
        r2, c2 = fold(res, i, i), fold(coef, i, 8 + i)
        low_res[i] = r2
        low_coef[i] = c2
        lows.append(jnp.where(lanes_of((16, 128)) < 32, r2, turn(c2, 32, 1)))
    for i in range(4):
        both = jnp.where(lanes_of((16, 128)) < 64, lows[i], turn(lows[i + 4], 64, 1))
        up[i * 8 : i * 8 + 8, :] = both[8:16]
        down[i * 8 : i * 8 + 8, :] = both[0:8]
    for i in range(8):
        at = 32 + i * 8
        tiles = []
        for first in (24, 0):
            a, b = [
                jnp.where(lane8 < 64, res[x, first : first + 8, :], turn(sol[x, first : first + 8, :], 64, 1))
                for x in (2 * i, 2 * i + 1)
            ]
            tiles.append((a, b))
        up[at : at + 8, :] = jnp.where(row8 < 4, turn(tiles[0][0], 4, 0), tiles[0][1])
        down[at : at + 8, :] = jnp.where(row8 < 4, tiles[1][0], turn(tiles[1][1], 4, 0))


def low_halo(msg, i, which):
    tile = msg[(i % 4) * 8 : (i % 4) * 8 + 8, :]
    return turn(tile, -(64 * (i // 4) + 32 * which), 1)


def middle_halo(msg, x, which, below):
    tile = msg[32 + (x // 2) * 8 : 40 + (x // 2) * 8, :]
    tile = turn(tile, 64, 1) if which else tile
    return turn(tile, 4, 0) if (x % 2 == 0) == below else tile


def pack_lanes(up, down, row, count, planes, width, base, top):
    lane = lanes_of((count, 128))
    ups, downs = up[row : row + count, :], down[row : row + count, :]
    for i, v in enumerate(planes):
        at = base + width * i
        here = (lane >= at) & (lane < at + width)
        ups = jnp.where(here, turn(v, at - (top - width), 1), ups)
        downs = jnp.where(here, turn(v, at, 1), downs)
    up[row : row + count, :] = ups
    down[row : row + count, :] = downs


def pack_low_own(low_res, low_coef, res, sol, up, down):
    up[...] = jnp.zeros((48, 128), F32)
    down[...] = jnp.zeros((48, 128), F32)
    pack_lanes(up, down, 0, 16, [low_res[i] for i in range(8)], 8, 0, 32)
    pack_lanes(up, down, 0, 16, [low_coef[i] for i in range(8)], 8, 64, 32)
    pack_lanes(up, down, 16, 32, [res[x, 0:32, :] for x in range(16)], 4, 0, 64)
    pack_lanes(up, down, 16, 32, [sol[x, 0:32, :] for x in range(16)], 2, 64, 64)


def keep_fine(after, res0, diag0, inv0, res_q, diag_q, inv_q, r0_up, r0_down):
    for ref, kept, skip in ((res0, res_q, XH), (diag0, diag_q, 0), (inv0, inv_q, 0)):
        for x in range(kept.shape[0]):
            top, tail = to_q0(ref, x + skip)
            kept[x, 0:64, :] = top
            kept[x, 64:72, :] = tail
    lane = lanes_of((Q0, 128))
    for msg, first in ((r0_up, NX0 - XH), (r0_down, 0)):
        side = jnp.zeros((Q0, 128), F32)
        for i in range(XH):
            msg[i * Q0 : i * Q0 + Q0, :] = res_q[first + i, :, 0:128]
            v = res_q[first + i, :, 128:256]
            base = 6 * i
            side = jnp.where((lane >= base) & (lane < base + 3), turn(v, base, 1), side)
            side = jnp.where((lane >= base + 3) & (lane < base + 6), turn(v, base + 3 - 125, 1), side)
        msg[XH * Q0 : XH * Q0 + Q0, :] = side


def pack_low_halo(own_up, own_down, below, above, up, down):
    for msg, own in ((up, own_up), (down, own_down)):
        msg[0:16, :] = own[0:16, :]
        msg[16:32, :] = jnp.zeros((16, 128), F32)
        msg[32:64, :] = own[16:48, :]
        msg[64:80, :] = jnp.zeros((16, 128), F32)
    for at, src, is_below in ((0, above, False), (8, below, True)):
        pack_lanes(up, down, 16 + at, 8, [low_halo(src, i, 0) for i in range(8)], 8, 0, 32)
        pack_lanes(up, down, 16 + at, 8, [low_halo(src, i, 1) for i in range(8)], 8, 64, 32)
        pack_lanes(up, down, 64 + at, 8, [middle_halo(src, x, 0, is_below) for x in range(16)], 4, 0, 64)
        pack_lanes(up, down, 64 + at, 8, [middle_halo(src, x, 1, is_below) for x in range(16)], 2, 64, 64)


def with_sides(own, left, right, base, width, own_lanes):
    lane = lanes_of(own.shape)
    v = jnp.where(lane < own_lanes, own, turn(right, own_lanes - base, 1))
    v = jnp.where(lane < own_lanes + width, v, 0.0)
    return jnp.where(lane < 128 - width, v, turn(left, 128 - width - base, 1))


def bottom(low_res, low_coef, below, above, left, right, sol2, res2, diag2, inv2, da2, db2):
    in_yz = inside_yz((R2, 128), 16, 24, 32, 64)
    empty = jnp.zeros((R2, 128), F32)
    for buffer in (da2, db2):
        buffer[0] = empty
        buffer[9] = empty
    from_left, from_right = left[0:R2, :], right[0:R2, :]
    for i in range(8):
        parts = []
        for a, ref in ((0, low_res), (1, low_coef)):
            own = jnp.concatenate([ref[i], low_halo(above, i, a), low_halo(below, i, a)], 0)
            parts.append(with_sides(own, from_left, from_right, a * 64 + i * 8, 8, 32))
        g = parts[1] + 0.375
        inverse = jnp.where(in_yz, 1.0 / g, 0.0)
        res2[i] = parts[0]
        diag2[i] = g
        inv2[i] = inverse
        d = parts[0] * inverse * (1.0 / THETA)
        da2[i + 1] = d
        sol2[i] = d
    pairs = coefficients(COARSE_SWEEPS)
    buffers = (da2, db2)
    for k in range(COARSE_SWEEPS - 1):
        src, dst = buffers[k % 2], buffers[(k + 1) % 2]
        line_sweep(src, dst, res2, diag2, inv2, 8, 0.0625, pairs[k], sol2)


def middle_after(
    sol2, res, sol, coef1, below, above, left, right, sol1, res1, diag1, inv1, da1, db1
):
    in_yz1 = inside_yz((Q1, 128), 32, 40, 64, 96)
    empty = jnp.zeros((Q1, 128), F32)
    for buffer in (da1, db1):
        buffer[0] = empty
        buffer[17] = empty
    for x in (0, 1, 18, 19):
        sol1[x] = empty
    from_left, from_right = left[R2 : R2 + Q1, :], right[R2 : R2 + Q1, :]
    lane = lanes_of((24, 128))
    half = lane // 2 + jnp.where(lane >= 96, 64, 0)
    first = rows_of((8, 128)) < 4
    for i in range(8):
        tail = jnp.where(first, sol2[i, 16:24, :], sol2[i, 24:32, :])
        lifted = pick(jnp.concatenate([sol2[i, 0:16, :], tail], 0), half)
        for x in (2 * i, 2 * i + 1):
            db1.at[x + 1][pl.ds(0, 24, stride=2), :] = lifted
            db1.at[x + 1][pl.ds(1, 24, stride=2), :] = lifted
            parts = []
            for a, ref in ((0, res), (1, sol)):
                own = jnp.concatenate(
                    [ref[x, 0:32, :], middle_halo(above, x, a, False), middle_halo(below, x, a, True)], 0
                )
                width = (4, 2)[a]
                parts.append(with_sides(own, from_left, from_right, a * 64 + width * x, width, 64))
            res1[x] = parts[0]
            sol1[x + 2] = jnp.where(in_yz1, parts[1], 0.0)

    def correct1(x, carry):
        g = jnp.concatenate([coef1[x], coef1[x, 32:40, :]], 0) + 1.5
        inverse = jnp.where(in_yz1, 1.0 / g, 0.0)
        diag1[x] = g
        inv1[x] = inverse
        p = db1[x + 1]
        near = beside(p) + (db1[x] + db1[x + 2])
        r = res1[x] - (g * p - 0.25 * near)
        res1[x] = r
        d = r * inverse * (1.0 / THETA)
        da1[x + 1] = d
        sol1[x + 2] += p + d
        return carry

    lax.fori_loop(0, 16, correct1, 0, unroll=True)
    pairs = coefficients(SWEEPS)
    buffers = (da1, db1)
    for k in range(SWEEPS - 1):
        src, dst = buffers[k % 2], buffers[(k + 1) % 2]
        line_sweep(src, dst, res1, diag1, inv1, 16, 0.25, pairs[k], sol1, 2)


def fine_after(
    sol1, sol0, res_q, diag_q, inv_q, low, high, out_sol, out_res, p0, res0, da0, db0
):
    gx = lax.axis_index("gx")
    half = lanes_of((R1, 128)) // 2
    first2 = rows_of((8, 128)) < 2
    for i in range(8):
        v = sol1[gx * 4 + i]
        v = jnp.concatenate([v[0:32], jnp.where(first2, v[32:40], turn(v[40:48], 4, 0))], 0)
        for side in range(2):
            lifted = pick(v, half + 64 * side)
            for x in (2 * i, 2 * i + 1):
                p0.at[x, side][pl.ds(0, R1, stride=2), :] = lifted
                p0.at[x, side][pl.ds(1, R1, stride=2), :] = lifted

    def lift(x):
        return jnp.concatenate([p0[x, 0, 0:Q0, :], p0[x, 1, 0:Q0, :]], 1)

    lane72 = lanes_of((Q0, 128))
    for msg, first in ((low, 0), (high, XH + NX0)):
        side = msg[XH * Q0 : XH * Q0 + Q0, :]
        for i in range(XH):
            base = 6 * i
            v = jnp.where(lane72 < 3, turn(side, -base, 1), 0.0)
            v = jnp.where(lane72 < 125, v, turn(side, 125 - base - 3, 1))
            res0[first + i, :, 0:128] = msg[i * Q0 : i * Q0 + Q0, :]
            res0[first + i, :, 128:256] = v

    def fetch(x, carry):
        res0[x + XH] = res_q[x]
        return carry

    lax.fori_loop(0, NX0, fetch, 0, unroll=True)

    def correct0(x, carry):
        p = lift(x + 1)
        near = beside(p) + (lift(x) + lift(x + 2))
        r = res0[x] - (diag_q[x] * p - near)
        res0[x] = r
        da0[x] = r * inv_q[x] * (1.0 / THETA)
        return carry

    lax.fori_loop(0, NXE, correct0, 0, unroll=True)

    def begin(x, carry):
        out_sol[x] = sol0[x] + p0[x + XH + 1, 0, 0:64, :]
        return carry

    lax.fori_loop(0, NX0, begin, 0, unroll=True)
    pairs = coefficients(SWEEPS)
    buffers = (da0, db0)
    for k in range(SWEEPS):
        src, dst = buffers[k % 2], buffers[(k + 1) % 2]

        def gather0(x, carry):
            out_sol[x] += src[x + XH, 0:64, 0:128]
            return carry

        lax.fori_loop(0, NX0, gather0, 0, unroll=True)
        fine_sweep(
            src, dst, res0, diag_q, inv_q, k + 1, NXE - 1 - k, pairs[k] if k < SWEEPS - 1 else None,
            lambda x, d: None,
        )

    def put(x, carry):
        out_res[x] = res0[x + XH, 0:64, 0:128]
        return carry

    lax.fori_loop(0, NX0, put, 0, unroll=True)


def per_device(s, c):
    up = jnp.concatenate([s[NX0 - XH :], c[NX0 - XH :]], 0)
    down = jnp.concatenate([s[:XH], c[:XH]], 0)
    low, high = ring(up, "gx", 1), ring(down, "gx", -1)
    up, down = call(pack_y, 4, [(256, 128)] * 2, [], s, c, low, high)
    below_y, above_y = ring(up, "gy", 1), ring(down, "gy", -1)
    own_up, own_down = call(pack_z_own, 4, [(2, 64, 128)] * 2, [], s, c, low, high)
    up, down = call(pack_z_halo, 4, [(2, R0, 128)] * 2, [], own_up, own_down, below_y, above_y)
    below, above = ring(up, "gz", 1), ring(down, "gz", -1)
    big = (NXE, R0, 256)
    sol0, res0, diag0, inv0, msg = call(
        fine_before,
        16,
        [(NX0, 64, 128), big, big, big, (200, 128)],
        [big, big, (8, 2, 80, 128)],
        s, c, low, high, below_y, above_y, below, above,
        micros=4.0,
    )
    low, high, far = ring(msg, "gx", 1), ring(msg, "gx", -1), ring(msg, "gx", 2)
    big = (NXE, Q0, 256)
    res_q, diag_q, inv_q, r0_up, r0_down = call(
        keep_fine,
        8,
        [(NX0, Q0, 256), big, big, (4 * Q0, 128), (4 * Q0, 128)],
        [],
        low, res0, diag0, inv0,
        micros=2.0,
    )
    r0_low, r0_high = ring(r0_up, "gx", 1), ring(r0_down, "gx", -1)
    mid = (16, R1, 128)
    res1, sol1, coef1, res2, coef2, up, down = call(
        middle_before,
        8,
        [mid, mid, mid, (8, 16, 128), (8, 16, 128), (96, 128), (96, 128)],
        [mid, mid, (18, R1, 128), (18, R1, 128), (16, 32, 128)],
        msg, low, high, far,
        micros=2.0,
    )
    below, above = ring(up, "gy", 1), ring(down, "gy", -1)
    own_up, own_down = call(pack_low_own, 4, [(48, 128)] * 2, [], res2, coef2, res1, sol1, micros=2.0)
    up, down = call(pack_low_halo, 4, [(R2 + Q1, 128)] * 2, [], own_up, own_down, below, above)
    left, right = ring(up, "gz", 1), ring(down, "gz", -1)
    bot, mid = (8, R2, 128), (16, Q1, 128)
    big = (NXE, Q0, 256)
    own = (NX0, NY0, NZ0)
    (sol2,) = call(
        bottom, 4, [bot], [bot] * 3 + [(10, R2, 128)] * 2, res2, coef2, below, above, left, right
    )
    (sol1,) = call(
        middle_after,
        8,
        [(20, Q1, 128)],
        [mid] * 3 + [(18, Q1, 128)] * 2,
        sol2, res1, sol1, coef1, below, above, left, right,
        micros=2.0,
    )
    return tuple(
        call(
            fine_after,
            16,
            [own, own],
            [(16, 2, 80, 128)] + [big] * 3,
            sol1, sol0, res_q, diag_q, inv_q, r0_low, r0_high,
        )
    )


def solution(mesh):
    return jax.shard_map(
        per_device,
        mesh=mesh,
        in_specs=(P("gx", "gy", "gz"), P("gx", "gy", "gz")),
        out_specs=(P("gx", "gy", "gz"), P("gx", "gy", "gz")),
        check_vma=False,
    )
```

time: 66.2 us -> 63.5 us (0.959)
  the two profiles are of different devices: /device:TPU:71 before, /device:TPU:7 now
where the time goes in v4:
time: 63.5 us; the launch traced here: 63.4 us
  waiting for transfers between devices  25 us (39%)
  starting transfers between devices  23.3 us (37%)
  Pallas kernels  13.2 us (21%)
  local copies, waits for them, and re-layouts  1.13 us (2%)
  between operations  0.78 us (1%)
    ppermute x15, waiting for transfers between devices, ring(): lax.ppermute(value, axis, [(i, (i + shift) % size) for i in range(size)])  25 us
    ppermute x15, starting transfers between devices, ring(): lax.ppermute(value, axis, [(i, (i + shift) % size) for i in range(size)])  23.3 us
    pallas_call x11, Pallas kernels, call(): pl.pallas_call(body, out_shape=[jax.ShapeDtypeStruct(s, F32) for s in out...  13.2 us
  transfers between devices with their start and end apart: 15, of which 11 were waited for; matrix products, arithmetic and copies ran while one was open for 0% of the time, Pallas kernels for 9%

profile of v4, /device:TPU:7, one launch (start us, length us, event | category | flops | bytes accessed | tf_op | source)
XLA Modules:
  0.0 63.4 jit_solution(5890240820828293549)
XLA Ops:
  0.6 1.1 %fusion = (f32[3,64,128]{2,1,0:T(8,128)S(1)}, f32[3,64,128]{2,1,0:T(8,128)S(1)}, f32[3,64,128]{2,1,0:T(8,128)S(1)}, f32[3,64,128]{2,1,0:T(8,128)S(1)}) fusion(f32[8,64,128]{2,1,0:T(8,128)} %s.5, f32[8,64,128]{2,1,0:T(8,128)} %c.5), kind=kLoop, calls=%fused_computation.2 | loop fusion | bytes 786432 | tf_op jit(solution)/shard_map/slice | solution.py:540
  1.8 2.8 %collective-permute-start.1 = (f32[6,64,128]{2,1,0:T(8,128)S(1)}, f32[6,64,128]{2,1,0:T(8,128)S(1)}, u32[]{:S(2)}, u32[]{:S(2)}) collective-permute-start(f32[6,64,128]{2,1,0:T(8,128)S(1)} %pad_maximum_fusion.1), channel_id=1, source_target_pairs={{0,192},{64,0},{128,64},{192,128},{1,193},{65,1},{129,65},{193,129... | collective-permute-start | bytes 589832 | tf_op jit(solution)/shard_map/ppermute | solution.py:88
  4.7 3.5 %collective-permute-done.1.high = f32[6,64,128]{2,1,0:T(8,128)S(1)} collective-permute-done((f32[6,64,128]{2,1,0:T(8,128)S(1)}, f32[6,64,128]{2,1,0:T(8,128)S(1)}, u32[]{:S(2)}, u32[]{:S(2)}) %collective-permute-start.1) | collective-permute-done | bytes 196640 | tf_op jit(solution)/shard_map/ppermute | solution.py:88
  8.2 3.2 %collective-permute-done.low = f32[6,64,128]{2,1,0:T(8,128)S(1)} collective-permute-done((f32[6,64,128]{2,1,0:T(8,128)S(1)}, f32[6,64,128]{2,1,0:T(8,128)S(1)}, u32[]{:S(2)}, u32[]{:S(2)}) %collective-permute-start) | collective-permute-done | bytes 196640 | tf_op jit(solution)/shard_map/ppermute | solution.py:88
  11.4 1.7 %collective-permute-start.2 = (f32[256,128]{1,0:T(8,128)S(1)}, f32[256,128]{1,0:T(8,128)S(1)}, u32[]{:S(2)}, u32[]{:S(2)}) collective-permute-start(f32[256,128]{1,0:T(8,128)S(1)} %get-tuple-element.29), channel_id=1, source_target_pairs={{0,8},{8,16},{16,24},{24,32},{32,40},{40,48},{48,56},{56,0},{1,9},... | collective-permute-start | bytes 393224 | tf_op jit(solution)/shard_map/ppermute | solution.py:88
  13.1 4.0 %collective-permute-start.3 = (f32[256,128]{1,0:T(8,128)S(1)}, f32[256,128]{1,0:T(8,128)S(1)}, u32[]{:S(2)}, u32[]{:S(2)}) collective-permute-start(f32[256,128]{1,0:T(8,128)S(1)} %get-tuple-element.30), channel_id=1, source_target_pairs={{0,56},{8,0},{16,8},{24,16},{32,24},{40,32},{48,40},{56,48},{1,57}... | collective-permute-start | bytes 393224 | tf_op jit(solution)/shard_map/ppermute | solution.py:88
  17.7 1.7 %collective-permute-done.2.below.below_y = f32[256,128]{1,0:T(8,128)S(1)} collective-permute-done((f32[256,128]{1,0:T(8,128)S(1)}, f32[256,128]{1,0:T(8,128)S(1)}, u32[]{:S(2)}, u32[]{:S(2)}) %collective-permute-start.2) | collective-permute-done | bytes 131104 | tf_op jit(solution)/shard_map/ppermute | solution.py:88
  19.7 2.8 %collective-permute-start.4 = (f32[2,88,128]{2,1,0:T(8,128)S(1)}, f32[2,88,128]{2,1,0:T(8,128)S(1)}, u32[]{:S(2)}, u32[]{:S(2)}) collective-permute-start(f32[2,88,128]{2,1,0:T(8,128)S(1)} %get-tuple-element.33), channel_id=1, source_target_pairs={{0,1},{1,2},{2,3},{3,4},{4,5},{5,6},{6,7},{7,0},{8,9},{9,10},{10,1... | collective-permute-start | bytes 270344 | tf_op jit(solution)/shard_map/ppermute | solution.py:88
  22.5 1.6 %collective-permute-done.4.below = f32[2,88,128]{2,1,0:T(8,128)S(1)} collective-permute-done((f32[2,88,128]{2,1,0:T(8,128)S(1)}, f32[2,88,128]{2,1,0:T(8,128)S(1)}, u32[]{:S(2)}, u32[]{:S(2)}) %collective-permute-start.4) | collective-permute-done | bytes 90144 | tf_op jit(solution)/shard_map/ppermute | solution.py:88
  24.1 3.6 %collective-permute-done.5.above = f32[2,88,128]{2,1,0:T(8,128)S(1)} collective-permute-done((f32[2,88,128]{2,1,0:T(8,128)S(1)}, f32[2,88,128]{2,1,0:T(8,128)S(1)}, u32[]{:S(2)}, u32[]{:S(2)}) %collective-permute-start.5) | collective-permute-done | bytes 90144 | tf_op jit(solution)/shard_map/ppermute | solution.py:88
  27.7 3.9 %shard_map.44 = (f32[8,64,128]{2,1,0:T(8,128)S(1)}, f32[14,88,256]{2,1,0:T(8,128)S(1)}, f32[14,88,256]{2,1,0:T(8,128)S(1)}, f32[14,88,256]{2,1,0:T(8,128)S(1)}, f32[200,128]{1,0:T(8,128)S(1)}) custom-call(f32[8,64,128]{2,1,0:T(8,128)S(1)} %copy-done, f32[8,64,128]{2,1,0:T(8,128)S(1)} %copy-done.1, f32[6,64,128]{2,1,0:T(8,128)S(1)} %collective-permute-done.low, ...), custom_call_target="tpu_custom_call" | custom-call | bytes 14760000 | tf_op jit(solution)/shard_map/pallas_call | solution.py:75
  31.7 2.7 %collective-permute-start.7 = (f32[200,128]{1,0:T(8,128)S(1)}, f32[200,128]{1,0:T(8,128)S(1)}, u32[]{:S(2)}, u32[]{:S(2)}) collective-permute-start(f32[200,128]{1,0:T(8,128)S(1)} %get-tuple-element.35.own), channel_id=1, source_target_pairs={{0,192},{64,0},{128,64},{192,128},{1,193},{65,1},{129,65},{193,129... | collective-permute-start | bytes 307208 | tf_op jit(solution)/shard_map/ppermute | solution.py:88
  34.3 2.3 %collective-permute-done.6.low.after = f32[200,128]{1,0:T(8,128)S(1)} collective-permute-done((f32[200,128]{1,0:T(8,128)S(1)}, f32[200,128]{1,0:T(8,128)S(1)}, u32[]{:S(2)}, u32[]{:S(2)}) %collective-permute-start.6) | collective-permute-done | bytes 102432 | tf_op jit(solution)/shard_map/ppermute | solution.py:88
  37.0 2.7 %collective-permute-start.14 = (f32[288,128]{1,0:T(8,128)S(1)}, f32[288,128]{1,0:T(8,128)S(1)}, u32[]{:S(2)}, u32[]{:S(2)}) collective-permute-start(f32[288,128]{1,0:T(8,128)S(1)} %get-tuple-element.55), channel_id=1, source_target_pairs={{0,192},{64,0},{128,64},{192,128},{1,193},{65,1},{129,65},{193,129... | collective-permute-start | bytes 442376 | tf_op jit(solution)/shard_map/ppermute | solution.py:88
  39.7 0.7 %collective-permute-done.8.far = f32[200,128]{1,0:T(8,128)S(1)} collective-permute-done((f32[200,128]{1,0:T(8,128)S(1)}, f32[200,128]{1,0:T(8,128)S(1)}, u32[]{:S(2)}, u32[]{:S(2)}) %collective-permute-start.8) | collective-permute-done | bytes 102432 | tf_op jit(solution)/shard_map/ppermute | solution.py:88
  40.4 2.0 %shard_map.45 = (f32[16,40,128]{2,1,0:T(8,128)S(1)}, f32[16,40,128]{2,1,0:T(8,128)S(1)}, f32[16,40,128]{2,1,0:T(8,128)S(1)}, f32[8,16,128]{2,1,0:T(8,128)S(1)}, ...) custom-call(f32[200,128]{1,0:T(8,128)S(1)} %get-tuple-element.35.own, ...), custom_call_target="tpu_custom_call" | custom-call | bytes 7380000 | tf_op jit(solution)/shard_map/pallas_call | solution.py:75
  42.4 3.1 %collective-permute-start.10 = (f32[96,128]{1,0:T(8,128)S(1)}, f32[96,128]{1,0:T(8,128)S(1)}, u32[]{:S(2)}, u32[]{:S(2)}) collective-permute-start(f32[96,128]{1,0:T(8,128)S(1)} %get-tuple-element.39), channel_id=1, source_target_pairs={{0,56},{8,0},{16,8},{24,16},{32,24},{40,32},{48,40},{56,48},{1,57}... | collective-permute-start | bytes 147464 | tf_op jit(solution)/shard_map/ppermute | solution.py:88
  45.9 0.8 %collective-permute-done.10.above = f32[96,128]{1,0:T(8,128)S(1)} collective-permute-done((f32[96,128]{1,0:T(8,128)S(1)}, f32[96,128]{1,0:T(8,128)S(1)}, u32[]{:S(2)}, u32[]{:S(2)}) %collective-permute-start.10) | collective-permute-done | bytes 49184 | tf_op jit(solution)/shard_map/ppermute | solution.py:88
  46.7 3.0 %collective-permute-done.9.below = f32[96,128]{1,0:T(8,128)S(1)} collective-permute-done((f32[96,128]{1,0:T(8,128)S(1)}, f32[96,128]{1,0:T(8,128)S(1)}, u32[]{:S(2)}, u32[]{:S(2)}) %collective-permute-start.9) | collective-permute-done | bytes 49184 | tf_op jit(solution)/shard_map/ppermute | solution.py:88
  50.2 3.2 %collective-permute-start.11 = (f32[80,128]{1,0:T(8,128)S(1)}, f32[80,128]{1,0:T(8,128)S(1)}, u32[]{:S(2)}, u32[]{:S(2)}) collective-permute-start(f32[80,128]{1,0:T(8,128)S(1)} %get-tuple-element.44), channel_id=1, source_target_pairs={{0,1},{1,2},{2,3},{3,4},{4,5},{5,6},{6,7},{7,0},{8,9},{9,10},{10,1... | collective-permute-start | bytes 122888 | tf_op jit(solution)/shard_map/ppermute | solution.py:88
  53.4 1.1 %collective-permute-done.11.left = f32[80,128]{1,0:T(8,128)S(1)} collective-permute-done((f32[80,128]{1,0:T(8,128)S(1)}, f32[80,128]{1,0:T(8,128)S(1)}, u32[]{:S(2)}, u32[]{:S(2)}) %collective-permute-start.11) | collective-permute-done | bytes 40992 | tf_op jit(solution)/shard_map/ppermute | solution.py:88
  54.5 3.5 %collective-permute-done.12.right = f32[80,128]{1,0:T(8,128)S(1)} collective-permute-done((f32[80,128]{1,0:T(8,128)S(1)}, f32[80,128]{1,0:T(8,128)S(1)}, u32[]{:S(2)}, u32[]{:S(2)}) %collective-permute-start.12) | collective-permute-done | bytes 40992 | tf_op jit(solution)/shard_map/ppermute | solution.py:88
  58.7 1.4 %shard_map.49.sol1 = f32[20,48,128]{2,1,0:T(8,128)S(1)} custom-call(f32[8,32,128]{2,1,0:T(8,128)S(1)} %shard_map.48.sol2, f32[16,40,128]{2,1,0:T(8,128)S(1)} %get-tuple-element.40.res, f32[16,40,128]{2,1,0:T(8,128)S(1)} %get-tuple-element.41.sol, f32[16,40,128]{2,1,0:T(8,128)S(1)} %get-tuple-element.46.coef1, f32[96,128]{1,0:T(8,128)S(1)} %collective-permute-done.9.below, ...), custom_call_target="tpu_custom_call" | custom-call | bytes 7380000 | tf_op jit(solution)/shard_map/pallas_call | solution.py:75
  60.1 3.3 %shard_map.51 = (f32[8,64,128]{2,1,0:T(8,128)}, f32[8,64,128]{2,1,0:T(8,128)}) custom-call(f32[20,48,128]{2,1,0:T(8,128)S(1)} %shard_map.49.sol1, f32[8,64,128]{2,1,0:T(8,128)S(1)} %get-tuple-element.47.sol0, f32[8,72,256]{2,1,0:T(8,128)S(1)} %get-tuple-element.51.res_q, f32[14,72,256]{2,1,0:T(8,128)S(1)} %get-tuple-element.52.diag_q, ...), custom_call_target="tpu_custom_call" | custom-call | bytes 3690000 | tf_op jit(solution)/shard_map/pallas_call | solution.py:75
  (24 shorter events, 3.0 us)
Async XLA Ops:
  0.6 10.7 %copy-start = (f32[8,64,128]{2,1,0:T(8,128)S(1)}, f32[8,64,128]{2,1,0:T(8,128)}, u32[]{:S(2)}) copy-start(f32[8,64,128]{2,1,0:T(8,128)} %s.5) | copy-start | bytes 786436
  0.6 10.7 %copy-start.1 = (f32[8,64,128]{2,1,0:T(8,128)S(1)}, f32[8,64,128]{2,1,0:T(8,128)}, u32[]{:S(2)}) copy-start(f32[8,64,128]{2,1,0:T(8,128)} %c.5) | copy-start | bytes 786436
  1.8 6.4 %collective-permute-start.1 = (f32[6,64,128]{2,1,0:T(8,128)S(1)}, f32[6,64,128]{2,1,0:T(8,128)S(1)}, u32[]{:S(2)}, u32[]{:S(2)}) collective-permute-start(f32[6,64,128]{2,1,0:T(8,128)S(1)} %pad_maximum_fusion.1), channel_id=1, source_target_pairs={{0,192},{64,0},{128,64},{192,128},{1,193},{65,1},{129,65},{193,129... | collective-permute-start | bytes 589832 | tf_op jit(solution)/shard_map/ppermute | solution.py:88
  4.6 6.7 %collective-permute-start = (f32[6,64,128]{2,1,0:T(8,128)S(1)}, f32[6,64,128]{2,1,0:T(8,128)S(1)}, u32[]{:S(2)}, u32[]{:S(2)}) collective-permute-start(f32[6,64,128]{2,1,0:T(8,128)S(1)} %pad_maximum_fusion), channel_id=1, source_target_pairs={{0,64},{64,128},{128,192},{192,0},{1,65},{65,129},{129,193},{193,1... | collective-permute-start | bytes 589832 | tf_op jit(solution)/shard_map/ppermute | solution.py:88
  11.4 8.0 %collective-permute-start.2 = (f32[256,128]{1,0:T(8,128)S(1)}, f32[256,128]{1,0:T(8,128)S(1)}, u32[]{:S(2)}, u32[]{:S(2)}) collective-permute-start(f32[256,128]{1,0:T(8,128)S(1)} %get-tuple-element.29), channel_id=1, source_target_pairs={{0,8},{8,16},{16,24},{24,32},{32,40},{40,48},{48,56},{56,0},{1,9},... | collective-permute-start | bytes 393224 | tf_op jit(solution)/shard_map/ppermute | solution.py:88
  13.1 6.3 %collective-permute-start.3 = (f32[256,128]{1,0:T(8,128)S(1)}, f32[256,128]{1,0:T(8,128)S(1)}, u32[]{:S(2)}, u32[]{:S(2)}) collective-permute-start(f32[256,128]{1,0:T(8,128)S(1)} %get-tuple-element.30), channel_id=1, source_target_pairs={{0,56},{8,0},{16,8},{24,16},{32,24},{40,32},{48,40},{56,48},{1,57}... | collective-permute-start | bytes 393224 | tf_op jit(solution)/shard_map/ppermute | solution.py:88
  19.7 4.4 %collective-permute-start.4 = (f32[2,88,128]{2,1,0:T(8,128)S(1)}, f32[2,88,128]{2,1,0:T(8,128)S(1)}, u32[]{:S(2)}, u32[]{:S(2)}) collective-permute-start(f32[2,88,128]{2,1,0:T(8,128)S(1)} %get-tuple-element.33), channel_id=1, source_target_pairs={{0,1},{1,2},{2,3},{3,4},{4,5},{5,6},{6,7},{7,0},{8,9},{9,10},{10,1... | collective-permute-start | bytes 270344 | tf_op jit(solution)/shard_map/ppermute | solution.py:88
  22.5 5.2 %collective-permute-start.5 = (f32[2,88,128]{2,1,0:T(8,128)S(1)}, f32[2,88,128]{2,1,0:T(8,128)S(1)}, u32[]{:S(2)}, u32[]{:S(2)}) collective-permute-start(f32[2,88,128]{2,1,0:T(8,128)S(1)} %get-tuple-element.34), channel_id=1, source_target_pairs={{0,7},{1,0},{2,1},{3,2},{4,3},{5,4},{6,5},{7,6},{8,15},{9,8},{10,9... | collective-permute-start | bytes 270344 | tf_op jit(solution)/shard_map/ppermute | solution.py:88
  31.6 5.1 %collective-permute-start.6 = (f32[200,128]{1,0:T(8,128)S(1)}, f32[200,128]{1,0:T(8,128)S(1)}, u32[]{:S(2)}, u32[]{:S(2)}) collective-permute-start(f32[200,128]{1,0:T(8,128)S(1)} %get-tuple-element.35.own), channel_id=1, source_target_pairs={{0,64},{64,128},{128,192},{192,0},{1,65},{65,129},{129,193},{193,1... | collective-permute-start | bytes 307208 | tf_op jit(solution)/shard_map/ppermute | solution.py:88
  31.7 8.0 %collective-permute-start.7 = (f32[200,128]{1,0:T(8,128)S(1)}, f32[200,128]{1,0:T(8,128)S(1)}, u32[]{:S(2)}, u32[]{:S(2)}) collective-permute-start(f32[200,128]{1,0:T(8,128)S(1)} %get-tuple-element.35.own), channel_id=1, source_target_pairs={{0,192},{64,0},{128,64},{192,128},{1,193},{65,1},{129,65},{193,129... | collective-permute-start | bytes 307208 | tf_op jit(solution)/shard_map/ppermute | solution.py:88
  34.3 6.1 %collective-permute-start.8 = (f32[200,128]{1,0:T(8,128)S(1)}, f32[200,128]{1,0:T(8,128)S(1)}, u32[]{:S(2)}, u32[]{:S(2)}) collective-permute-start(f32[200,128]{1,0:T(8,128)S(1)} %get-tuple-element.35.own), channel_id=1, source_target_pairs={{0,128},{64,192},{128,0},{192,64},{1,129},{65,193},{129,1},{193,65... | collective-permute-start | bytes 307208 | tf_op jit(solution)/shard_map/ppermute | solution.py:88
  37.0 23.2 %collective-permute-start.13 = (f32[288,128]{1,0:T(8,128)S(1)}, f32[288,128]{1,0:T(8,128)S(1)}, u32[]{:S(2)}, u32[]{:S(2)}) collective-permute-start(f32[288,128]{1,0:T(8,128)S(1)} %get-tuple-element.54), channel_id=1, source_target_pairs={{0,64},{64,128},{128,192},{192,0},{1,65},{65,129},{129,193},{193,1... | collective-permute-start | bytes 442376 | tf_op jit(solution)/shard_map/ppermute | solution.py:88
  37.0 23.1 %collective-permute-start.14 = (f32[288,128]{1,0:T(8,128)S(1)}, f32[288,128]{1,0:T(8,128)S(1)}, u32[]{:S(2)}, u32[]{:S(2)}) collective-permute-start(f32[288,128]{1,0:T(8,128)S(1)} %get-tuple-element.55), channel_id=1, source_target_pairs={{0,192},{64,0},{128,64},{192,128},{1,193},{65,1},{129,65},{193,129... | collective-permute-start | bytes 442376 | tf_op jit(solution)/shard_map/ppermute | solution.py:88
  42.4 4.3 %collective-permute-start.10 = (f32[96,128]{1,0:T(8,128)S(1)}, f32[96,128]{1,0:T(8,128)S(1)}, u32[]{:S(2)}, u32[]{:S(2)}) collective-permute-start(f32[96,128]{1,0:T(8,128)S(1)} %get-tuple-element.39), channel_id=1, source_target_pairs={{0,56},{8,0},{16,8},{24,16},{32,24},{40,32},{48,40},{56,48},{1,57}... | collective-permute-start | bytes 147464 | tf_op jit(solution)/shard_map/ppermute | solution.py:88
  45.5 4.2 %collective-permute-start.9 = (f32[96,128]{1,0:T(8,128)S(1)}, f32[96,128]{1,0:T(8,128)S(1)}, u32[]{:S(2)}, u32[]{:S(2)}) collective-permute-start(f32[96,128]{1,0:T(8,128)S(1)} %get-tuple-element.38), channel_id=1, source_target_pairs={{0,8},{8,16},{16,24},{24,32},{32,40},{40,48},{48,56},{56,0},{1,9},... | collective-permute-start | bytes 147464 | tf_op jit(solution)/shard_map/ppermute | solution.py:88
  50.2 4.3 %collective-permute-start.11 = (f32[80,128]{1,0:T(8,128)S(1)}, f32[80,128]{1,0:T(8,128)S(1)}, u32[]{:S(2)}, u32[]{:S(2)}) collective-permute-start(f32[80,128]{1,0:T(8,128)S(1)} %get-tuple-element.44), channel_id=1, source_target_pairs={{0,1},{1,2},{2,3},{3,4},{4,5},{5,6},{6,7},{7,0},{8,9},{9,10},{10,1... | collective-permute-start | bytes 122888 | tf_op jit(solution)/shard_map/ppermute | solution.py:88
  53.4 4.6 %collective-permute-start.12 = (f32[80,128]{1,0:T(8,128)S(1)}, f32[80,128]{1,0:T(8,128)S(1)}, u32[]{:S(2)}, u32[]{:S(2)}) collective-permute-start(f32[80,128]{1,0:T(8,128)S(1)} %get-tuple-element.45), channel_id=1, source_target_pairs={{0,7},{1,0},{2,1},{3,2},{4,3},{5,4},{6,5},{7,6},{8,15},{9,8},{10,9... | collective-permute-start | bytes 122888 | tf_op jit(solution)/shard_map/ppermute | solution.py:88

commit v5 on v4

--- a/solution.py
+++ b/solution.py
@@ -96,7 +96,7 @@
     return high.at[which * XH + x - XH - NX0]
 
 
-def pack_y(s, c, low, high, up, down):
+def pack_y(s, c, high, low, up, down):
     for a in range(2):
         for x in range(NXE):
             src = plane_of((s, c), low, high, a, x)
@@ -131,7 +131,7 @@
     return jnp.concatenate([above[at * 8 : at * 8 + 8, :], middle, below[at * 8 : at * 8 + 8, :]], 0)
 
 
-def pack_z_own(s, c, low, high, up, down):
+def pack_z_own(s, c, high, low, up, down):
     pack_wide(up, down, 0, 64, lambda a, x: plane_of((s, c), low, high, a, x)[...])
 
 
@@ -161,7 +161,7 @@
 
 
 def fine_before(
-    s, c, low, high, below_y, above_y, below, above, sol, res, diag, inv, msg, da, db, rows
+    s, c, high, low, below_y, above_y, below, above, sol, res, diag, inv, msg, da, db, rows
 ):
     lane = lanes_of((R0, 128))
     for a in range(2):
@@ -365,7 +365,7 @@
         msg[XH * Q0 : XH * Q0 + Q0, :] = side
 
 
-def pack_low_halo(own_up, own_down, below, above, up, down):
+def pack_low_halo(own_up, own_down, above, below, up, down):
     for msg, own in ((up, own_up), (down, own_down)):
         msg[0:16, :] = own[0:16, :]
         msg[16:32, :] = jnp.zeros((16, 128), F32)
@@ -385,7 +385,7 @@
     return jnp.where(lane < 128 - width, v, turn(left, 128 - width - base, 1))
 
 
-def bottom(low_res, low_coef, below, above, left, right, sol2, res2, diag2, inv2, da2, db2):
+def bottom(low_res, low_coef, above, below, left, right, sol2, res2, diag2, inv2, da2, db2):
     in_yz = inside_yz((R2, 128), 16, 24, 32, 64)
     empty = jnp.zeros((R2, 128), F32)
     for buffer in (da2, db2):
@@ -413,7 +413,7 @@
 
 
 def middle_after(
-    sol2, res, sol, coef1, below, above, left, right, sol1, res1, diag1, inv1, da1, db1
+    sol2, res, sol, coef1, above, below, left, right, sol1, res1, diag1, inv1, da1, db1
 ):
     in_yz1 = inside_yz((Q1, 128), 32, 40, 64, 96)
     empty = jnp.zeros((Q1, 128), F32)
@@ -539,9 +539,9 @@
     up = jnp.concatenate([s[NX0 - XH :], c[NX0 - XH :]], 0)
     down = jnp.concatenate([s[:XH], c[:XH]], 0)
     low, high = ring(up, "gx", 1), ring(down, "gx", -1)
-    up, down = call(pack_y, 4, [(256, 128)] * 2, [], s, c, low, high)
+    up, down = call(pack_y, 4, [(256, 128)] * 2, [], s, c, high, low)
     below_y, above_y = ring(up, "gy", 1), ring(down, "gy", -1)
-    own_up, own_down = call(pack_z_own, 4, [(2, 64, 128)] * 2, [], s, c, low, high)
+    own_up, own_down = call(pack_z_own, 4, [(2, 64, 128)] * 2, [], s, c, high, low)
     up, down = call(pack_z_halo, 4, [(2, R0, 128)] * 2, [], own_up, own_down, below_y, above_y)
     below, above = ring(up, "gz", 1), ring(down, "gz", -1)
     big = (NXE, R0, 256)
@@ -550,7 +550,7 @@
         16,
         [(NX0, 64, 128), big, big, big, (200, 128)],
         [big, big, (8, 2, 80, 128)],
-        s, c, low, high, below_y, above_y, below, above,
+        s, c, high, low, below_y, above_y, below, above,
         micros=4.0,
     )
     low, high, far = ring(msg, "gx", 1), ring(msg, "gx", -1), ring(msg, "gx", 2)
@@ -575,20 +575,20 @@
     )
     below, above = ring(up, "gy", 1), ring(down, "gy", -1)
     own_up, own_down = call(pack_low_own, 4, [(48, 128)] * 2, [], res2, coef2, res1, sol1, micros=2.0)
-    up, down = call(pack_low_halo, 4, [(R2 + Q1, 128)] * 2, [], own_up, own_down, below, above)
+    up, down = call(pack_low_halo, 4, [(R2 + Q1, 128)] * 2, [], own_up, own_down, above, below)
     left, right = ring(up, "gz", 1), ring(down, "gz", -1)
     bot, mid = (8, R2, 128), (16, Q1, 128)
     big = (NXE, Q0, 256)
     own = (NX0, NY0, NZ0)
     (sol2,) = call(
-        bottom, 4, [bot], [bot] * 3 + [(10, R2, 128)] * 2, res2, coef2, below, above, left, right
+        bottom, 4, [bot], [bot] * 3 + [(10, R2, 128)] * 2, res2, coef2, above, below, left, right
     )
     (sol1,) = call(
         middle_after,
         8,
         [(20, Q1, 128)],
         [mid] * 3 + [(18, Q1, 128)] * 2,
-        sol2, res1, sol1, coef1, below, above, left, right,
+        sol2, res1, sol1, coef1, above, below, left, right,
         micros=2.0,
     )
     return tuple(

time: 63.5 us -> 58.2 us (0.917)
  the two profiles are of different devices: /device:TPU:7 before, /device:TPU:71 now
where the time goes in v5:
time: 58.2 us; the launch traced here: 58.1 us
  waiting for transfers between devices  22.7 us (39%)
  starting transfers between devices  20.3 us (35%)
  Pallas kernels  13.2 us (23%)
  local copies, waits for them, and re-layouts  1.13 us (2%)
  between operations  0.76 us (1%)
    ppermute x15, waiting for transfers between devices, ring(): lax.ppermute(value, axis, [(i, (i + shift) % size) for i in range(size)])  22.7 us
    ppermute x15, starting transfers between devices, ring(): lax.ppermute(value, axis, [(i, (i + shift) % size) for i in range(size)])  20.3 us
    pallas_call x11, Pallas kernels, call(): pl.pallas_call(body, out_shape=[jax.ShapeDtypeStruct(s, F32) for s in out...  13.2 us
  transfers between devices with their start and end apart: 15, of which 11 were waited for; matrix products, arithmetic and copies ran while one was open for 0% of the time, Pallas kernels for 10%

profile of v5, /device:TPU:71, one launch (start us, length us, event | category | flops | bytes accessed | tf_op | source)
XLA Modules:
  0.0 58.1 jit_solution(7201905223817579195)
XLA Ops:
  0.6 1.1 %fusion = (f32[3,64,128]{2,1,0:T(8,128)S(1)}, f32[3,64,128]{2,1,0:T(8,128)S(1)}, f32[3,64,128]{2,1,0:T(8,128)S(1)}, f32[3,64,128]{2,1,0:T(8,128)S(1)}) fusion(f32[8,64,128]{2,1,0:T(8,128)} %s.5, f32[8,64,128]{2,1,0:T(8,128)} %c.5), kind=kLoop, calls=%fused_computation.2 | loop fusion | bytes 786432 | tf_op jit(solution)/shard_map/slice | solution.py:539
  1.8 1.4 %collective-permute-start.1 = (f32[6,64,128]{2,1,0:T(8,128)S(1)}, f32[6,64,128]{2,1,0:T(8,128)S(1)}, u32[]{:S(2)}, u32[]{:S(2)}) collective-permute-start(f32[6,64,128]{2,1,0:T(8,128)S(1)} %pad_maximum_fusion.1), channel_id=1, source_target_pairs={{0,64},{64,128},{128,192},{192,0},{1,65},{65,129},{129,193},{193,1... | collective-permute-start | bytes 589832 | tf_op jit(solution)/shard_map/ppermute | solution.py:88
  3.2 1.5 %collective-permute-start = (f32[6,64,128]{2,1,0:T(8,128)S(1)}, f32[6,64,128]{2,1,0:T(8,128)S(1)}, u32[]{:S(2)}, u32[]{:S(2)}) collective-permute-start(f32[6,64,128]{2,1,0:T(8,128)S(1)} %pad_maximum_fusion), channel_id=1, source_target_pairs={{0,192},{64,0},{128,64},{192,128},{1,193},{65,1},{129,65},{193,129... | collective-permute-start | bytes 589832 | tf_op jit(solution)/shard_map/ppermute | solution.py:88
  4.7 4.3 %collective-permute-done.1.low = f32[6,64,128]{2,1,0:T(8,128)S(1)} collective-permute-done((f32[6,64,128]{2,1,0:T(8,128)S(1)}, f32[6,64,128]{2,1,0:T(8,128)S(1)}, u32[]{:S(2)}, u32[]{:S(2)}) %collective-permute-start.1) | collective-permute-done | bytes 196640 | tf_op jit(solution)/shard_map/ppermute | solution.py:88
  9.0 1.7 %collective-permute-start.2 = (f32[256,128]{1,0:T(8,128)S(1)}, f32[256,128]{1,0:T(8,128)S(1)}, u32[]{:S(2)}, u32[]{:S(2)}) collective-permute-start(f32[256,128]{1,0:T(8,128)S(1)} %get-tuple-element.29), channel_id=1, source_target_pairs={{0,8},{8,16},{16,24},{24,32},{32,40},{40,48},{48,56},{56,0},{1,9},... | collective-permute-start | bytes 393224 | tf_op jit(solution)/shard_map/ppermute | solution.py:88
  11.3 1.6 %collective-permute-done.2.below.below_y = f32[256,128]{1,0:T(8,128)S(1)} collective-permute-done((f32[256,128]{1,0:T(8,128)S(1)}, f32[256,128]{1,0:T(8,128)S(1)}, u32[]{:S(2)}, u32[]{:S(2)}) %collective-permute-start.2) | collective-permute-done | bytes 131104 | tf_op jit(solution)/shard_map/ppermute | solution.py:88
  12.9 3.0 %collective-permute-done.3.above.above_y = f32[256,128]{1,0:T(8,128)S(1)} collective-permute-done((f32[256,128]{1,0:T(8,128)S(1)}, f32[256,128]{1,0:T(8,128)S(1)}, u32[]{:S(2)}, u32[]{:S(2)}) %collective-permute-start.3) | collective-permute-done | bytes 131104 | tf_op jit(solution)/shard_map/ppermute | solution.py:88
  16.2 2.8 %collective-permute-start.4 = (f32[2,88,128]{2,1,0:T(8,128)S(1)}, f32[2,88,128]{2,1,0:T(8,128)S(1)}, u32[]{:S(2)}, u32[]{:S(2)}) collective-permute-start(f32[2,88,128]{2,1,0:T(8,128)S(1)} %get-tuple-element.33), channel_id=1, source_target_pairs={{0,1},{1,2},{2,3},{3,4},{4,5},{5,6},{6,7},{7,0},{8,9},{9,10},{10,1... | collective-permute-start | bytes 270344 | tf_op jit(solution)/shard_map/ppermute | solution.py:88
  19.0 1.6 %collective-permute-done.4.below = f32[2,88,128]{2,1,0:T(8,128)S(1)} collective-permute-done((f32[2,88,128]{2,1,0:T(8,128)S(1)}, f32[2,88,128]{2,1,0:T(8,128)S(1)}, u32[]{:S(2)}, u32[]{:S(2)}) %collective-permute-start.4) | collective-permute-done | bytes 90144 | tf_op jit(solution)/shard_map/ppermute | solution.py:88
  20.6 3.6 %collective-permute-done.5.above = f32[2,88,128]{2,1,0:T(8,128)S(1)} collective-permute-done((f32[2,88,128]{2,1,0:T(8,128)S(1)}, f32[2,88,128]{2,1,0:T(8,128)S(1)}, u32[]{:S(2)}, u32[]{:S(2)}) %collective-permute-start.5) | collective-permute-done | bytes 90144 | tf_op jit(solution)/shard_map/ppermute | solution.py:88
  24.2 3.9 %shard_map.44 = (f32[8,64,128]{2,1,0:T(8,128)S(1)}, f32[14,88,256]{2,1,0:T(8,128)S(1)}, f32[14,88,256]{2,1,0:T(8,128)S(1)}, f32[14,88,256]{2,1,0:T(8,128)S(1)}, f32[200,128]{1,0:T(8,128)S(1)}) custom-call(f32[8,64,128]{2,1,0:T(8,128)S(1)} %copy-done, f32[8,64,128]{2,1,0:T(8,128)S(1)} %copy-done.1, f32[6,64,128]{2,1,0:T(8,128)S(1)} %collective-permute-done.high, ...), custom_call_target="tpu_custom_call" | custom-call | bytes 14760000 | tf_op jit(solution)/shard_map/pallas_call | solution.py:75
  28.1 1.4 %collective-permute-start.6 = (f32[200,128]{1,0:T(8,128)S(1)}, f32[200,128]{1,0:T(8,128)S(1)}, u32[]{:S(2)}, u32[]{:S(2)}) collective-permute-start(f32[200,128]{1,0:T(8,128)S(1)} %get-tuple-element.35.own), channel_id=1, source_target_pairs={{0,64},{64,128},{128,192},{192,0},{1,65},{65,129},{129,193},{193,1... | collective-permute-start | bytes 307208 | tf_op jit(solution)/shard_map/ppermute | solution.py:88
  29.5 1.5 %collective-permute-start.7 = (f32[200,128]{1,0:T(8,128)S(1)}, f32[200,128]{1,0:T(8,128)S(1)}, u32[]{:S(2)}, u32[]{:S(2)}) collective-permute-start(f32[200,128]{1,0:T(8,128)S(1)} %get-tuple-element.35.own), channel_id=1, source_target_pairs={{0,192},{64,0},{128,64},{192,128},{1,193},{65,1},{129,65},{193,129... | collective-permute-start | bytes 307208 | tf_op jit(solution)/shard_map/ppermute | solution.py:88
  30.9 1.3 %collective-permute-start.8 = (f32[200,128]{1,0:T(8,128)S(1)}, f32[200,128]{1,0:T(8,128)S(1)}, u32[]{:S(2)}, u32[]{:S(2)}) collective-permute-start(f32[200,128]{1,0:T(8,128)S(1)} %get-tuple-element.35.own), channel_id=1, source_target_pairs={{0,128},{64,192},{128,0},{192,64},{1,129},{65,193},{129,1},{193,65... | collective-permute-start | bytes 307208 | tf_op jit(solution)/shard_map/ppermute | solution.py:88
  32.3 0.9 %collective-permute-done.6.low.after = f32[200,128]{1,0:T(8,128)S(1)} collective-permute-done((f32[200,128]{1,0:T(8,128)S(1)}, f32[200,128]{1,0:T(8,128)S(1)}, u32[]{:S(2)}, u32[]{:S(2)}) %collective-permute-start.6) | collective-permute-done | bytes 102432 | tf_op jit(solution)/shard_map/ppermute | solution.py:88
  33.9 2.3 %collective-permute-start.14 = (f32[288,128]{1,0:T(8,128)S(1)}, f32[288,128]{1,0:T(8,128)S(1)}, u32[]{:S(2)}, u32[]{:S(2)}) collective-permute-start(f32[288,128]{1,0:T(8,128)S(1)} %get-tuple-element.55), channel_id=1, source_target_pairs={{0,192},{64,0},{128,64},{192,128},{1,193},{65,1},{129,65},{193,129... | collective-permute-start | bytes 442376 | tf_op jit(solution)/shard_map/ppermute | solution.py:88
  36.7 2.0 %shard_map.45 = (f32[16,40,128]{2,1,0:T(8,128)S(1)}, f32[16,40,128]{2,1,0:T(8,128)S(1)}, f32[16,40,128]{2,1,0:T(8,128)S(1)}, f32[8,16,128]{2,1,0:T(8,128)S(1)}, ...) custom-call(f32[200,128]{1,0:T(8,128)S(1)} %get-tuple-element.35.own, ...), custom_call_target="tpu_custom_call" | custom-call | bytes 7380000 | tf_op jit(solution)/shard_map/pallas_call | solution.py:75
  38.7 3.0 %collective-permute-start.10 = (f32[96,128]{1,0:T(8,128)S(1)}, f32[96,128]{1,0:T(8,128)S(1)}, u32[]{:S(2)}, u32[]{:S(2)}) collective-permute-start(f32[96,128]{1,0:T(8,128)S(1)} %get-tuple-element.39), channel_id=1, source_target_pairs={{0,8},{8,16},{16,24},{24,32},{32,40},{40,48},{48,56},{56,0},{1,9},... | collective-permute-start | bytes 147464 | tf_op jit(solution)/shard_map/ppermute | solution.py:88
  42.9 1.8 %collective-permute-done.9.above = f32[96,128]{1,0:T(8,128)S(1)} collective-permute-done((f32[96,128]{1,0:T(8,128)S(1)}, f32[96,128]{1,0:T(8,128)S(1)}, u32[]{:S(2)}, u32[]{:S(2)}) %collective-permute-start.9) | collective-permute-done | bytes 49184 | tf_op jit(solution)/shard_map/ppermute | solution.py:88
  45.2 2.9 %collective-permute-start.11 = (f32[80,128]{1,0:T(8,128)S(1)}, f32[80,128]{1,0:T(8,128)S(1)}, u32[]{:S(2)}, u32[]{:S(2)}) collective-permute-start(f32[80,128]{1,0:T(8,128)S(1)} %get-tuple-element.44), channel_id=1, source_target_pairs={{0,1},{1,2},{2,3},{3,4},{4,5},{5,6},{6,7},{7,0},{8,9},{9,10},{10,1... | collective-permute-start | bytes 122888 | tf_op jit(solution)/shard_map/ppermute | solution.py:88
  48.1 1.1 %collective-permute-done.11.left = f32[80,128]{1,0:T(8,128)S(1)} collective-permute-done((f32[80,128]{1,0:T(8,128)S(1)}, f32[80,128]{1,0:T(8,128)S(1)}, u32[]{:S(2)}, u32[]{:S(2)}) %collective-permute-start.11) | collective-permute-done | bytes 40992 | tf_op jit(solution)/shard_map/ppermute | solution.py:88
  49.2 3.5 %collective-permute-done.12.right = f32[80,128]{1,0:T(8,128)S(1)} collective-permute-done((f32[80,128]{1,0:T(8,128)S(1)}, f32[80,128]{1,0:T(8,128)S(1)}, u32[]{:S(2)}, u32[]{:S(2)}) %collective-permute-start.12) | collective-permute-done | bytes 40992 | tf_op jit(solution)/shard_map/ppermute | solution.py:88
  53.4 1.4 %shard_map.49.sol1 = f32[20,48,128]{2,1,0:T(8,128)S(1)} custom-call(f32[8,32,128]{2,1,0:T(8,128)S(1)} %shard_map.48.sol2, f32[16,40,128]{2,1,0:T(8,128)S(1)} %get-tuple-element.40.res, f32[16,40,128]{2,1,0:T(8,128)S(1)} %get-tuple-element.41.sol, f32[16,40,128]{2,1,0:T(8,128)S(1)} %get-tuple-element.46.coef1, f32[96,128]{1,0:T(8,128)S(1)} %collective-permute-done.9.above, ...), custom_call_target="tpu_custom_call" | custom-call | bytes 7380000 | tf_op jit(solution)/shard_map/pallas_call | solution.py:75
  54.9 3.3 %shard_map.51 = (f32[8,64,128]{2,1,0:T(8,128)}, f32[8,64,128]{2,1,0:T(8,128)}) custom-call(f32[20,48,128]{2,1,0:T(8,128)S(1)} %shard_map.49.sol1, f32[8,64,128]{2,1,0:T(8,128)S(1)} %get-tuple-element.47.sol0, f32[8,72,256]{2,1,0:T(8,128)S(1)} %get-tuple-element.51.res_q, f32[14,72,256]{2,1,0:T(8,128)S(1)} %get-tuple-element.52.diag_q, ...), custom_call_target="tpu_custom_call" | custom-call | bytes 3690000 | tf_op jit(solution)/shard_map/pallas_call | solution.py:75
  (24 shorter events, 4.5 us)
Async XLA Ops:
  0.6 8.4 %copy-start = (f32[8,64,128]{2,1,0:T(8,128)S(1)}, f32[8,64,128]{2,1,0:T(8,128)}, u32[]{:S(2)}) copy-start(f32[8,64,128]{2,1,0:T(8,128)} %s.5) | copy-start | bytes 786436
  0.6 8.4 %copy-start.1 = (f32[8,64,128]{2,1,0:T(8,128)S(1)}, f32[8,64,128]{2,1,0:T(8,128)}, u32[]{:S(2)}) copy-start(f32[8,64,128]{2,1,0:T(8,128)} %c.5) | copy-start | bytes 786436
  1.8 7.2 %collective-permute-start.1 = (f32[6,64,128]{2,1,0:T(8,128)S(1)}, f32[6,64,128]{2,1,0:T(8,128)S(1)}, u32[]{:S(2)}, u32[]{:S(2)}) collective-permute-start(f32[6,64,128]{2,1,0:T(8,128)S(1)} %pad_maximum_fusion.1), channel_id=1, source_target_pairs={{0,64},{64,128},{128,192},{192,0},{1,65},{65,129},{129,193},{193,1... | collective-permute-start | bytes 589832 | tf_op jit(solution)/shard_map/ppermute | solution.py:88
  3.2 5.8 %collective-permute-start = (f32[6,64,128]{2,1,0:T(8,128)S(1)}, f32[6,64,128]{2,1,0:T(8,128)S(1)}, u32[]{:S(2)}, u32[]{:S(2)}) collective-permute-start(f32[6,64,128]{2,1,0:T(8,128)S(1)} %pad_maximum_fusion), channel_id=1, source_target_pairs={{0,192},{64,0},{128,64},{192,128},{1,193},{65,1},{129,65},{193,129... | collective-permute-start | bytes 589832 | tf_op jit(solution)/shard_map/ppermute | solution.py:88
  9.0 3.9 %collective-permute-start.2 = (f32[256,128]{1,0:T(8,128)S(1)}, f32[256,128]{1,0:T(8,128)S(1)}, u32[]{:S(2)}, u32[]{:S(2)}) collective-permute-start(f32[256,128]{1,0:T(8,128)S(1)} %get-tuple-element.29), channel_id=1, source_target_pairs={{0,8},{8,16},{16,24},{24,32},{32,40},{40,48},{48,56},{56,0},{1,9},... | collective-permute-start | bytes 393224 | tf_op jit(solution)/shard_map/ppermute | solution.py:88
  10.8 5.2 %collective-permute-start.3 = (f32[256,128]{1,0:T(8,128)S(1)}, f32[256,128]{1,0:T(8,128)S(1)}, u32[]{:S(2)}, u32[]{:S(2)}) collective-permute-start(f32[256,128]{1,0:T(8,128)S(1)} %get-tuple-element.30), channel_id=1, source_target_pairs={{0,56},{8,0},{16,8},{24,16},{32,24},{40,32},{48,40},{56,48},{1,57}... | collective-permute-start | bytes 393224 | tf_op jit(solution)/shard_map/ppermute | solution.py:88
  16.2 4.4 %collective-permute-start.4 = (f32[2,88,128]{2,1,0:T(8,128)S(1)}, f32[2,88,128]{2,1,0:T(8,128)S(1)}, u32[]{:S(2)}, u32[]{:S(2)}) collective-permute-start(f32[2,88,128]{2,1,0:T(8,128)S(1)} %get-tuple-element.33), channel_id=1, source_target_pairs={{0,1},{1,2},{2,3},{3,4},{4,5},{5,6},{6,7},{7,0},{8,9},{9,10},{10,1... | collective-permute-start | bytes 270344 | tf_op jit(solution)/shard_map/ppermute | solution.py:88
  19.0 5.2 %collective-permute-start.5 = (f32[2,88,128]{2,1,0:T(8,128)S(1)}, f32[2,88,128]{2,1,0:T(8,128)S(1)}, u32[]{:S(2)}, u32[]{:S(2)}) collective-permute-start(f32[2,88,128]{2,1,0:T(8,128)S(1)} %get-tuple-element.34), channel_id=1, source_target_pairs={{0,7},{1,0},{2,1},{3,2},{4,3},{5,4},{6,5},{7,6},{8,15},{9,8},{10,9... | collective-permute-start | bytes 270344 | tf_op jit(solution)/shard_map/ppermute | solution.py:88
  28.1 5.1 %collective-permute-start.6 = (f32[200,128]{1,0:T(8,128)S(1)}, f32[200,128]{1,0:T(8,128)S(1)}, u32[]{:S(2)}, u32[]{:S(2)}) collective-permute-start(f32[200,128]{1,0:T(8,128)S(1)} %get-tuple-element.35.own), channel_id=1, source_target_pairs={{0,64},{64,128},{128,192},{192,0},{1,65},{65,129},{129,193},{193,1... | collective-permute-start | bytes 307208 | tf_op jit(solution)/shard_map/ppermute | solution.py:88
  29.5 6.8 %collective-permute-start.7 = (f32[200,128]{1,0:T(8,128)S(1)}, f32[200,128]{1,0:T(8,128)S(1)}, u32[]{:S(2)}, u32[]{:S(2)}) collective-permute-start(f32[200,128]{1,0:T(8,128)S(1)} %get-tuple-element.35.own), channel_id=1, source_target_pairs={{0,192},{64,0},{128,64},{192,128},{1,193},{65,1},{129,65},{193,129... | collective-permute-start | bytes 307208 | tf_op jit(solution)/shard_map/ppermute | solution.py:88
  30.9 5.8 %collective-permute-start.8 = (f32[200,128]{1,0:T(8,128)S(1)}, f32[200,128]{1,0:T(8,128)S(1)}, u32[]{:S(2)}, u32[]{:S(2)}) collective-permute-start(f32[200,128]{1,0:T(8,128)S(1)} %get-tuple-element.35.own), channel_id=1, source_target_pairs={{0,128},{64,192},{128,0},{192,64},{1,129},{65,193},{129,1},{193,65... | collective-permute-start | bytes 307208 | tf_op jit(solution)/shard_map/ppermute | solution.py:88
  33.5 21.3 %collective-permute-start.13 = (f32[288,128]{1,0:T(8,128)S(1)}, f32[288,128]{1,0:T(8,128)S(1)}, u32[]{:S(2)}, u32[]{:S(2)}) collective-permute-start(f32[288,128]{1,0:T(8,128)S(1)} %get-tuple-element.54), channel_id=1, source_target_pairs={{0,64},{64,128},{128,192},{192,0},{1,65},{65,129},{129,193},{193,1... | collective-permute-start | bytes 442376 | tf_op jit(solution)/shard_map/ppermute | solution.py:88
  33.9 20.9 %collective-permute-start.14 = (f32[288,128]{1,0:T(8,128)S(1)}, f32[288,128]{1,0:T(8,128)S(1)}, u32[]{:S(2)}, u32[]{:S(2)}) collective-permute-start(f32[288,128]{1,0:T(8,128)S(1)} %get-tuple-element.55), channel_id=1, source_target_pairs={{0,192},{64,0},{128,64},{192,128},{1,193},{65,1},{129,65},{193,129... | collective-permute-start | bytes 442376 | tf_op jit(solution)/shard_map/ppermute | solution.py:88
  38.7 4.2 %collective-permute-start.10 = (f32[96,128]{1,0:T(8,128)S(1)}, f32[96,128]{1,0:T(8,128)S(1)}, u32[]{:S(2)}, u32[]{:S(2)}) collective-permute-start(f32[96,128]{1,0:T(8,128)S(1)} %get-tuple-element.39), channel_id=1, source_target_pairs={{0,8},{8,16},{16,24},{24,32},{32,40},{40,48},{48,56},{56,0},{1,9},... | collective-permute-start | bytes 147464 | tf_op jit(solution)/shard_map/ppermute | solution.py:88
  41.7 2.9 %collective-permute-start.9 = (f32[96,128]{1,0:T(8,128)S(1)}, f32[96,128]{1,0:T(8,128)S(1)}, u32[]{:S(2)}, u32[]{:S(2)}) collective-permute-start(f32[96,128]{1,0:T(8,128)S(1)} %get-tuple-element.38), channel_id=1, source_target_pairs={{0,56},{8,0},{16,8},{24,16},{32,24},{40,32},{48,40},{56,48},{1,57}... | collective-permute-start | bytes 147464 | tf_op jit(solution)/shard_map/ppermute | solution.py:88
  45.2 4.0 %collective-permute-start.11 = (f32[80,128]{1,0:T(8,128)S(1)}, f32[80,128]{1,0:T(8,128)S(1)}, u32[]{:S(2)}, u32[]{:S(2)}) collective-permute-start(f32[80,128]{1,0:T(8,128)S(1)} %get-tuple-element.44), channel_id=1, source_target_pairs={{0,1},{1,2},{2,3},{3,4},{4,5},{5,6},{6,7},{7,0},{8,9},{9,10},{10,1... | collective-permute-start | bytes 122888 | tf_op jit(solution)/shard_map/ppermute | solution.py:88
  48.1 4.6 %collective-permute-start.12 = (f32[80,128]{1,0:T(8,128)S(1)}, f32[80,128]{1,0:T(8,128)S(1)}, u32[]{:S(2)}, u32[]{:S(2)}) collective-permute-start(f32[80,128]{1,0:T(8,128)S(1)} %get-tuple-element.45), channel_id=1, source_target_pairs={{0,7},{1,0},{2,1},{3,2},{4,3},{5,4},{6,5},{7,6},{8,15},{9,8},{10,9... | collective-permute-start | bytes 122888 | tf_op jit(solution)/shard_map/ppermute | solution.py:88

commit v6 on v5

--- a/solution.py
+++ b/solution.py
@@ -88,25 +88,55 @@
     return lax.ppermute(value, axis, [(i, (i + shift) % size) for i in range(size)])
 
 
+SLABS = [(0, x) for x in range(NXE)] + [(1, x) for x in range(1, NXE - 1)]
+SLAB = {slab: at for at, slab in enumerate(SLABS)}
+YROWS = 240
+
+
 def plane_of(own, low, high, which, x):
     if x < XH:
-        return low.at[which * XH + x]
+        return low.at[x if which == 0 else XH + x - 1]
     if x < XH + NX0:
         return own[which].at[x - XH]
-    return high.at[which * XH + x - XH - NX0]
+    return high.at[x - XH - NX0 + (0 if which == 0 else XH)]
+
+
+def pack_x(s, c, up, down, work, done):
+    copies = []
+
+    def fetch(src, dst):
+        copies.append(pltpu.make_async_copy(src, dst, done.at[len(copies)]))
+        copies[-1].start()
+
+    fetch(s.at[pl.ds(NX0 - XH, XH)], up.at[pl.ds(0, XH)])
+    fetch(c.at[pl.ds(NX0 - XH, 1)], work.at[pl.ds(0, 1)])
+    fetch(s.at[pl.ds(0, XH)], down.at[pl.ds(0, XH)])
+    fetch(c.at[pl.ds(XH - 1, 1)], work.at[pl.ds(1, 1)])
+    fetch(c.at[pl.ds(NX0 - XH + 1, XH - 1)], up.at[pl.ds(XH, XH - 1)])
+    fetch(c.at[pl.ds(0, XH - 1)], down.at[pl.ds(XH, XH - 1)])
+    for copy in copies:
+        copy.wait()
+    up[0] = up[0] * (1.0 / (work[0] + 6.0)) * (1.0 / THETA)
+    down[XH - 1] = down[XH - 1] * (1.0 / (work[1] + 6.0)) * (1.0 / THETA)
+
+
+def fetch_own(after, s, c, s_out, c_out, done):
+    copies = [pltpu.make_async_copy(s, s_out, done.at[0]), pltpu.make_async_copy(c, c_out, done.at[1])]
+    for copy in copies:
+        copy.start()
+    for copy in copies:
+        copy.wait()
 
 
 def pack_y(s, c, high, low, up, down):
-    for a in range(2):
-        for x in range(NXE):
-            src = plane_of((s, c), low, high, a, x)
-            at = a * NXE + x
-            up[at * 8 : at * 8 + 8, :] = src[56:64, :]
-            down[at * 8 : at * 8 + 8, :] = src[0:8, :]
-            up[224 + at : 225 + at, :] = src[55:56, :]
-            down[224 + at : 225 + at, :] = src[8:9, :]
-    up[252:256, :] = jnp.zeros((4, 128), F32)
-    down[252:256, :] = jnp.zeros((4, 128), F32)
+    for (a, x), at in SLAB.items():
+        src = plane_of((s, c), low, high, a, x)
+        up[at * 8 : at * 8 + 8, :] = src[56:64, :]
+        down[at * 8 : at * 8 + 8, :] = src[0:8, :]
+        up[208 + at : 209 + at, :] = src[55:56, :]
+        down[208 + at : 209 + at, :] = src[8:9, :]
+    up[234:YROWS, :] = jnp.zeros((YROWS - 234, 128), F32)
+    down[234:YROWS, :] = jnp.zeros((YROWS - 234, 128), F32)
 
 
 def pack_wide(up, down, row, count, plane):
@@ -114,7 +144,7 @@
     for a in range(2):
         ups = jnp.zeros((count, 128), F32)
         downs = jnp.zeros((count, 128), F32)
-        for x in range(NXE):
+        for x in range(a, NXE - a):
             v = plane(a, x)
             here = (lane >= W * x) & (lane < W * x + W)
             ups = jnp.where(here, turn(v, W * x - (128 - W), 1), ups)
@@ -124,10 +154,10 @@
 
 
 def halo_rows(below, above, a, x):
-    at = a * NXE + x
+    at = SLAB[a, x]
     row = rows_of((8, 128))
-    middle = jnp.where(row == 0, above[224 + at : 225 + at, :], 0.0)
-    middle = jnp.where(row == 7, below[224 + at : 225 + at, :], middle)
+    middle = jnp.where(row == 0, above[208 + at : 209 + at, :], 0.0)
+    middle = jnp.where(row == 7, below[208 + at : 209 + at, :], middle)
     return jnp.concatenate([above[at * 8 : at * 8 + 8, :], middle, below[at * 8 : at * 8 + 8, :]], 0)
 
 
@@ -141,18 +171,14 @@
     pack_wide(up, down, 64, 24, lambda a, x: halo_rows(below, above, a, x))
 
 
-def fine_sweep(src, dst, res, diag, inverse, first, stop, pair, also):
-    def body(x, carry):
+def fine_sweep(src, dst, res, diag, inverse, first, stop, pair):
+    for x in range(first, stop):
         d = src[x]
         near = beside(d) + (src[x - 1] + src[x + 1])
         r = res[x] - (diag[x] * d - near)
         res[x] = r
-        also(x, d)
         if pair is not None:
             dst[x] = pair[0] * d + (pair[1] * inverse[x]) * r
-        return carry
-
-    lax.fori_loop(first, stop, body, 0, unroll=True)
 
 
 def to_q0(ref, x):
@@ -161,12 +187,12 @@
 
 
 def fine_before(
-    s, c, high, low, below_y, above_y, below, above, sol, res, diag, inv, msg, da, db, rows
+    s, c, high, low, below_y, above_y, below, above, sol, res, diag, inv, msg, da, db, dc, rows
 ):
     lane = lanes_of((R0, 128))
     for a in range(2):
         left, right = below[a], above[a]
-        for x in range(NXE):
+        for x in range(a, NXE - a):
             side = jnp.where(lane < W, turn(right, -W * x, 1), 0.0)
             side = jnp.where(lane >= 128 - W, turn(left, 128 - W - W * x, 1), side)
             ref = (res, diag)[a]
@@ -191,34 +217,25 @@
     in_yz = inside_yz((R0, 256), 64, 76, 128, 192)
     low_x, high_x = gx > 0, gx < lax.axis_size("gx") - 1
 
-    def start(x, carry):
+    for x in range(NXE):
+        here = in_yz & (low_x if x < XH else high_x) if x < XH or x >= XH + NX0 else in_yz
+        if x in (0, NXE - 1):
+            da[x] = jnp.where(here, res[x], 0.0)
+            continue
         g = diag[x] + 6.0
         diag[x] = g
-        here = ((x >= XH) | low_x) & ((x < XH + NX0) | high_x)
-        inverse = jnp.where(in_yz & here, 1.0 / g, 0.0)
+        inverse = jnp.where(here, 1.0 / g, 0.0)
         inv[x] = inverse
         da[x] = res[x] * inverse * (1.0 / THETA)
-        return carry
-
-    lax.fori_loop(0, NXE, start, 0, unroll=True)
-
     pairs = coefficients(SWEEPS)
-    buffers = (da, db)
+    steps = (da, db, dc)
     for k in range(SWEEPS):
-        src, dst = buffers[k % 2], buffers[(k + 1) % 2]
         last = k == SWEEPS - 1
-
-        def nothing(x, d):
-            return None
-
-        fine_sweep(src, dst, res, diag, inv, k + 1, NXE - 1 - k, None if last else pairs[k], nothing)
-
-        def gather(x, carry):
-            own = src[XH + x, 0:64, 0:128]
-            sol[x] = own if k == 0 else sol[x] + own
-            return carry
-
-        lax.fori_loop(0, NX0, gather, 0, unroll=True)
+        fine_sweep(
+            steps[k], None if last else steps[k + 1], res, diag, inv, k + 1, NXE - 1 - k, None if last else pairs[k]
+        )
+    for x in range(NX0):
+        sol[x] = sum(d[XH + x, 0:64, 0:128] for d in steps)
 
     halo = jnp.zeros((R1, 128), F32)
     for i in range(4):
@@ -349,7 +366,7 @@
 
 def keep_fine(after, res0, diag0, inv0, res_q, diag_q, inv_q, r0_up, r0_down):
     for ref, kept, skip in ((res0, res_q, XH), (diag0, diag_q, 0), (inv0, inv_q, 0)):
-        for x in range(kept.shape[0]):
+        for x in range(NX0) if skip else range(1, NXE - 1):
             top, tail = to_q0(ref, x + skip)
             kept[x, 0:64, :] = top
             kept[x, 64:72, :] = tail
@@ -362,6 +379,11 @@
             base = 6 * i
             side = jnp.where((lane >= base) & (lane < base + 3), turn(v, base, 1), side)
             side = jnp.where((lane >= base + 3) & (lane < base + 6), turn(v, base + 3 - 125, 1), side)
+        far = 2 * XH + NX0 - 6 if first else 2 * XH - 1
+        msg[4 * Q0 : 5 * Q0, :] = diag_q[far, :, 0:128]
+        v = diag_q[far, :, 128:256]
+        side = jnp.where((lane >= 18) & (lane < 21), turn(v, 18, 1), side)
+        side = jnp.where((lane >= 21) & (lane < 24), turn(v, 21 - 125, 1), side)
         msg[XH * Q0 : XH * Q0 + Q0, :] = side
 
 
@@ -465,7 +487,7 @@
 
 
 def fine_after(
-    sol1, sol0, res_q, diag_q, inv_q, low, high, out_sol, out_res, p0, res0, da0, db0
+    sol1, sol0, res_q, diag_q, inv_q, low, high, out_sol, out_res, p0, res0, da0, db0, dc0
 ):
     gx = lax.axis_index("gx")
     half = lanes_of((R1, 128)) // 2
@@ -483,63 +505,67 @@
         return jnp.concatenate([p0[x, 0, 0:Q0, :], p0[x, 1, 0:Q0, :]], 1)
 
     lane72 = lanes_of((Q0, 128))
-    for msg, first in ((low, 0), (high, XH + NX0)):
+
+    def with_lanes(main, side, base):
+        v = jnp.where(lane72 < 3, turn(side, -base, 1), 0.0)
+        v = jnp.where(lane72 < 125, v, turn(side, 125 - base - 3, 1))
+        return jnp.concatenate([main, v], 1)
+
+    outer = {}
+    for msg, first, far in ((low, 0, 0), (high, XH + NX0, NXE - 1)):
         side = msg[XH * Q0 : XH * Q0 + Q0, :]
         for i in range(XH):
-            base = 6 * i
-            v = jnp.where(lane72 < 3, turn(side, -base, 1), 0.0)
-            v = jnp.where(lane72 < 125, v, turn(side, 125 - base - 3, 1))
-            res0[first + i, :, 0:128] = msg[i * Q0 : i * Q0 + Q0, :]
-            res0[first + i, :, 128:256] = v
-
-    def fetch(x, carry):
-        res0[x + XH] = res_q[x]
-        return carry
-
-    lax.fori_loop(0, NX0, fetch, 0, unroll=True)
-
-    def correct0(x, carry):
+            outer[first + i] = with_lanes(msg[i * Q0 : i * Q0 + Q0, :], side, 6 * i)
+        outer["diag", far] = with_lanes(msg[4 * Q0 : 5 * Q0, :], side, 18)
+    in_yz = inside_yz((Q0, 256), 64, 68, 128, 192)
+    low_x, high_x = gx > 0, gx < lax.axis_size("gx") - 1
+    for x in range(NXE):
         p = lift(x + 1)
         near = beside(p) + (lift(x) + lift(x + 2))
-        r = res0[x] - (diag_q[x] * p - near)
+        if x in (0, NXE - 1):
+            g = outer["diag", x]
+            inverse = jnp.where(in_yz & (low_x if x == 0 else high_x), 1.0 / g, 0.0)
+        else:
+            g, inverse = diag_q[x], inv_q[x]
+        r = (outer[x] if x in outer else res_q[x - XH]) - (g * p - near)
         res0[x] = r
-        da0[x] = r * inv_q[x] * (1.0 / THETA)
-        return carry
-
-    lax.fori_loop(0, NXE, correct0, 0, unroll=True)
-
-    def begin(x, carry):
-        out_sol[x] = sol0[x] + p0[x + XH + 1, 0, 0:64, :]
-        return carry
-
-    lax.fori_loop(0, NX0, begin, 0, unroll=True)
+        da0[x] = r * inverse * (1.0 / THETA)
     pairs = coefficients(SWEEPS)
-    buffers = (da0, db0)
-    for k in range(SWEEPS):
-        src, dst = buffers[k % 2], buffers[(k + 1) % 2]
-
-        def gather0(x, carry):
-            out_sol[x] += src[x + XH, 0:64, 0:128]
-            return carry
-
-        lax.fori_loop(0, NX0, gather0, 0, unroll=True)
-        fine_sweep(
-            src, dst, res0, diag_q, inv_q, k + 1, NXE - 1 - k, pairs[k] if k < SWEEPS - 1 else None,
-            lambda x, d: None,
-        )
-
-    def put(x, carry):
-        out_res[x] = res0[x + XH, 0:64, 0:128]
-        return carry
-
-    lax.fori_loop(0, NX0, put, 0, unroll=True)
+    steps = (da0, db0, dc0)
+    for k in range(SWEEPS - 1):
+        fine_sweep(steps[k], steps[k + 1], res0, diag_q, inv_q, k + 1, NXE - 1 - k, pairs[k])
+    for x in range(NX0):
+        at = x + XH
+        d = dc0[at]
+        near = beside(d)[0:64, 0:128] + (dc0[at - 1, 0:64, 0:128] + dc0[at + 1, 0:64, 0:128])
+        d = d[0:64, 0:128]
+        out_res[x] = res0[at, 0:64, 0:128] - (diag_q[at, 0:64, 0:128] * d - near)
+        own = da0[at, 0:64, 0:128] + db0[at, 0:64, 0:128] + d
+        out_sol[x] = sol0[x] + p0[at + 1, 0, 0:64, :] + own
 
 
 def per_device(s, c):
-    up = jnp.concatenate([s[NX0 - XH :], c[NX0 - XH :]], 0)
-    down = jnp.concatenate([s[:XH], c[:XH]], 0)
+    s, c = (pltpu.with_memory_space_constraint(v, pltpu.HBM) for v in (s, c))
+    face = jax.ShapeDtypeStruct((2 * XH - 1, NY0, NZ0), F32)
+    up, down = pl.pallas_call(
+        pack_x,
+        out_shape=[face] * 2,
+        in_specs=[pl.BlockSpec(memory_space=pl.ANY)] * 2,
+        out_specs=[pl.BlockSpec(memory_space=pltpu.VMEM)] * 2,
+        scratch_shapes=[pltpu.VMEM((2, NY0, NZ0), F32), pltpu.SemaphoreType.DMA((6,))],
+        compiler_params=pltpu.CompilerParams(vmem_limit_bytes=4 * MIB),
+    )(s, c)
+    s, c = pl.pallas_call(
+        fetch_own,
+        out_shape=[jax.ShapeDtypeStruct((NX0, NY0, NZ0), F32)] * 2,
+        in_specs=[pl.BlockSpec(memory_space=pl.ANY)] * 3,
+        out_specs=[pl.BlockSpec(memory_space=pltpu.VMEM)] * 2,
+        scratch_shapes=[pltpu.SemaphoreType.DMA((2,))],
+        compiler_params=pltpu.CompilerParams(vmem_limit_bytes=4 * MIB),
+        cost_estimate=pl.CostEstimate(flops=0, bytes_accessed=3690000, transcendentals=0),
+    )(up, s, c)
     low, high = ring(up, "gx", 1), ring(down, "gx", -1)
-    up, down = call(pack_y, 4, [(256, 128)] * 2, [], s, c, high, low)
+    up, down = call(pack_y, 4, [(YROWS, 128)] * 2, [], s, c, high, low)
     below_y, above_y = ring(up, "gy", 1), ring(down, "gy", -1)
     own_up, own_down = call(pack_z_own, 4, [(2, 64, 128)] * 2, [], s, c, high, low)
     up, down = call(pack_z_halo, 4, [(2, R0, 128)] * 2, [], own_up, own_down, below_y, above_y)
@@ -549,7 +575,7 @@
         fine_before,
         16,
         [(NX0, 64, 128), big, big, big, (200, 128)],
-        [big, big, (8, 2, 80, 128)],
+        [big, big, big, (8, 2, 80, 128)],
         s, c, high, low, below_y, above_y, below, above,
         micros=4.0,
     )
@@ -558,7 +584,7 @@
     res_q, diag_q, inv_q, r0_up, r0_down = call(
         keep_fine,
         8,
-        [(NX0, Q0, 256), big, big, (4 * Q0, 128), (4 * Q0, 128)],
+        [(NX0, Q0, 256), big, big, (5 * Q0, 128), (5 * Q0, 128)],
         [],
         low, res0, diag0, inv0,
         micros=2.0,
@@ -596,7 +622,7 @@
             fine_after,
             16,
             [own, own],
-            [(16, 2, 80, 128)] + [big] * 3,
+            [(16, 2, 80, 128)] + [big] * 4,
             sol1, sol0, res_q, diag_q, inv_q, r0_low, r0_high,
         )
     )

time: 58.2 us -> 57.4 us (0.986)
  Pallas kernels: 13.2 us -> 15.4 us
  waiting for transfers between devices: 22.7 us -> 20.8 us
  local copies, waits for them, and re-layouts: 1.13 us -> 0 us
    pallas_call x0 -> x2, Pallas kernels: none -> 2.12 us  [the longest x1 1.07 us: per_device(): pl.pallas_call(pack_x, out_shape=[face] * 2, in_specs=[pl.BlockSpec(memor...]
    ppermute x15, waiting for transfers between devices: 22.7 us -> 20.8 us  [ring(): lax.ppermute(value, axis, [(i, (i + shift) % size) for i in range(size)])]
    slice x1 -> x0, local copies, waits for them, and re-layouts: 1.12 us -> none  [per_device(): up = jnp.concatenate([s[NX0 - XH:], c[NX0 - XH:]], 0)]
  transfers between devices with their start and end apart: 15 -> 15, of which waited for: 11 -> 11; matrix products, arithmetic and copies ran while one was open for 0% -> 0% of each run, Pallas kernels for 10% -> 12%
where the time goes in v6:
time: 57.4 us; the launch traced here: 57.3 us
  waiting for transfers between devices  20.8 us (36%)
  starting transfers between devices  20.3 us (35%)
  Pallas kernels  15.4 us (27%)
  between operations  0.74 us (1%)
    ppermute x15, waiting for transfers between devices, ring(): lax.ppermute(value, axis, [(i, (i + shift) % size) for i in range(size)])  20.8 us
    ppermute x15, starting transfers between devices, ring(): lax.ppermute(value, axis, [(i, (i + shift) % size) for i in range(size)])  20.3 us
    pallas_call x11, Pallas kernels, call(): pl.pallas_call(body, out_shape=[jax.ShapeDtypeStruct(s, F32) for s in out...  13.3 us
  transfers between devices with their start and end apart: 15, of which 11 were waited for; matrix products, arithmetic and copies ran while one was open for 0% of the time, Pallas kernels for 12%

profile of v6, /device:TPU:71, one launch (start us, length us, event | category | flops | bytes accessed | tf_op | source)
XLA Modules:
  0.0 57.3 jit_solution(12273487876044770196)
XLA Ops:
  0.6 1.1 %shard_map.41 = (f32[5,64,128]{2,1,0:T(8,128)S(1)}, f32[5,64,128]{2,1,0:T(8,128)S(1)}) custom-call(f32[8,64,128]{2,1,0:T(8,128)} %s.3, f32[8,64,128]{2,1,0:T(8,128)} %c.3), custom_call_target="tpu_custom_call" | custom-call | tf_op jit(solution)/shard_map/pallas_call | solution.py:550
  1.7 1.4 %collective-permute-start.1 = (f32[5,64,128]{2,1,0:T(8,128)S(1)}, f32[5,64,128]{2,1,0:T(8,128)S(1)}, u32[]{:S(2)}, u32[]{:S(2)}) collective-permute-start(f32[5,64,128]{2,1,0:T(8,128)S(1)} %get-tuple-element.33.after), channel_id=1, source_target_pairs={{0,64},{64,128},{128,192},{192,0},{1,65},{65,129},{129,193},{193,1... | collective-permute-start | bytes 491528 | tf_op jit(solution)/shard_map/ppermute | solution.py:88
  3.1 1.5 %collective-permute-start = (f32[5,64,128]{2,1,0:T(8,128)S(1)}, f32[5,64,128]{2,1,0:T(8,128)S(1)}, u32[]{:S(2)}, u32[]{:S(2)}) collective-permute-start(f32[5,64,128]{2,1,0:T(8,128)S(1)} %get-tuple-element.36), channel_id=1, source_target_pairs={{0,192},{64,0},{128,64},{192,128},{1,193},{65,1},{129,65},{193,129... | collective-permute-start | bytes 491528 | tf_op jit(solution)/shard_map/ppermute | solution.py:88
  4.6 1.0 %shard_map.42 = (f32[8,64,128]{2,1,0:T(8,128)S(1)}, f32[8,64,128]{2,1,0:T(8,128)S(1)}) custom-call(f32[5,64,128]{2,1,0:T(8,128)S(1)} %get-tuple-element.33.after, f32[8,64,128]{2,1,0:T(8,128)} %s.3, f32[8,64,128]{2,1,0:T(8,128)} %c.3), custom_call_target="tpu_custom_call" | custom-call | bytes 3690000 | tf_op jit(solution)/shard_map/pallas_call | solution.py:558
  5.7 2.5 %collective-permute-done.1.low = f32[5,64,128]{2,1,0:T(8,128)S(1)} collective-permute-done((f32[5,64,128]{2,1,0:T(8,128)S(1)}, f32[5,64,128]{2,1,0:T(8,128)S(1)}, u32[]{:S(2)}, u32[]{:S(2)}) %collective-permute-start.1) | collective-permute-done | bytes 163872 | tf_op jit(solution)/shard_map/ppermute | solution.py:88
  8.2 1.7 %collective-permute-start.2 = (f32[240,128]{1,0:T(8,128)S(1)}, f32[240,128]{1,0:T(8,128)S(1)}, u32[]{:S(2)}, u32[]{:S(2)}) collective-permute-start(f32[240,128]{1,0:T(8,128)S(1)} %get-tuple-element.37), channel_id=1, source_target_pairs={{0,8},{8,16},{16,24},{24,32},{32,40},{40,48},{48,56},{56,0},{1,9},... | collective-permute-start | bytes 368648 | tf_op jit(solution)/shard_map/ppermute | solution.py:88
  10.5 1.6 %collective-permute-done.2.below.below_y = f32[240,128]{1,0:T(8,128)S(1)} collective-permute-done((f32[240,128]{1,0:T(8,128)S(1)}, f32[240,128]{1,0:T(8,128)S(1)}, u32[]{:S(2)}, u32[]{:S(2)}) %collective-permute-start.2) | collective-permute-done | bytes 122912 | tf_op jit(solution)/shard_map/ppermute | solution.py:88
  12.0 3.0 %collective-permute-done.3.above.above_y = f32[240,128]{1,0:T(8,128)S(1)} collective-permute-done((f32[240,128]{1,0:T(8,128)S(1)}, f32[240,128]{1,0:T(8,128)S(1)}, u32[]{:S(2)}, u32[]{:S(2)}) %collective-permute-start.3) | collective-permute-done | bytes 122912 | tf_op jit(solution)/shard_map/ppermute | solution.py:88
  15.3 2.7 %collective-permute-start.4 = (f32[2,88,128]{2,1,0:T(8,128)S(1)}, f32[2,88,128]{2,1,0:T(8,128)S(1)}, u32[]{:S(2)}, u32[]{:S(2)}) collective-permute-start(f32[2,88,128]{2,1,0:T(8,128)S(1)} %get-tuple-element.41), channel_id=1, source_target_pairs={{0,1},{1,2},{2,3},{3,4},{4,5},{5,6},{6,7},{7,0},{8,9},{9,10},{10,1... | collective-permute-start | bytes 270344 | tf_op jit(solution)/shard_map/ppermute | solution.py:88
  18.0 1.6 %collective-permute-done.4.below = f32[2,88,128]{2,1,0:T(8,128)S(1)} collective-permute-done((f32[2,88,128]{2,1,0:T(8,128)S(1)}, f32[2,88,128]{2,1,0:T(8,128)S(1)}, u32[]{:S(2)}, u32[]{:S(2)}) %collective-permute-start.4) | collective-permute-done | bytes 90144 | tf_op jit(solution)/shard_map/ppermute | solution.py:88
  19.6 3.6 %collective-permute-done.5.above = f32[2,88,128]{2,1,0:T(8,128)S(1)} collective-permute-done((f32[2,88,128]{2,1,0:T(8,128)S(1)}, f32[2,88,128]{2,1,0:T(8,128)S(1)}, u32[]{:S(2)}, u32[]{:S(2)}) %collective-permute-start.5) | collective-permute-done | bytes 90144 | tf_op jit(solution)/shard_map/ppermute | solution.py:88
  23.2 4.0 %shard_map.46 = (f32[8,64,128]{2,1,0:T(8,128)S(1)}, f32[14,88,256]{2,1,0:T(8,128)S(1)}, f32[14,88,256]{2,1,0:T(8,128)S(1)}, f32[14,88,256]{2,1,0:T(8,128)S(1)}, f32[200,128]{1,0:T(8,128)S(1)}) custom-call(f32[8,64,128]{2,1,0:T(8,128)S(1)} %get-tuple-element.34.s, f32[8,64,128]{2,1,0:T(8,128)S(1)} %get-tuple-element.35.c, ...), custom_call_target="tpu_custom_call" | custom-call | bytes 14760000 | tf_op jit(solution)/shard_map/pallas_call | solution.py:75
  27.2 1.4 %collective-permute-start.6 = (f32[200,128]{1,0:T(8,128)S(1)}, f32[200,128]{1,0:T(8,128)S(1)}, u32[]{:S(2)}, u32[]{:S(2)}) collective-permute-start(f32[200,128]{1,0:T(8,128)S(1)} %get-tuple-element.43.own), channel_id=1, source_target_pairs={{0,64},{64,128},{128,192},{192,0},{1,65},{65,129},{129,193},{193,1... | collective-permute-start | bytes 307208 | tf_op jit(solution)/shard_map/ppermute | solution.py:88
  28.6 1.5 %collective-permute-start.7 = (f32[200,128]{1,0:T(8,128)S(1)}, f32[200,128]{1,0:T(8,128)S(1)}, u32[]{:S(2)}, u32[]{:S(2)}) collective-permute-start(f32[200,128]{1,0:T(8,128)S(1)} %get-tuple-element.43.own), channel_id=1, source_target_pairs={{0,192},{64,0},{128,64},{192,128},{1,193},{65,1},{129,65},{193,129... | collective-permute-start | bytes 307208 | tf_op jit(solution)/shard_map/ppermute | solution.py:88
  30.1 1.3 %collective-permute-start.8 = (f32[200,128]{1,0:T(8,128)S(1)}, f32[200,128]{1,0:T(8,128)S(1)}, u32[]{:S(2)}, u32[]{:S(2)}) collective-permute-start(f32[200,128]{1,0:T(8,128)S(1)} %get-tuple-element.43.own), channel_id=1, source_target_pairs={{0,128},{64,192},{128,0},{192,64},{1,129},{65,193},{129,1},{193,65... | collective-permute-start | bytes 307208 | tf_op jit(solution)/shard_map/ppermute | solution.py:88
  33.0 2.3 %collective-permute-start.14 = (f32[360,128]{1,0:T(8,128)S(1)}, f32[360,128]{1,0:T(8,128)S(1)}, u32[]{:S(2)}, u32[]{:S(2)}) collective-permute-start(f32[360,128]{1,0:T(8,128)S(1)} %get-tuple-element.63), channel_id=1, source_target_pairs={{0,192},{64,0},{128,64},{192,128},{1,193},{65,1},{129,65},{193,129... | collective-permute-start | bytes 552968 | tf_op jit(solution)/shard_map/ppermute | solution.py:88
  35.8 2.0 %shard_map.47 = (f32[16,40,128]{2,1,0:T(8,128)S(1)}, f32[16,40,128]{2,1,0:T(8,128)S(1)}, f32[16,40,128]{2,1,0:T(8,128)S(1)}, f32[8,16,128]{2,1,0:T(8,128)S(1)}, ...) custom-call(f32[200,128]{1,0:T(8,128)S(1)} %get-tuple-element.43.own, ...), custom_call_target="tpu_custom_call" | custom-call | bytes 7380000 | tf_op jit(solution)/shard_map/pallas_call | solution.py:75
  37.8 3.0 %collective-permute-start.10 = (f32[96,128]{1,0:T(8,128)S(1)}, f32[96,128]{1,0:T(8,128)S(1)}, u32[]{:S(2)}, u32[]{:S(2)}) collective-permute-start(f32[96,128]{1,0:T(8,128)S(1)} %get-tuple-element.47), channel_id=1, source_target_pairs={{0,8},{8,16},{16,24},{24,32},{32,40},{40,48},{48,56},{56,0},{1,9},... | collective-permute-start | bytes 147464 | tf_op jit(solution)/shard_map/ppermute | solution.py:88
  42.0 1.8 %collective-permute-done.9.above = f32[96,128]{1,0:T(8,128)S(1)} collective-permute-done((f32[96,128]{1,0:T(8,128)S(1)}, f32[96,128]{1,0:T(8,128)S(1)}, u32[]{:S(2)}, u32[]{:S(2)}) %collective-permute-start.9) | collective-permute-done | bytes 49184 | tf_op jit(solution)/shard_map/ppermute | solution.py:88
  44.3 3.0 %collective-permute-start.11 = (f32[80,128]{1,0:T(8,128)S(1)}, f32[80,128]{1,0:T(8,128)S(1)}, u32[]{:S(2)}, u32[]{:S(2)}) collective-permute-start(f32[80,128]{1,0:T(8,128)S(1)} %get-tuple-element.52), channel_id=1, source_target_pairs={{0,1},{1,2},{2,3},{3,4},{4,5},{5,6},{6,7},{7,0},{8,9},{9,10},{10,1... | collective-permute-start | bytes 122888 | tf_op jit(solution)/shard_map/ppermute | solution.py:88
  47.3 1.1 %collective-permute-done.11.left = f32[80,128]{1,0:T(8,128)S(1)} collective-permute-done((f32[80,128]{1,0:T(8,128)S(1)}, f32[80,128]{1,0:T(8,128)S(1)}, u32[]{:S(2)}, u32[]{:S(2)}) %collective-permute-start.11) | collective-permute-done | bytes 40992 | tf_op jit(solution)/shard_map/ppermute | solution.py:88
  48.4 3.5 %collective-permute-done.12.right = f32[80,128]{1,0:T(8,128)S(1)} collective-permute-done((f32[80,128]{1,0:T(8,128)S(1)}, f32[80,128]{1,0:T(8,128)S(1)}, u32[]{:S(2)}, u32[]{:S(2)}) %collective-permute-start.12) | collective-permute-done | bytes 40992 | tf_op jit(solution)/shard_map/ppermute | solution.py:88
  52.6 1.4 %shard_map.51.sol1 = f32[20,48,128]{2,1,0:T(8,128)S(1)} custom-call(f32[8,32,128]{2,1,0:T(8,128)S(1)} %shard_map.50.sol2, f32[16,40,128]{2,1,0:T(8,128)S(1)} %get-tuple-element.48.res, f32[16,40,128]{2,1,0:T(8,128)S(1)} %get-tuple-element.49.sol, f32[16,40,128]{2,1,0:T(8,128)S(1)} %get-tuple-element.54.coef1, f32[96,128]{1,0:T(8,128)S(1)} %collective-permute-done.9.above, ...), custom_call_target="tpu_custom_call" | custom-call | bytes 7380000 | tf_op jit(solution)/shard_map/pallas_call | solution.py:75
  54.0 3.3 %shard_map.53 = (f32[8,64,128]{2,1,0:T(8,128)}, f32[8,64,128]{2,1,0:T(8,128)}) custom-call(f32[20,48,128]{2,1,0:T(8,128)S(1)} %shard_map.51.sol1, f32[8,64,128]{2,1,0:T(8,128)S(1)} %get-tuple-element.55.sol0, f32[8,72,256]{2,1,0:T(8,128)S(1)} %get-tuple-element.59.res_q, f32[14,72,256]{2,1,0:T(8,128)S(1)} %get-tuple-element.60.diag_q, ...), custom_call_target="tpu_custom_call" | custom-call | bytes 3690000 | tf_op jit(solution)/shard_map/pallas_call | solution.py:75
  (19 shorter events, 5.2 us)
Async XLA Ops:
  1.7 6.5 %collective-permute-start.1 = (f32[5,64,128]{2,1,0:T(8,128)S(1)}, f32[5,64,128]{2,1,0:T(8,128)S(1)}, u32[]{:S(2)}, u32[]{:S(2)}) collective-permute-start(f32[5,64,128]{2,1,0:T(8,128)S(1)} %get-tuple-element.33.after), channel_id=1, source_target_pairs={{0,64},{64,128},{128,192},{192,0},{1,65},{65,129},{129,193},{193,1... | collective-permute-start | bytes 491528 | tf_op jit(solution)/shard_map/ppermute | solution.py:88
  3.1 5.1 %collective-permute-start = (f32[5,64,128]{2,1,0:T(8,128)S(1)}, f32[5,64,128]{2,1,0:T(8,128)S(1)}, u32[]{:S(2)}, u32[]{:S(2)}) collective-permute-start(f32[5,64,128]{2,1,0:T(8,128)S(1)} %get-tuple-element.36), channel_id=1, source_target_pairs={{0,192},{64,0},{128,64},{192,128},{1,193},{65,1},{129,65},{193,129... | collective-permute-start | bytes 491528 | tf_op jit(solution)/shard_map/ppermute | solution.py:88
  8.2 3.8 %collective-permute-start.2 = (f32[240,128]{1,0:T(8,128)S(1)}, f32[240,128]{1,0:T(8,128)S(1)}, u32[]{:S(2)}, u32[]{:S(2)}) collective-permute-start(f32[240,128]{1,0:T(8,128)S(1)} %get-tuple-element.37), channel_id=1, source_target_pairs={{0,8},{8,16},{16,24},{24,32},{32,40},{40,48},{48,56},{56,0},{1,9},... | collective-permute-start | bytes 368648 | tf_op jit(solution)/shard_map/ppermute | solution.py:88
  10.0 5.1 %collective-permute-start.3 = (f32[240,128]{1,0:T(8,128)S(1)}, f32[240,128]{1,0:T(8,128)S(1)}, u32[]{:S(2)}, u32[]{:S(2)}) collective-permute-start(f32[240,128]{1,0:T(8,128)S(1)} %get-tuple-element.38), channel_id=1, source_target_pairs={{0,56},{8,0},{16,8},{24,16},{32,24},{40,32},{48,40},{56,48},{1,57}... | collective-permute-start | bytes 368648 | tf_op jit(solution)/shard_map/ppermute | solution.py:88
  15.3 4.3 %collective-permute-start.4 = (f32[2,88,128]{2,1,0:T(8,128)S(1)}, f32[2,88,128]{2,1,0:T(8,128)S(1)}, u32[]{:S(2)}, u32[]{:S(2)}) collective-permute-start(f32[2,88,128]{2,1,0:T(8,128)S(1)} %get-tuple-element.41), channel_id=1, source_target_pairs={{0,1},{1,2},{2,3},{3,4},{4,5},{5,6},{6,7},{7,0},{8,9},{9,10},{10,1... | collective-permute-start | bytes 270344 | tf_op jit(solution)/shard_map/ppermute | solution.py:88
  18.0 5.2 %collective-permute-start.5 = (f32[2,88,128]{2,1,0:T(8,128)S(1)}, f32[2,88,128]{2,1,0:T(8,128)S(1)}, u32[]{:S(2)}, u32[]{:S(2)}) collective-permute-start(f32[2,88,128]{2,1,0:T(8,128)S(1)} %get-tuple-element.42), channel_id=1, source_target_pairs={{0,7},{1,0},{2,1},{3,2},{4,3},{5,4},{6,5},{7,6},{8,15},{9,8},{10,9... | collective-permute-start | bytes 270344 | tf_op jit(solution)/shard_map/ppermute | solution.py:88
  27.2 5.1 %collective-permute-start.6 = (f32[200,128]{1,0:T(8,128)S(1)}, f32[200,128]{1,0:T(8,128)S(1)}, u32[]{:S(2)}, u32[]{:S(2)}) collective-permute-start(f32[200,128]{1,0:T(8,128)S(1)} %get-tuple-element.43.own), channel_id=1, source_target_pairs={{0,64},{64,128},{128,192},{192,0},{1,65},{65,129},{129,193},{193,1... | collective-permute-start | bytes 307208 | tf_op jit(solution)/shard_map/ppermute | solution.py:88
  28.6 6.8 %collective-permute-start.7 = (f32[200,128]{1,0:T(8,128)S(1)}, f32[200,128]{1,0:T(8,128)S(1)}, u32[]{:S(2)}, u32[]{:S(2)}) collective-permute-start(f32[200,128]{1,0:T(8,128)S(1)} %get-tuple-element.43.own), channel_id=1, source_target_pairs={{0,192},{64,0},{128,64},{192,128},{1,193},{65,1},{129,65},{193,129... | collective-permute-start | bytes 307208 | tf_op jit(solution)/shard_map/ppermute | solution.py:88
  30.1 5.7 %collective-permute-start.8 = (f32[200,128]{1,0:T(8,128)S(1)}, f32[200,128]{1,0:T(8,128)S(1)}, u32[]{:S(2)}, u32[]{:S(2)}) collective-permute-start(f32[200,128]{1,0:T(8,128)S(1)} %get-tuple-element.43.own), channel_id=1, source_target_pairs={{0,128},{64,192},{128,0},{192,64},{1,129},{65,193},{129,1},{193,65... | collective-permute-start | bytes 307208 | tf_op jit(solution)/shard_map/ppermute | solution.py:88
  32.6 21.4 %collective-permute-start.13 = (f32[360,128]{1,0:T(8,128)S(1)}, f32[360,128]{1,0:T(8,128)S(1)}, u32[]{:S(2)}, u32[]{:S(2)}) collective-permute-start(f32[360,128]{1,0:T(8,128)S(1)} %get-tuple-element.62), channel_id=1, source_target_pairs={{0,64},{64,128},{128,192},{192,0},{1,65},{65,129},{129,193},{193,1... | collective-permute-start | bytes 552968 | tf_op jit(solution)/shard_map/ppermute | solution.py:88
  33.0 21.0 %collective-permute-start.14 = (f32[360,128]{1,0:T(8,128)S(1)}, f32[360,128]{1,0:T(8,128)S(1)}, u32[]{:S(2)}, u32[]{:S(2)}) collective-permute-start(f32[360,128]{1,0:T(8,128)S(1)} %get-tuple-element.63), channel_id=1, source_target_pairs={{0,192},{64,0},{128,64},{192,128},{1,193},{65,1},{129,65},{193,129... | collective-permute-start | bytes 552968 | tf_op jit(solution)/shard_map/ppermute | solution.py:88
  37.8 4.2 %collective-permute-start.10 = (f32[96,128]{1,0:T(8,128)S(1)}, f32[96,128]{1,0:T(8,128)S(1)}, u32[]{:S(2)}, u32[]{:S(2)}) collective-permute-start(f32[96,128]{1,0:T(8,128)S(1)} %get-tuple-element.47), channel_id=1, source_target_pairs={{0,8},{8,16},{16,24},{24,32},{32,40},{40,48},{48,56},{56,0},{1,9},... | collective-permute-start | bytes 147464 | tf_op jit(solution)/shard_map/ppermute | solution.py:88
  40.8 2.9 %collective-permute-start.9 = (f32[96,128]{1,0:T(8,128)S(1)}, f32[96,128]{1,0:T(8,128)S(1)}, u32[]{:S(2)}, u32[]{:S(2)}) collective-permute-start(f32[96,128]{1,0:T(8,128)S(1)} %get-tuple-element.46), channel_id=1, source_target_pairs={{0,56},{8,0},{16,8},{24,16},{32,24},{40,32},{48,40},{56,48},{1,57}... | collective-permute-start | bytes 147464 | tf_op jit(solution)/shard_map/ppermute | solution.py:88
  44.3 4.1 %collective-permute-start.11 = (f32[80,128]{1,0:T(8,128)S(1)}, f32[80,128]{1,0:T(8,128)S(1)}, u32[]{:S(2)}, u32[]{:S(2)}) collective-permute-start(f32[80,128]{1,0:T(8,128)S(1)} %get-tuple-element.52), channel_id=1, source_target_pairs={{0,1},{1,2},{2,3},{3,4},{4,5},{5,6},{6,7},{7,0},{8,9},{9,10},{10,1... | collective-permute-start | bytes 122888 | tf_op jit(solution)/shard_map/ppermute | solution.py:88
  47.3 4.6 %collective-permute-start.12 = (f32[80,128]{1,0:T(8,128)S(1)}, f32[80,128]{1,0:T(8,128)S(1)}, u32[]{:S(2)}, u32[]{:S(2)}) collective-permute-start(f32[80,128]{1,0:T(8,128)S(1)} %get-tuple-element.53), channel_id=1, source_target_pairs={{0,7},{1,0},{2,1},{3,2},{4,3},{5,4},{6,5},{7,6},{8,15},{9,8},{10,9... | collective-permute-start | bytes 122888 | tf_op jit(solution)/shard_map/ppermute | solution.py:88

commit v7 on v6

--- a/solution.py
+++ b/solution.py
@@ -88,9 +88,11 @@
     return lax.ppermute(value, axis, [(i, (i + shift) % size) for i in range(size)])
 
 
-SLABS = [(0, x) for x in range(NXE)] + [(1, x) for x in range(1, NXE - 1)]
-SLAB = {slab: at for at, slab in enumerate(SLABS)}
-YROWS = 240
+OWN_SLABS = [(a, x) for a in range(2) for x in range(XH, XH + NX0)]
+SIDE_SLABS = [(a, x) for a in range(2) for x in range(a, NXE - a) if (a, x) not in OWN_SLABS]
+SLAB = {slab: (which, at) for which, slabs in enumerate((OWN_SLABS, SIDE_SLABS)) for at, slab in enumerate(slabs)}
+EXTRA = (8 * len(OWN_SLABS), 8 * len(SIDE_SLABS))
+YROWS = (EXTRA[0] + 16, EXTRA[1] + 16)
 
 
 def plane_of(own, low, high, which, x):
@@ -120,23 +122,31 @@
     down[XH - 1] = down[XH - 1] * (1.0 / (work[1] + 6.0)) * (1.0 / THETA)
 
 
-def fetch_own(after, s, c, s_out, c_out, done):
+def put_rows(src, slab, up, down):
+    which, at = SLAB[slab]
+    up[at * 8 : at * 8 + 8, :] = src[56:64, :]
+    down[at * 8 : at * 8 + 8, :] = src[0:8, :]
+    extra = EXTRA[which] + at
+    up[extra : extra + 1, :] = src[55:56, :]
+    down[extra : extra + 1, :] = src[8:9, :]
+
+
+def fetch_own(after, s, c, s_out, c_out, up, down, done):
     copies = [pltpu.make_async_copy(s, s_out, done.at[0]), pltpu.make_async_copy(c, c_out, done.at[1])]
     for copy in copies:
         copy.start()
     for copy in copies:
         copy.wait()
-
-
-def pack_y(s, c, high, low, up, down):
-    for (a, x), at in SLAB.items():
-        src = plane_of((s, c), low, high, a, x)
-        up[at * 8 : at * 8 + 8, :] = src[56:64, :]
-        down[at * 8 : at * 8 + 8, :] = src[0:8, :]
-        up[208 + at : 209 + at, :] = src[55:56, :]
-        down[208 + at : 209 + at, :] = src[8:9, :]
-    up[234:YROWS, :] = jnp.zeros((YROWS - 234, 128), F32)
-    down[234:YROWS, :] = jnp.zeros((YROWS - 234, 128), F32)
+    for a, x in OWN_SLABS:
+        put_rows((s_out, c_out)[a].at[x - XH], (a, x), up, down)
+
+
+def pack_y(high, low, up, down):
+    for a, x in SIDE_SLABS:
+        put_rows(plane_of(None, low, high, a, x), (a, x), up, down)
+    used = EXTRA[1] + len(SIDE_SLABS)
+    up[used:, :] = jnp.zeros((YROWS[1] - used, 128), F32)
+    down[used:, :] = jnp.zeros((YROWS[1] - used, 128), F32)
 
 
 def pack_wide(up, down, row, count, plane):
@@ -154,10 +164,12 @@
 
 
 def halo_rows(below, above, a, x):
-    at = SLAB[a, x]
+    which, at = SLAB[a, x]
+    below, above = below[which], above[which]
+    extra = EXTRA[which] + at
     row = rows_of((8, 128))
-    middle = jnp.where(row == 0, above[208 + at : 209 + at, :], 0.0)
-    middle = jnp.where(row == 7, below[208 + at : 209 + at, :], middle)
+    middle = jnp.where(row == 0, above[extra : extra + 1, :], 0.0)
+    middle = jnp.where(row == 7, below[extra : extra + 1, :], middle)
     return jnp.concatenate([above[at * 8 : at * 8 + 8, :], middle, below[at * 8 : at * 8 + 8, :]], 0)
 
 
@@ -165,10 +177,10 @@
     pack_wide(up, down, 0, 64, lambda a, x: plane_of((s, c), low, high, a, x)[...])
 
 
-def pack_z_halo(own_up, own_down, below, above, up, down):
+def pack_z_halo(own_up, own_down, below0, above0, below1, above1, up, down):
     up[:, 0:64, :] = own_up[...]
     down[:, 0:64, :] = own_down[...]
-    pack_wide(up, down, 64, 24, lambda a, x: halo_rows(below, above, a, x))
+    pack_wide(up, down, 64, 24, lambda a, x: halo_rows((below0, below1), (above0, above1), a, x))
 
 
 def fine_sweep(src, dst, res, diag, inverse, first, stop, pair):
@@ -187,7 +199,7 @@
 
 
 def fine_before(
-    s, c, high, low, below_y, above_y, below, above, sol, res, diag, inv, msg, da, db, dc, rows
+    s, c, high, low, below0, above0, below1, above1, below, above, sol, res, diag, inv, msg, da, db, dc, rows
 ):
     lane = lanes_of((R0, 128))
     for a in range(2):
@@ -197,7 +209,7 @@
             side = jnp.where(lane >= 128 - W, turn(left, 128 - W - W * x, 1), side)
             ref = (res, diag)[a]
             ref[x, 0:64, 0:128] = plane_of((s, c), low, high, a, x)[...]
-            ref[x, 64:88, 0:128] = halo_rows(below_y, above_y, a, x)
+            ref[x, 64:88, 0:128] = halo_rows((below0, below1), (above0, above1), a, x)
             ref[x, :, 128:256] = side
     lane40 = lanes_of((R1, 128))
 
@@ -264,7 +276,7 @@
     lax.fori_loop(0, planes, body, 0, unroll=True)
 
 
-def middle_before(own, low, high, far, res, sol, coef, low_res, low_coef, up, down, diag, inv, da, db, rows):
+def middle_before(own, low, far, high, res, sol, coef, low_res, low_coef, up, down, diag, inv, da, db, rows):
     gx = lax.axis_index("gx")
     size = lax.axis_size("gx")
     lane40 = lanes_of((R1, 128))
@@ -407,7 +419,7 @@
     return jnp.where(lane < 128 - width, v, turn(left, 128 - width - base, 1))
 
 
-def bottom(low_res, low_coef, above, below, left, right, sol2, res2, diag2, inv2, da2, db2):
+def bottom(low_res, low_coef, below, above, left, right, sol2, res2, diag2, inv2, da2, db2):
     in_yz = inside_yz((R2, 128), 16, 24, 32, 64)
     empty = jnp.zeros((R2, 128), F32)
     for buffer in (da2, db2):
@@ -435,7 +447,7 @@
 
 
 def middle_after(
-    sol2, res, sol, coef1, above, below, left, right, sol1, res1, diag1, inv1, da1, db1
+    sol2, res, sol, coef1, below, above, left, right, sol1, res1, diag1, inv1, da1, db1
 ):
     in_yz1 = inside_yz((Q1, 128), 32, 40, 64, 96)
     empty = jnp.zeros((Q1, 128), F32)
@@ -555,20 +567,21 @@
         scratch_shapes=[pltpu.VMEM((2, NY0, NZ0), F32), pltpu.SemaphoreType.DMA((6,))],
         compiler_params=pltpu.CompilerParams(vmem_limit_bytes=4 * MIB),
     )(s, c)
-    s, c = pl.pallas_call(
+    s, c, own_up, own_down = pl.pallas_call(
         fetch_own,
-        out_shape=[jax.ShapeDtypeStruct((NX0, NY0, NZ0), F32)] * 2,
+        out_shape=[jax.ShapeDtypeStruct((NX0, NY0, NZ0), F32)] * 2 + [jax.ShapeDtypeStruct((YROWS[0], 128), F32)] * 2,
         in_specs=[pl.BlockSpec(memory_space=pl.ANY)] * 3,
-        out_specs=[pl.BlockSpec(memory_space=pltpu.VMEM)] * 2,
+        out_specs=[pl.BlockSpec(memory_space=pltpu.VMEM)] * 4,
         scratch_shapes=[pltpu.SemaphoreType.DMA((2,))],
         compiler_params=pltpu.CompilerParams(vmem_limit_bytes=4 * MIB),
         cost_estimate=pl.CostEstimate(flops=0, bytes_accessed=3690000, transcendentals=0),
     )(up, s, c)
     low, high = ring(up, "gx", 1), ring(down, "gx", -1)
-    up, down = call(pack_y, 4, [(YROWS, 128)] * 2, [], s, c, high, low)
-    below_y, above_y = ring(up, "gy", 1), ring(down, "gy", -1)
+    below0, above0 = ring(own_up, "gy", 1), ring(own_down, "gy", -1)
+    up, down = call(pack_y, 4, [(YROWS[1], 128)] * 2, [], high, low)
+    below1, above1 = ring(up, "gy", 1), ring(down, "gy", -1)
     own_up, own_down = call(pack_z_own, 4, [(2, 64, 128)] * 2, [], s, c, high, low)
-    up, down = call(pack_z_halo, 4, [(2, R0, 128)] * 2, [], own_up, own_down, below_y, above_y)
+    up, down = call(pack_z_halo, 4, [(2, R0, 128)] * 2, [], own_up, own_down, below0, above0, below1, above1)
     below, above = ring(up, "gz", 1), ring(down, "gz", -1)
     big = (NXE, R0, 256)
     sol0, res0, diag0, inv0, msg = call(
@@ -576,7 +589,7 @@
         16,
         [(NX0, 64, 128), big, big, big, (200, 128)],
         [big, big, big, (8, 2, 80, 128)],
-        s, c, high, low, below_y, above_y, below, above,
+        s, c, high, low, below0, above0, below1, above1, below, above,
         micros=4.0,
     )
     low, high, far = ring(msg, "gx", 1), ring(msg, "gx", -1), ring(msg, "gx", 2)
@@ -596,7 +609,7 @@
         8,
         [mid, mid, mid, (8, 16, 128), (8, 16, 128), (96, 128), (96, 128)],
         [mid, mid, (18, R1, 128), (18, R1, 128), (16, 32, 128)],
-        msg, low, high, far,
+        msg, low, far, high,
         micros=2.0,
     )
     below, above = ring(up, "gy", 1), ring(down, "gy", -1)
@@ -607,14 +620,14 @@
     big = (NXE, Q0, 256)
     own = (NX0, NY0, NZ0)
     (sol2,) = call(
-        bottom, 4, [bot], [bot] * 3 + [(10, R2, 128)] * 2, res2, coef2, above, below, left, right
+        bottom, 4, [bot], [bot] * 3 + [(10, R2, 128)] * 2, res2, coef2, below, above, left, right
     )
     (sol1,) = call(
         middle_after,
         8,
         [(20, Q1, 128)],
         [mid] * 3 + [(18, Q1, 128)] * 2,
-        sol2, res1, sol1, coef1, above, below, left, right,
+        sol2, res1, sol1, coef1, below, above, left, right,
         micros=2.0,
     )
     return tuple(

time: 57.4 us -> 57 us (level)
  waiting for transfers between devices: 20.8 us -> 18.6 us
  starting transfers between devices: 20.3 us -> 22.1 us
    ppermute x15 -> x17, waiting for transfers between devices: 20.8 us -> 18.6 us  [ring(): lax.ppermute(value, axis, [(i, (i + shift) % size) for i in range(size)])]
    ppermute x15 -> x17, starting transfers between devices: 20.3 us -> 22.1 us  [ring(): lax.ppermute(value, axis, [(i, (i + shift) % size) for i in range(size)])]
  transfers between devices with their start and end apart: 15 -> 17, of which waited for: 11 -> 11; matrix products, arithmetic and copies ran while one was open for 0% -> 0% of each run, Pallas kernels for 12% -> 12%
where the time goes in v7:
time: 57 us; the launch traced here: 56.9 us
  starting transfers between devices  22.1 us (39%)
  waiting for transfers between devices  18.6 us (33%)
  Pallas kernels  15.4 us (27%)
  between operations  0.76 us (1%)
    ppermute x17, starting transfers between devices, ring(): lax.ppermute(value, axis, [(i, (i + shift) % size) for i in range(size)])  22.1 us
    ppermute x17, waiting for transfers between devices, ring(): lax.ppermute(value, axis, [(i, (i + shift) % size) for i in range(size)])  18.6 us
    pallas_call x11, Pallas kernels, call(): pl.pallas_call(body, out_shape=[jax.ShapeDtypeStruct(s, F32) for s in out...  13.3 us
  transfers between devices with their start and end apart: 17, of which 11 were waited for; matrix products, arithmetic and copies ran while one was open for 0% of the time, Pallas kernels for 12%

profile of v7, /device:TPU:71, one launch (start us, length us, event | category | flops | bytes accessed | tf_op | source)
XLA Modules:
  0.0 56.9 jit_solution(8794788913357349633)
XLA Ops:
  0.6 1.1 %shard_map.41 = (f32[5,64,128]{2,1,0:T(8,128)S(1)}, f32[5,64,128]{2,1,0:T(8,128)S(1)}) custom-call(f32[8,64,128]{2,1,0:T(8,128)} %s.3, f32[8,64,128]{2,1,0:T(8,128)} %c.3), custom_call_target="tpu_custom_call" | custom-call | tf_op jit(solution)/shard_map/pallas_call | solution.py:562
  1.7 1.4 %collective-permute-start.1 = (f32[5,64,128]{2,1,0:T(8,128)S(1)}, f32[5,64,128]{2,1,0:T(8,128)S(1)}, u32[]{:S(2)}, u32[]{:S(2)}) collective-permute-start(f32[5,64,128]{2,1,0:T(8,128)S(1)} %get-tuple-element.35.after), channel_id=1, source_target_pairs={{0,64},{64,128},{128,192},{192,0},{1,65},{65,129},{129,193},{193,1... | collective-permute-start | bytes 491528 | tf_op jit(solution)/shard_map/ppermute | solution.py:88
  3.1 1.5 %collective-permute-start = (f32[5,64,128]{2,1,0:T(8,128)S(1)}, f32[5,64,128]{2,1,0:T(8,128)S(1)}, u32[]{:S(2)}, u32[]{:S(2)}) collective-permute-start(f32[5,64,128]{2,1,0:T(8,128)S(1)} %get-tuple-element.38), channel_id=1, source_target_pairs={{0,192},{64,0},{128,64},{192,128},{1,193},{65,1},{129,65},{193,129... | collective-permute-start | bytes 491528 | tf_op jit(solution)/shard_map/ppermute | solution.py:88
  4.6 1.1 %shard_map.42 = (f32[8,64,128]{2,1,0:T(8,128)S(1)}, f32[8,64,128]{2,1,0:T(8,128)S(1)}, f32[144,128]{1,0:T(8,128)S(1)}, f32[144,128]{1,0:T(8,128)S(1)}) custom-call(f32[5,64,128]{2,1,0:T(8,128)S(1)} %get-tuple-element.35.after, f32[8,64,128]{2,1,0:T(8,128)} %s.3, f32[8,64,128]{2,1,0:T(8,128)} %c.3), custom_call_target="tpu_custom_call" | custom-call | bytes 3690000 | tf_op jit(solution)/shard_map/pallas_call | solution.py:570
  5.7 1.7 %collective-permute-start.2 = (f32[144,128]{1,0:T(8,128)S(1)}, f32[144,128]{1,0:T(8,128)S(1)}, u32[]{:S(2)}, u32[]{:S(2)}) collective-permute-start(f32[144,128]{1,0:T(8,128)S(1)} %get-tuple-element.39), channel_id=1, source_target_pairs={{0,8},{8,16},{16,24},{24,32},{32,40},{40,48},{48,56},{56,0},{1,9},... | collective-permute-start | bytes 221192 | tf_op jit(solution)/shard_map/ppermute | solution.py:88
  8.2 2.1 %collective-permute-start.4 = (f32[96,128]{1,0:T(8,128)S(1)}, f32[96,128]{1,0:T(8,128)S(1)}, u32[]{:S(2)}, u32[]{:S(2)}) collective-permute-start(f32[96,128]{1,0:T(8,128)S(1)} %get-tuple-element.41), channel_id=1, source_target_pairs={{0,8},{8,16},{16,24},{24,32},{32,40},{40,48},{48,56},{56,0},{1,9},... | collective-permute-start | bytes 147464 | tf_op jit(solution)/shard_map/ppermute | solution.py:88
  10.9 1.1 %collective-permute-done.3.above0 = f32[144,128]{1,0:T(8,128)S(1)} collective-permute-done((f32[144,128]{1,0:T(8,128)S(1)}, f32[144,128]{1,0:T(8,128)S(1)}, u32[]{:S(2)}, u32[]{:S(2)}) %collective-permute-start.3) | collective-permute-done | bytes 73760 | tf_op jit(solution)/shard_map/ppermute | solution.py:88
  12.0 2.5 %collective-permute-done.5.above1 = f32[96,128]{1,0:T(8,128)S(1)} collective-permute-done((f32[96,128]{1,0:T(8,128)S(1)}, f32[96,128]{1,0:T(8,128)S(1)}, u32[]{:S(2)}, u32[]{:S(2)}) %collective-permute-start.5) | collective-permute-done | bytes 49184 | tf_op jit(solution)/shard_map/ppermute | solution.py:88
  14.7 2.9 %collective-permute-start.6 = (f32[2,88,128]{2,1,0:T(8,128)S(1)}, f32[2,88,128]{2,1,0:T(8,128)S(1)}, u32[]{:S(2)}, u32[]{:S(2)}) collective-permute-start(f32[2,88,128]{2,1,0:T(8,128)S(1)} %get-tuple-element.45), channel_id=1, source_target_pairs={{0,1},{1,2},{2,3},{3,4},{4,5},{5,6},{6,7},{7,0},{8,9},{9,10},{10,1... | collective-permute-start | bytes 270344 | tf_op jit(solution)/shard_map/ppermute | solution.py:88
  17.6 1.6 %collective-permute-done.6.below = f32[2,88,128]{2,1,0:T(8,128)S(1)} collective-permute-done((f32[2,88,128]{2,1,0:T(8,128)S(1)}, f32[2,88,128]{2,1,0:T(8,128)S(1)}, u32[]{:S(2)}, u32[]{:S(2)}) %collective-permute-start.6) | collective-permute-done | bytes 90144 | tf_op jit(solution)/shard_map/ppermute | solution.py:88
  19.2 3.6 %collective-permute-done.7.above = f32[2,88,128]{2,1,0:T(8,128)S(1)} collective-permute-done((f32[2,88,128]{2,1,0:T(8,128)S(1)}, f32[2,88,128]{2,1,0:T(8,128)S(1)}, u32[]{:S(2)}, u32[]{:S(2)}) %collective-permute-start.7) | collective-permute-done | bytes 90144 | tf_op jit(solution)/shard_map/ppermute | solution.py:88
  22.8 4.0 %shard_map.46 = (f32[8,64,128]{2,1,0:T(8,128)S(1)}, f32[14,88,256]{2,1,0:T(8,128)S(1)}, f32[14,88,256]{2,1,0:T(8,128)S(1)}, f32[14,88,256]{2,1,0:T(8,128)S(1)}, f32[200,128]{1,0:T(8,128)S(1)}) custom-call(f32[8,64,128]{2,1,0:T(8,128)S(1)} %get-tuple-element.36.s, f32[8,64,128]{2,1,0:T(8,128)S(1)} %get-tuple-element.37.c, ...), custom_call_target="tpu_custom_call" | custom-call | bytes 14760000 | tf_op jit(solution)/shard_map/pallas_call | solution.py:75
  27.8 1.8 %collective-permute-start.10 = (f32[200,128]{1,0:T(8,128)S(1)}, f32[200,128]{1,0:T(8,128)S(1)}, u32[]{:S(2)}, u32[]{:S(2)}) collective-permute-start(f32[200,128]{1,0:T(8,128)S(1)} %get-tuple-element.47.own), channel_id=1, source_target_pairs={{0,192},{64,0},{128,64},{192,128},{1,193},{65,1},{129,65},{193,129... | collective-permute-start | bytes 307208 | tf_op jit(solution)/shard_map/ppermute | solution.py:88
  29.6 1.0 %collective-permute-start.9 = (f32[200,128]{1,0:T(8,128)S(1)}, f32[200,128]{1,0:T(8,128)S(1)}, u32[]{:S(2)}, u32[]{:S(2)}) collective-permute-start(f32[200,128]{1,0:T(8,128)S(1)} %get-tuple-element.47.own), channel_id=1, source_target_pairs={{0,128},{64,192},{128,0},{192,64},{1,129},{65,193},{129,1},{193,65... | collective-permute-start | bytes 307208 | tf_op jit(solution)/shard_map/ppermute | solution.py:88
  30.6 1.3 %collective-permute-done.8.low.after = f32[200,128]{1,0:T(8,128)S(1)} collective-permute-done((f32[200,128]{1,0:T(8,128)S(1)}, f32[200,128]{1,0:T(8,128)S(1)}, u32[]{:S(2)}, u32[]{:S(2)}) %collective-permute-start.8) | collective-permute-done | bytes 102432 | tf_op jit(solution)/shard_map/ppermute | solution.py:88
  32.3 2.7 %collective-permute-start.16 = (f32[360,128]{1,0:T(8,128)S(1)}, f32[360,128]{1,0:T(8,128)S(1)}, u32[]{:S(2)}, u32[]{:S(2)}) collective-permute-start(f32[360,128]{1,0:T(8,128)S(1)} %get-tuple-element.67), channel_id=1, source_target_pairs={{0,192},{64,0},{128,64},{192,128},{1,193},{65,1},{129,65},{193,129... | collective-permute-start | bytes 552968 | tf_op jit(solution)/shard_map/ppermute | solution.py:88
  35.4 2.0 %shard_map.47 = (f32[16,40,128]{2,1,0:T(8,128)S(1)}, f32[16,40,128]{2,1,0:T(8,128)S(1)}, f32[16,40,128]{2,1,0:T(8,128)S(1)}, f32[8,16,128]{2,1,0:T(8,128)S(1)}, ...) custom-call(f32[200,128]{1,0:T(8,128)S(1)} %get-tuple-element.47.own, ...), custom_call_target="tpu_custom_call" | custom-call | bytes 7380000 | tf_op jit(solution)/shard_map/pallas_call | solution.py:75
  37.4 3.0 %collective-permute-start.11 = (f32[96,128]{1,0:T(8,128)S(1)}, f32[96,128]{1,0:T(8,128)S(1)}, u32[]{:S(2)}, u32[]{:S(2)}) collective-permute-start(f32[96,128]{1,0:T(8,128)S(1)} %get-tuple-element.50), channel_id=1, source_target_pairs={{0,8},{8,16},{16,24},{24,32},{32,40},{40,48},{48,56},{56,0},{1,9},... | collective-permute-start | bytes 147464 | tf_op jit(solution)/shard_map/ppermute | solution.py:88
  41.6 1.8 %collective-permute-done.12.above = f32[96,128]{1,0:T(8,128)S(1)} collective-permute-done((f32[96,128]{1,0:T(8,128)S(1)}, f32[96,128]{1,0:T(8,128)S(1)}, u32[]{:S(2)}, u32[]{:S(2)}) %collective-permute-start.12) | collective-permute-done | bytes 49184 | tf_op jit(solution)/shard_map/ppermute | solution.py:88
  43.9 2.9 %collective-permute-start.13 = (f32[80,128]{1,0:T(8,128)S(1)}, f32[80,128]{1,0:T(8,128)S(1)}, u32[]{:S(2)}, u32[]{:S(2)}) collective-permute-start(f32[80,128]{1,0:T(8,128)S(1)} %get-tuple-element.56), channel_id=1, source_target_pairs={{0,1},{1,2},{2,3},{3,4},{4,5},{5,6},{6,7},{7,0},{8,9},{9,10},{10,1... | collective-permute-start | bytes 122888 | tf_op jit(solution)/shard_map/ppermute | solution.py:88
  46.8 1.1 %collective-permute-done.13.left = f32[80,128]{1,0:T(8,128)S(1)} collective-permute-done((f32[80,128]{1,0:T(8,128)S(1)}, f32[80,128]{1,0:T(8,128)S(1)}, u32[]{:S(2)}, u32[]{:S(2)}) %collective-permute-start.13) | collective-permute-done | bytes 40992 | tf_op jit(solution)/shard_map/ppermute | solution.py:88
  47.9 3.5 %collective-permute-done.14.right = f32[80,128]{1,0:T(8,128)S(1)} collective-permute-done((f32[80,128]{1,0:T(8,128)S(1)}, f32[80,128]{1,0:T(8,128)S(1)}, u32[]{:S(2)}, u32[]{:S(2)}) %collective-permute-start.14) | collective-permute-done | bytes 40992 | tf_op jit(solution)/shard_map/ppermute | solution.py:88
  52.1 1.4 %shard_map.51.sol1 = f32[20,48,128]{2,1,0:T(8,128)S(1)} custom-call(f32[8,32,128]{2,1,0:T(8,128)S(1)} %shard_map.50.sol2, f32[16,40,128]{2,1,0:T(8,128)S(1)} %get-tuple-element.52.res, f32[16,40,128]{2,1,0:T(8,128)S(1)} %get-tuple-element.53.sol, f32[16,40,128]{2,1,0:T(8,128)S(1)} %get-tuple-element.58.coef1, f32[96,128]{1,0:T(8,128)S(1)} %collective-permute-done.11.below, ...), custom_call_target="tpu_custom_call" | custom-call | bytes 7380000 | tf_op jit(solution)/shard_map/pallas_call | solution.py:75
  53.6 3.3 %shard_map.53 = (f32[8,64,128]{2,1,0:T(8,128)}, f32[8,64,128]{2,1,0:T(8,128)}) custom-call(f32[20,48,128]{2,1,0:T(8,128)S(1)} %shard_map.51.sol1, f32[8,64,128]{2,1,0:T(8,128)S(1)} %get-tuple-element.59.sol0, f32[8,72,256]{2,1,0:T(8,128)S(1)} %get-tuple-element.63.res_q, f32[14,72,256]{2,1,0:T(8,128)S(1)} %get-tuple-element.64.diag_q, ...), custom_call_target="tpu_custom_call" | custom-call | bytes 3690000 | tf_op jit(solution)/shard_map/pallas_call | solution.py:75
  (23 shorter events, 5.8 us)
Async XLA Ops:
  1.7 6.5 %collective-permute-start.1 = (f32[5,64,128]{2,1,0:T(8,128)S(1)}, f32[5,64,128]{2,1,0:T(8,128)S(1)}, u32[]{:S(2)}, u32[]{:S(2)}) collective-permute-start(f32[5,64,128]{2,1,0:T(8,128)S(1)} %get-tuple-element.35.after), channel_id=1, source_target_pairs={{0,64},{64,128},{128,192},{192,0},{1,65},{65,129},{129,193},{193,1... | collective-permute-start | bytes 491528 | tf_op jit(solution)/shard_map/ppermute | solution.py:88
  3.1 5.1 %collective-permute-start = (f32[5,64,128]{2,1,0:T(8,128)S(1)}, f32[5,64,128]{2,1,0:T(8,128)S(1)}, u32[]{:S(2)}, u32[]{:S(2)}) collective-permute-start(f32[5,64,128]{2,1,0:T(8,128)S(1)} %get-tuple-element.38), channel_id=1, source_target_pairs={{0,192},{64,0},{128,64},{192,128},{1,193},{65,1},{129,65},{193,129... | collective-permute-start | bytes 491528 | tf_op jit(solution)/shard_map/ppermute | solution.py:88
  5.7 5.2 %collective-permute-start.2 = (f32[144,128]{1,0:T(8,128)S(1)}, f32[144,128]{1,0:T(8,128)S(1)}, u32[]{:S(2)}, u32[]{:S(2)}) collective-permute-start(f32[144,128]{1,0:T(8,128)S(1)} %get-tuple-element.39), channel_id=1, source_target_pairs={{0,8},{8,16},{16,24},{24,32},{32,40},{40,48},{48,56},{56,0},{1,9},... | collective-permute-start | bytes 221192 | tf_op jit(solution)/shard_map/ppermute | solution.py:88
  7.4 4.6 %collective-permute-start.3 = (f32[144,128]{1,0:T(8,128)S(1)}, f32[144,128]{1,0:T(8,128)S(1)}, u32[]{:S(2)}, u32[]{:S(2)}) collective-permute-start(f32[144,128]{1,0:T(8,128)S(1)} %get-tuple-element.40), channel_id=1, source_target_pairs={{0,56},{8,0},{16,8},{24,16},{32,24},{40,32},{48,40},{56,48},{1,57}... | collective-permute-start | bytes 221192 | tf_op jit(solution)/shard_map/ppermute | solution.py:88
  8.2 3.8 %collective-permute-start.4 = (f32[96,128]{1,0:T(8,128)S(1)}, f32[96,128]{1,0:T(8,128)S(1)}, u32[]{:S(2)}, u32[]{:S(2)}) collective-permute-start(f32[96,128]{1,0:T(8,128)S(1)} %get-tuple-element.41), channel_id=1, source_target_pairs={{0,8},{8,16},{16,24},{24,32},{32,40},{40,48},{48,56},{56,0},{1,9},... | collective-permute-start | bytes 147464 | tf_op jit(solution)/shard_map/ppermute | solution.py:88
  10.4 4.1 %collective-permute-start.5 = (f32[96,128]{1,0:T(8,128)S(1)}, f32[96,128]{1,0:T(8,128)S(1)}, u32[]{:S(2)}, u32[]{:S(2)}) collective-permute-start(f32[96,128]{1,0:T(8,128)S(1)} %get-tuple-element.42), channel_id=1, source_target_pairs={{0,56},{8,0},{16,8},{24,16},{32,24},{40,32},{48,40},{56,48},{1,57}... | collective-permute-start | bytes 147464 | tf_op jit(solution)/shard_map/ppermute | solution.py:88
  14.7 4.5 %collective-permute-start.6 = (f32[2,88,128]{2,1,0:T(8,128)S(1)}, f32[2,88,128]{2,1,0:T(8,128)S(1)}, u32[]{:S(2)}, u32[]{:S(2)}) collective-permute-start(f32[2,88,128]{2,1,0:T(8,128)S(1)} %get-tuple-element.45), channel_id=1, source_target_pairs={{0,1},{1,2},{2,3},{3,4},{4,5},{5,6},{6,7},{7,0},{8,9},{9,10},{10,1... | collective-permute-start | bytes 270344 | tf_op jit(solution)/shard_map/ppermute | solution.py:88
  17.6 5.2 %collective-permute-start.7 = (f32[2,88,128]{2,1,0:T(8,128)S(1)}, f32[2,88,128]{2,1,0:T(8,128)S(1)}, u32[]{:S(2)}, u32[]{:S(2)}) collective-permute-start(f32[2,88,128]{2,1,0:T(8,128)S(1)} %get-tuple-element.46), channel_id=1, source_target_pairs={{0,7},{1,0},{2,1},{3,2},{4,3},{5,4},{6,5},{7,6},{8,15},{9,8},{10,9... | collective-permute-start | bytes 270344 | tf_op jit(solution)/shard_map/ppermute | solution.py:88
  26.8 5.1 %collective-permute-start.8 = (f32[200,128]{1,0:T(8,128)S(1)}, f32[200,128]{1,0:T(8,128)S(1)}, u32[]{:S(2)}, u32[]{:S(2)}) collective-permute-start(f32[200,128]{1,0:T(8,128)S(1)} %get-tuple-element.47.own), channel_id=1, source_target_pairs={{0,64},{64,128},{128,192},{192,0},{1,65},{65,129},{129,193},{193,1... | collective-permute-start | bytes 307208 | tf_op jit(solution)/shard_map/ppermute | solution.py:88
  27.8 7.1 %collective-permute-start.10 = (f32[200,128]{1,0:T(8,128)S(1)}, f32[200,128]{1,0:T(8,128)S(1)}, u32[]{:S(2)}, u32[]{:S(2)}) collective-permute-start(f32[200,128]{1,0:T(8,128)S(1)} %get-tuple-element.47.own), channel_id=1, source_target_pairs={{0,192},{64,0},{128,64},{192,128},{1,193},{65,1},{129,65},{193,129... | collective-permute-start | bytes 307208 | tf_op jit(solution)/shard_map/ppermute | solution.py:88
  29.6 5.9 %collective-permute-start.9 = (f32[200,128]{1,0:T(8,128)S(1)}, f32[200,128]{1,0:T(8,128)S(1)}, u32[]{:S(2)}, u32[]{:S(2)}) collective-permute-start(f32[200,128]{1,0:T(8,128)S(1)} %get-tuple-element.47.own), channel_id=1, source_target_pairs={{0,128},{64,192},{128,0},{192,64},{1,129},{65,193},{129,1},{193,65... | collective-permute-start | bytes 307208 | tf_op jit(solution)/shard_map/ppermute | solution.py:88
  32.2 21.4 %collective-permute-start.15 = (f32[360,128]{1,0:T(8,128)S(1)}, f32[360,128]{1,0:T(8,128)S(1)}, u32[]{:S(2)}, u32[]{:S(2)}) collective-permute-start(f32[360,128]{1,0:T(8,128)S(1)} %get-tuple-element.66), channel_id=1, source_target_pairs={{0,64},{64,128},{128,192},{192,0},{1,65},{65,129},{129,193},{193,1... | collective-permute-start | bytes 552968 | tf_op jit(solution)/shard_map/ppermute | solution.py:88
  32.3 21.3 %collective-permute-start.16 = (f32[360,128]{1,0:T(8,128)S(1)}, f32[360,128]{1,0:T(8,128)S(1)}, u32[]{:S(2)}, u32[]{:S(2)}) collective-permute-start(f32[360,128]{1,0:T(8,128)S(1)} %get-tuple-element.67), channel_id=1, source_target_pairs={{0,192},{64,0},{128,64},{192,128},{1,193},{65,1},{129,65},{193,129... | collective-permute-start | bytes 552968 | tf_op jit(solution)/shard_map/ppermute | solution.py:88
  37.4 4.2 %collective-permute-start.11 = (f32[96,128]{1,0:T(8,128)S(1)}, f32[96,128]{1,0:T(8,128)S(1)}, u32[]{:S(2)}, u32[]{:S(2)}) collective-permute-start(f32[96,128]{1,0:T(8,128)S(1)} %get-tuple-element.50), channel_id=1, source_target_pairs={{0,8},{8,16},{16,24},{24,32},{32,40},{40,48},{48,56},{56,0},{1,9},... | collective-permute-start | bytes 147464 | tf_op jit(solution)/shard_map/ppermute | solution.py:88
  40.4 2.9 %collective-permute-start.12 = (f32[96,128]{1,0:T(8,128)S(1)}, f32[96,128]{1,0:T(8,128)S(1)}, u32[]{:S(2)}, u32[]{:S(2)}) collective-permute-start(f32[96,128]{1,0:T(8,128)S(1)} %get-tuple-element.51), channel_id=1, source_target_pairs={{0,56},{8,0},{16,8},{24,16},{32,24},{40,32},{48,40},{56,48},{1,57}... | collective-permute-start | bytes 147464 | tf_op jit(solution)/shard_map/ppermute | solution.py:88
  43.9 4.0 %collective-permute-start.13 = (f32[80,128]{1,0:T(8,128)S(1)}, f32[80,128]{1,0:T(8,128)S(1)}, u32[]{:S(2)}, u32[]{:S(2)}) collective-permute-start(f32[80,128]{1,0:T(8,128)S(1)} %get-tuple-element.56), channel_id=1, source_target_pairs={{0,1},{1,2},{2,3},{3,4},{4,5},{5,6},{6,7},{7,0},{8,9},{9,10},{10,1... | collective-permute-start | bytes 122888 | tf_op jit(solution)/shard_map/ppermute | solution.py:88
  46.8 4.6 %collective-permute-start.14 = (f32[80,128]{1,0:T(8,128)S(1)}, f32[80,128]{1,0:T(8,128)S(1)}, u32[]{:S(2)}, u32[]{:S(2)}) collective-permute-start(f32[80,128]{1,0:T(8,128)S(1)} %get-tuple-element.57), channel_id=1, source_target_pairs={{0,7},{1,0},{2,1},{3,2},{4,3},{5,4},{6,5},{7,6},{8,15},{9,8},{10,9... | collective-permute-start | bytes 122888 | tf_op jit(solution)/shard_map/ppermute | solution.py:88

commit v8 on v7

--- a/solution.py
+++ b/solution.py
@@ -183,14 +183,16 @@
     pack_wide(up, down, 64, 24, lambda a, x: halo_rows((below0, below1), (above0, above1), a, x))
 
 
-def fine_sweep(src, dst, res, diag, inverse, first, stop, pair):
+def fine_sweep(src, dst, res, diag, inverse, first, stop, pair, parts):
     for x in range(first, stop):
         d = src[x]
         near = beside(d) + (src[x - 1] + src[x + 1])
-        r = res[x] - (diag[x] * d - near)
-        res[x] = r
-        if pair is not None:
-            dst[x] = pair[0] * d + (pair[1] * inverse[x]) * r
+        for low, high in parts:
+            part = d[low:high]
+            r = res[x, low:high, :] - (diag[x, low:high, :] * part - near[low:high])
+            res[x, low:high, :] = r
+            if pair is not None:
+                dst[x, low:high, :] = pair[0] * part + (pair[1] * inverse[x, low:high, :]) * r
 
 
 def to_q0(ref, x):
@@ -241,10 +243,14 @@
         da[x] = res[x] * inverse * (1.0 / THETA)
     pairs = coefficients(SWEEPS)
     steps = (da, db, dc)
+    for x in range(NXE):
+        db[x, 72:80, :] = jnp.zeros((8, 256), F32)
+        dc[x, 72:80, :] = jnp.zeros((8, 256), F32)
     for k in range(SWEEPS):
         last = k == SWEEPS - 1
         fine_sweep(
-            steps[k], None if last else steps[k + 1], res, diag, inv, k + 1, NXE - 1 - k, None if last else pairs[k]
+            steps[k], None if last else steps[k + 1], res, diag, inv, k + 1, NXE - 1 - k,
+            None if last else pairs[k], ((0, 72), (80, 88)),
         )
     for x in range(NX0):
         sol[x] = sum(d[XH + x, 0:64, 0:128] for d in steps)
@@ -545,7 +551,7 @@
     pairs = coefficients(SWEEPS)
     steps = (da0, db0, dc0)
     for k in range(SWEEPS - 1):
-        fine_sweep(steps[k], steps[k + 1], res0, diag_q, inv_q, k + 1, NXE - 1 - k, pairs[k])
+        fine_sweep(steps[k], steps[k + 1], res0, diag_q, inv_q, k + 1, NXE - 1 - k, pairs[k], ((0, 72),))
     for x in range(NX0):
         at = x + XH
         d = dc0[at]

time: 57 us -> 56.8 us (level)
  no operation moved by 1% of the time
where the time goes in v8:
time: 56.8 us; the launch traced here: 56.6 us
  starting transfers between devices  22.1 us (39%)
  waiting for transfers between devices  18.6 us (33%)
  Pallas kernels  15.2 us (27%)
  between operations  0.76 us (1%)
    ppermute x17, starting transfers between devices, ring(): lax.ppermute(value, axis, [(i, (i + shift) % size) for i in range(size)])  22.1 us
    ppermute x17, waiting for transfers between devices, ring(): lax.ppermute(value, axis, [(i, (i + shift) % size) for i in range(size)])  18.6 us
    pallas_call x11, Pallas kernels, call(): pl.pallas_call(body, out_shape=[jax.ShapeDtypeStruct(s, F32) for s in out...  13.1 us
  transfers between devices with their start and end apart: 17, of which 11 were waited for; matrix products, arithmetic and copies ran while one was open for 0% of the time, Pallas kernels for 12%

profile of v8, /device:TPU:71, one launch (start us, length us, event | category | flops | bytes accessed | tf_op | source)
XLA Modules:
  0.0 56.6 jit_solution(9029484260011206551)
XLA Ops:
  0.6 1.1 %shard_map.41 = (f32[5,64,128]{2,1,0:T(8,128)S(1)}, f32[5,64,128]{2,1,0:T(8,128)S(1)}) custom-call(f32[8,64,128]{2,1,0:T(8,128)} %s.3, f32[8,64,128]{2,1,0:T(8,128)} %c.3), custom_call_target="tpu_custom_call" | custom-call | tf_op jit(solution)/shard_map/pallas_call | solution.py:568
  1.7 1.4 %collective-permute-start.1 = (f32[5,64,128]{2,1,0:T(8,128)S(1)}, f32[5,64,128]{2,1,0:T(8,128)S(1)}, u32[]{:S(2)}, u32[]{:S(2)}) collective-permute-start(f32[5,64,128]{2,1,0:T(8,128)S(1)} %get-tuple-element.35.after), channel_id=1, source_target_pairs={{0,64},{64,128},{128,192},{192,0},{1,65},{65,129},{129,193},{193,1... | collective-permute-start | bytes 491528 | tf_op jit(solution)/shard_map/ppermute | solution.py:88
  3.1 1.5 %collective-permute-start = (f32[5,64,128]{2,1,0:T(8,128)S(1)}, f32[5,64,128]{2,1,0:T(8,128)S(1)}, u32[]{:S(2)}, u32[]{:S(2)}) collective-permute-start(f32[5,64,128]{2,1,0:T(8,128)S(1)} %get-tuple-element.38), channel_id=1, source_target_pairs={{0,192},{64,0},{128,64},{192,128},{1,193},{65,1},{129,65},{193,129... | collective-permute-start | bytes 491528 | tf_op jit(solution)/shard_map/ppermute | solution.py:88
  4.6 1.1 %shard_map.42 = (f32[8,64,128]{2,1,0:T(8,128)S(1)}, f32[8,64,128]{2,1,0:T(8,128)S(1)}, f32[144,128]{1,0:T(8,128)S(1)}, f32[144,128]{1,0:T(8,128)S(1)}) custom-call(f32[5,64,128]{2,1,0:T(8,128)S(1)} %get-tuple-element.35.after, f32[8,64,128]{2,1,0:T(8,128)} %s.3, f32[8,64,128]{2,1,0:T(8,128)} %c.3), custom_call_target="tpu_custom_call" | custom-call | bytes 3690000 | tf_op jit(solution)/shard_map/pallas_call | solution.py:576
  5.7 1.7 %collective-permute-start.2 = (f32[144,128]{1,0:T(8,128)S(1)}, f32[144,128]{1,0:T(8,128)S(1)}, u32[]{:S(2)}, u32[]{:S(2)}) collective-permute-start(f32[144,128]{1,0:T(8,128)S(1)} %get-tuple-element.39), channel_id=1, source_target_pairs={{0,8},{8,16},{16,24},{24,32},{32,40},{40,48},{48,56},{56,0},{1,9},... | collective-permute-start | bytes 221192 | tf_op jit(solution)/shard_map/ppermute | solution.py:88
  8.2 2.1 %collective-permute-start.4 = (f32[96,128]{1,0:T(8,128)S(1)}, f32[96,128]{1,0:T(8,128)S(1)}, u32[]{:S(2)}, u32[]{:S(2)}) collective-permute-start(f32[96,128]{1,0:T(8,128)S(1)} %get-tuple-element.41), channel_id=1, source_target_pairs={{0,8},{8,16},{16,24},{24,32},{32,40},{40,48},{48,56},{56,0},{1,9},... | collective-permute-start | bytes 147464 | tf_op jit(solution)/shard_map/ppermute | solution.py:88
  10.9 1.1 %collective-permute-done.3.above0 = f32[144,128]{1,0:T(8,128)S(1)} collective-permute-done((f32[144,128]{1,0:T(8,128)S(1)}, f32[144,128]{1,0:T(8,128)S(1)}, u32[]{:S(2)}, u32[]{:S(2)}) %collective-permute-start.3) | collective-permute-done | bytes 73760 | tf_op jit(solution)/shard_map/ppermute | solution.py:88
  12.0 2.5 %collective-permute-done.5.above1 = f32[96,128]{1,0:T(8,128)S(1)} collective-permute-done((f32[96,128]{1,0:T(8,128)S(1)}, f32[96,128]{1,0:T(8,128)S(1)}, u32[]{:S(2)}, u32[]{:S(2)}) %collective-permute-start.5) | collective-permute-done | bytes 49184 | tf_op jit(solution)/shard_map/ppermute | solution.py:88
  14.7 2.9 %collective-permute-start.6 = (f32[2,88,128]{2,1,0:T(8,128)S(1)}, f32[2,88,128]{2,1,0:T(8,128)S(1)}, u32[]{:S(2)}, u32[]{:S(2)}) collective-permute-start(f32[2,88,128]{2,1,0:T(8,128)S(1)} %get-tuple-element.45), channel_id=1, source_target_pairs={{0,1},{1,2},{2,3},{3,4},{4,5},{5,6},{6,7},{7,0},{8,9},{9,10},{10,1... | collective-permute-start | bytes 270344 | tf_op jit(solution)/shard_map/ppermute | solution.py:88
  17.6 1.6 %collective-permute-done.6.below = f32[2,88,128]{2,1,0:T(8,128)S(1)} collective-permute-done((f32[2,88,128]{2,1,0:T(8,128)S(1)}, f32[2,88,128]{2,1,0:T(8,128)S(1)}, u32[]{:S(2)}, u32[]{:S(2)}) %collective-permute-start.6) | collective-permute-done | bytes 90144 | tf_op jit(solution)/shard_map/ppermute | solution.py:88
  19.2 3.6 %collective-permute-done.7.above = f32[2,88,128]{2,1,0:T(8,128)S(1)} collective-permute-done((f32[2,88,128]{2,1,0:T(8,128)S(1)}, f32[2,88,128]{2,1,0:T(8,128)S(1)}, u32[]{:S(2)}, u32[]{:S(2)}) %collective-permute-start.7) | collective-permute-done | bytes 90144 | tf_op jit(solution)/shard_map/ppermute | solution.py:88
  22.8 3.8 %shard_map.46 = (f32[8,64,128]{2,1,0:T(8,128)S(1)}, f32[14,88,256]{2,1,0:T(8,128)S(1)}, f32[14,88,256]{2,1,0:T(8,128)S(1)}, f32[14,88,256]{2,1,0:T(8,128)S(1)}, f32[200,128]{1,0:T(8,128)S(1)}) custom-call(f32[8,64,128]{2,1,0:T(8,128)S(1)} %get-tuple-element.36.s, f32[8,64,128]{2,1,0:T(8,128)S(1)} %get-tuple-element.37.c, ...), custom_call_target="tpu_custom_call" | custom-call | bytes 14760000 | tf_op jit(solution)/shard_map/pallas_call | solution.py:75
  27.6 1.8 %collective-permute-start.10 = (f32[200,128]{1,0:T(8,128)S(1)}, f32[200,128]{1,0:T(8,128)S(1)}, u32[]{:S(2)}, u32[]{:S(2)}) collective-permute-start(f32[200,128]{1,0:T(8,128)S(1)} %get-tuple-element.47.own), channel_id=1, source_target_pairs={{0,192},{64,0},{128,64},{192,128},{1,193},{65,1},{129,65},{193,129... | collective-permute-start | bytes 307208 | tf_op jit(solution)/shard_map/ppermute | solution.py:88
  29.4 1.0 %collective-permute-start.9 = (f32[200,128]{1,0:T(8,128)S(1)}, f32[200,128]{1,0:T(8,128)S(1)}, u32[]{:S(2)}, u32[]{:S(2)}) collective-permute-start(f32[200,128]{1,0:T(8,128)S(1)} %get-tuple-element.47.own), channel_id=1, source_target_pairs={{0,128},{64,192},{128,0},{192,64},{1,129},{65,193},{129,1},{193,65... | collective-permute-start | bytes 307208 | tf_op jit(solution)/shard_map/ppermute | solution.py:88
  30.4 1.3 %collective-permute-done.8.low.after = f32[200,128]{1,0:T(8,128)S(1)} collective-permute-done((f32[200,128]{1,0:T(8,128)S(1)}, f32[200,128]{1,0:T(8,128)S(1)}, u32[]{:S(2)}, u32[]{:S(2)}) %collective-permute-start.8) | collective-permute-done | bytes 102432 | tf_op jit(solution)/shard_map/ppermute | solution.py:88
  32.1 2.7 %collective-permute-start.16 = (f32[360,128]{1,0:T(8,128)S(1)}, f32[360,128]{1,0:T(8,128)S(1)}, u32[]{:S(2)}, u32[]{:S(2)}) collective-permute-start(f32[360,128]{1,0:T(8,128)S(1)} %get-tuple-element.67), channel_id=1, source_target_pairs={{0,192},{64,0},{128,64},{192,128},{1,193},{65,1},{129,65},{193,129... | collective-permute-start | bytes 552968 | tf_op jit(solution)/shard_map/ppermute | solution.py:88
  35.2 2.0 %shard_map.47 = (f32[16,40,128]{2,1,0:T(8,128)S(1)}, f32[16,40,128]{2,1,0:T(8,128)S(1)}, f32[16,40,128]{2,1,0:T(8,128)S(1)}, f32[8,16,128]{2,1,0:T(8,128)S(1)}, ...) custom-call(f32[200,128]{1,0:T(8,128)S(1)} %get-tuple-element.47.own, ...), custom_call_target="tpu_custom_call" | custom-call | bytes 7380000 | tf_op jit(solution)/shard_map/pallas_call | solution.py:75
  37.2 3.0 %collective-permute-start.11 = (f32[96,128]{1,0:T(8,128)S(1)}, f32[96,128]{1,0:T(8,128)S(1)}, u32[]{:S(2)}, u32[]{:S(2)}) collective-permute-start(f32[96,128]{1,0:T(8,128)S(1)} %get-tuple-element.50), channel_id=1, source_target_pairs={{0,8},{8,16},{16,24},{24,32},{32,40},{40,48},{48,56},{56,0},{1,9},... | collective-permute-start | bytes 147464 | tf_op jit(solution)/shard_map/ppermute | solution.py:88
  41.4 1.8 %collective-permute-done.12.above = f32[96,128]{1,0:T(8,128)S(1)} collective-permute-done((f32[96,128]{1,0:T(8,128)S(1)}, f32[96,128]{1,0:T(8,128)S(1)}, u32[]{:S(2)}, u32[]{:S(2)}) %collective-permute-start.12) | collective-permute-done | bytes 49184 | tf_op jit(solution)/shard_map/ppermute | solution.py:88
  43.7 2.9 %collective-permute-start.13 = (f32[80,128]{1,0:T(8,128)S(1)}, f32[80,128]{1,0:T(8,128)S(1)}, u32[]{:S(2)}, u32[]{:S(2)}) collective-permute-start(f32[80,128]{1,0:T(8,128)S(1)} %get-tuple-element.56), channel_id=1, source_target_pairs={{0,1},{1,2},{2,3},{3,4},{4,5},{5,6},{6,7},{7,0},{8,9},{9,10},{10,1... | collective-permute-start | bytes 122888 | tf_op jit(solution)/shard_map/ppermute | solution.py:88
  46.6 1.1 %collective-permute-done.13.left = f32[80,128]{1,0:T(8,128)S(1)} collective-permute-done((f32[80,128]{1,0:T(8,128)S(1)}, f32[80,128]{1,0:T(8,128)S(1)}, u32[]{:S(2)}, u32[]{:S(2)}) %collective-permute-start.13) | collective-permute-done | bytes 40992 | tf_op jit(solution)/shard_map/ppermute | solution.py:88
  47.7 3.5 %collective-permute-done.14.right = f32[80,128]{1,0:T(8,128)S(1)} collective-permute-done((f32[80,128]{1,0:T(8,128)S(1)}, f32[80,128]{1,0:T(8,128)S(1)}, u32[]{:S(2)}, u32[]{:S(2)}) %collective-permute-start.14) | collective-permute-done | bytes 40992 | tf_op jit(solution)/shard_map/ppermute | solution.py:88
  51.9 1.4 %shard_map.51.sol1 = f32[20,48,128]{2,1,0:T(8,128)S(1)} custom-call(f32[8,32,128]{2,1,0:T(8,128)S(1)} %shard_map.50.sol2, f32[16,40,128]{2,1,0:T(8,128)S(1)} %get-tuple-element.52.res, f32[16,40,128]{2,1,0:T(8,128)S(1)} %get-tuple-element.53.sol, f32[16,40,128]{2,1,0:T(8,128)S(1)} %get-tuple-element.58.coef1, f32[96,128]{1,0:T(8,128)S(1)} %collective-permute-done.11.below, ...), custom_call_target="tpu_custom_call" | custom-call | bytes 7380000 | tf_op jit(solution)/shard_map/pallas_call | solution.py:75
  53.3 3.3 %shard_map.53 = (f32[8,64,128]{2,1,0:T(8,128)}, f32[8,64,128]{2,1,0:T(8,128)}) custom-call(f32[20,48,128]{2,1,0:T(8,128)S(1)} %shard_map.51.sol1, f32[8,64,128]{2,1,0:T(8,128)S(1)} %get-tuple-element.59.sol0, f32[8,72,256]{2,1,0:T(8,128)S(1)} %get-tuple-element.63.res_q, f32[14,72,256]{2,1,0:T(8,128)S(1)} %get-tuple-element.64.diag_q, ...), custom_call_target="tpu_custom_call" | custom-call | bytes 3690000 | tf_op jit(solution)/shard_map/pallas_call | solution.py:75
  (23 shorter events, 5.8 us)
Async XLA Ops:
  1.7 6.5 %collective-permute-start.1 = (f32[5,64,128]{2,1,0:T(8,128)S(1)}, f32[5,64,128]{2,1,0:T(8,128)S(1)}, u32[]{:S(2)}, u32[]{:S(2)}) collective-permute-start(f32[5,64,128]{2,1,0:T(8,128)S(1)} %get-tuple-element.35.after), channel_id=1, source_target_pairs={{0,64},{64,128},{128,192},{192,0},{1,65},{65,129},{129,193},{193,1... | collective-permute-start | bytes 491528 | tf_op jit(solution)/shard_map/ppermute | solution.py:88
  3.1 5.1 %collective-permute-start = (f32[5,64,128]{2,1,0:T(8,128)S(1)}, f32[5,64,128]{2,1,0:T(8,128)S(1)}, u32[]{:S(2)}, u32[]{:S(2)}) collective-permute-start(f32[5,64,128]{2,1,0:T(8,128)S(1)} %get-tuple-element.38), channel_id=1, source_target_pairs={{0,192},{64,0},{128,64},{192,128},{1,193},{65,1},{129,65},{193,129... | collective-permute-start | bytes 491528 | tf_op jit(solution)/shard_map/ppermute | solution.py:88
  5.7 5.2 %collective-permute-start.2 = (f32[144,128]{1,0:T(8,128)S(1)}, f32[144,128]{1,0:T(8,128)S(1)}, u32[]{:S(2)}, u32[]{:S(2)}) collective-permute-start(f32[144,128]{1,0:T(8,128)S(1)} %get-tuple-element.39), channel_id=1, source_target_pairs={{0,8},{8,16},{16,24},{24,32},{32,40},{40,48},{48,56},{56,0},{1,9},... | collective-permute-start | bytes 221192 | tf_op jit(solution)/shard_map/ppermute | solution.py:88
  7.4 4.6 %collective-permute-start.3 = (f32[144,128]{1,0:T(8,128)S(1)}, f32[144,128]{1,0:T(8,128)S(1)}, u32[]{:S(2)}, u32[]{:S(2)}) collective-permute-start(f32[144,128]{1,0:T(8,128)S(1)} %get-tuple-element.40), channel_id=1, source_target_pairs={{0,56},{8,0},{16,8},{24,16},{32,24},{40,32},{48,40},{56,48},{1,57}... | collective-permute-start | bytes 221192 | tf_op jit(solution)/shard_map/ppermute | solution.py:88
  8.2 3.8 %collective-permute-start.4 = (f32[96,128]{1,0:T(8,128)S(1)}, f32[96,128]{1,0:T(8,128)S(1)}, u32[]{:S(2)}, u32[]{:S(2)}) collective-permute-start(f32[96,128]{1,0:T(8,128)S(1)} %get-tuple-element.41), channel_id=1, source_target_pairs={{0,8},{8,16},{16,24},{24,32},{32,40},{40,48},{48,56},{56,0},{1,9},... | collective-permute-start | bytes 147464 | tf_op jit(solution)/shard_map/ppermute | solution.py:88
  10.4 4.1 %collective-permute-start.5 = (f32[96,128]{1,0:T(8,128)S(1)}, f32[96,128]{1,0:T(8,128)S(1)}, u32[]{:S(2)}, u32[]{:S(2)}) collective-permute-start(f32[96,128]{1,0:T(8,128)S(1)} %get-tuple-element.42), channel_id=1, source_target_pairs={{0,56},{8,0},{16,8},{24,16},{32,24},{40,32},{48,40},{56,48},{1,57}... | collective-permute-start | bytes 147464 | tf_op jit(solution)/shard_map/ppermute | solution.py:88
  14.7 4.5 %collective-permute-start.6 = (f32[2,88,128]{2,1,0:T(8,128)S(1)}, f32[2,88,128]{2,1,0:T(8,128)S(1)}, u32[]{:S(2)}, u32[]{:S(2)}) collective-permute-start(f32[2,88,128]{2,1,0:T(8,128)S(1)} %get-tuple-element.45), channel_id=1, source_target_pairs={{0,1},{1,2},{2,3},{3,4},{4,5},{5,6},{6,7},{7,0},{8,9},{9,10},{10,1... | collective-permute-start | bytes 270344 | tf_op jit(solution)/shard_map/ppermute | solution.py:88
  17.6 5.2 %collective-permute-start.7 = (f32[2,88,128]{2,1,0:T(8,128)S(1)}, f32[2,88,128]{2,1,0:T(8,128)S(1)}, u32[]{:S(2)}, u32[]{:S(2)}) collective-permute-start(f32[2,88,128]{2,1,0:T(8,128)S(1)} %get-tuple-element.46), channel_id=1, source_target_pairs={{0,7},{1,0},{2,1},{3,2},{4,3},{5,4},{6,5},{7,6},{8,15},{9,8},{10,9... | collective-permute-start | bytes 270344 | tf_op jit(solution)/shard_map/ppermute | solution.py:88
  26.6 5.1 %collective-permute-start.8 = (f32[200,128]{1,0:T(8,128)S(1)}, f32[200,128]{1,0:T(8,128)S(1)}, u32[]{:S(2)}, u32[]{:S(2)}) collective-permute-start(f32[200,128]{1,0:T(8,128)S(1)} %get-tuple-element.47.own), channel_id=1, source_target_pairs={{0,64},{64,128},{128,192},{192,0},{1,65},{65,129},{129,193},{193,1... | collective-permute-start | bytes 307208 | tf_op jit(solution)/shard_map/ppermute | solution.py:88
  27.6 7.1 %collective-permute-start.10 = (f32[200,128]{1,0:T(8,128)S(1)}, f32[200,128]{1,0:T(8,128)S(1)}, u32[]{:S(2)}, u32[]{:S(2)}) collective-permute-start(f32[200,128]{1,0:T(8,128)S(1)} %get-tuple-element.47.own), channel_id=1, source_target_pairs={{0,192},{64,0},{128,64},{192,128},{1,193},{65,1},{129,65},{193,129... | collective-permute-start | bytes 307208 | tf_op jit(solution)/shard_map/ppermute | solution.py:88
  29.4 5.9 %collective-permute-start.9 = (f32[200,128]{1,0:T(8,128)S(1)}, f32[200,128]{1,0:T(8,128)S(1)}, u32[]{:S(2)}, u32[]{:S(2)}) collective-permute-start(f32[200,128]{1,0:T(8,128)S(1)} %get-tuple-element.47.own), channel_id=1, source_target_pairs={{0,128},{64,192},{128,0},{192,64},{1,129},{65,193},{129,1},{193,65... | collective-permute-start | bytes 307208 | tf_op jit(solution)/shard_map/ppermute | solution.py:88
  32.0 21.4 %collective-permute-start.15 = (f32[360,128]{1,0:T(8,128)S(1)}, f32[360,128]{1,0:T(8,128)S(1)}, u32[]{:S(2)}, u32[]{:S(2)}) collective-permute-start(f32[360,128]{1,0:T(8,128)S(1)} %get-tuple-element.66), channel_id=1, source_target_pairs={{0,64},{64,128},{128,192},{192,0},{1,65},{65,129},{129,193},{193,1... | collective-permute-start | bytes 552968 | tf_op jit(solution)/shard_map/ppermute | solution.py:88
  32.1 21.3 %collective-permute-start.16 = (f32[360,128]{1,0:T(8,128)S(1)}, f32[360,128]{1,0:T(8,128)S(1)}, u32[]{:S(2)}, u32[]{:S(2)}) collective-permute-start(f32[360,128]{1,0:T(8,128)S(1)} %get-tuple-element.67), channel_id=1, source_target_pairs={{0,192},{64,0},{128,64},{192,128},{1,193},{65,1},{129,65},{193,129... | collective-permute-start | bytes 552968 | tf_op jit(solution)/shard_map/ppermute | solution.py:88
  37.2 4.2 %collective-permute-start.11 = (f32[96,128]{1,0:T(8,128)S(1)}, f32[96,128]{1,0:T(8,128)S(1)}, u32[]{:S(2)}, u32[]{:S(2)}) collective-permute-start(f32[96,128]{1,0:T(8,128)S(1)} %get-tuple-element.50), channel_id=1, source_target_pairs={{0,8},{8,16},{16,24},{24,32},{32,40},{40,48},{48,56},{56,0},{1,9},... | collective-permute-start | bytes 147464 | tf_op jit(solution)/shard_map/ppermute | solution.py:88
  40.2 2.9 %collective-permute-start.12 = (f32[96,128]{1,0:T(8,128)S(1)}, f32[96,128]{1,0:T(8,128)S(1)}, u32[]{:S(2)}, u32[]{:S(2)}) collective-permute-start(f32[96,128]{1,0:T(8,128)S(1)} %get-tuple-element.51), channel_id=1, source_target_pairs={{0,56},{8,0},{16,8},{24,16},{32,24},{40,32},{48,40},{56,48},{1,57}... | collective-permute-start | bytes 147464 | tf_op jit(solution)/shard_map/ppermute | solution.py:88
  43.7 4.0 %collective-permute-start.13 = (f32[80,128]{1,0:T(8,128)S(1)}, f32[80,128]{1,0:T(8,128)S(1)}, u32[]{:S(2)}, u32[]{:S(2)}) collective-permute-start(f32[80,128]{1,0:T(8,128)S(1)} %get-tuple-element.56), channel_id=1, source_target_pairs={{0,1},{1,2},{2,3},{3,4},{4,5},{5,6},{6,7},{7,0},{8,9},{9,10},{10,1... | collective-permute-start | bytes 122888 | tf_op jit(solution)/shard_map/ppermute | solution.py:88
  46.6 4.6 %collective-permute-start.14 = (f32[80,128]{1,0:T(8,128)S(1)}, f32[80,128]{1,0:T(8,128)S(1)}, u32[]{:S(2)}, u32[]{:S(2)}) collective-permute-start(f32[80,128]{1,0:T(8,128)S(1)} %get-tuple-element.57), channel_id=1, source_target_pairs={{0,7},{1,0},{2,1},{3,2},{4,3},{5,4},{6,5},{7,6},{8,15},{9,8},{10,9... | collective-permute-start | bytes 122888 | tf_op jit(solution)/shard_map/ppermute | solution.py:88

commit v9 on v8

--- a/solution.py
+++ b/solution.py
@@ -271,6 +271,10 @@
     def body(x, carry):
         d = src[x + 1]
         near = beside(d) + (src[x] + src[x + 2])
+        if pair is None:
+            own = slice(0, 32)
+            res[x, own, :] = res[x, own, :] - (diag[x, own, :] * d[own] - scale * near[own])
+            return carry
         r = res[x] - (diag[x] * d - scale * near)
         res[x] = r
         if pair is not None:

time: 56.8 us -> 56.7 us (level)
  no operation moved by 1% of the time
where the time goes in v9:
time: 56.7 us; the launch traced here: 56.6 us
  starting transfers between devices  22.1 us (39%)
  waiting for transfers between devices  18.6 us (33%)
  Pallas kernels  15.2 us (27%)
  between operations  0.76 us (1%)
    ppermute x17, starting transfers between devices, ring(): lax.ppermute(value, axis, [(i, (i + shift) % size) for i in range(size)])  22.1 us
    ppermute x17, waiting for transfers between devices, ring(): lax.ppermute(value, axis, [(i, (i + shift) % size) for i in range(size)])  18.6 us
    pallas_call x11, Pallas kernels, call(): pl.pallas_call(body, out_shape=[jax.ShapeDtypeStruct(s, F32) for s in out...  13 us
  transfers between devices with their start and end apart: 17, of which 11 were waited for; matrix products, arithmetic and copies ran while one was open for 0% of the time, Pallas kernels for 12%

profile of v9, /device:TPU:71, one launch (start us, length us, event | category | flops | bytes accessed | tf_op | source)
XLA Modules:
  0.0 56.6 jit_solution(18262571150026703463)
XLA Ops:
  0.6 1.1 %shard_map.41 = (f32[5,64,128]{2,1,0:T(8,128)S(1)}, f32[5,64,128]{2,1,0:T(8,128)S(1)}) custom-call(f32[8,64,128]{2,1,0:T(8,128)} %s.3, f32[8,64,128]{2,1,0:T(8,128)} %c.3), custom_call_target="tpu_custom_call" | custom-call | tf_op jit(solution)/shard_map/pallas_call | solution.py:572
  1.7 1.4 %collective-permute-start.1 = (f32[5,64,128]{2,1,0:T(8,128)S(1)}, f32[5,64,128]{2,1,0:T(8,128)S(1)}, u32[]{:S(2)}, u32[]{:S(2)}) collective-permute-start(f32[5,64,128]{2,1,0:T(8,128)S(1)} %get-tuple-element.35.after), channel_id=1, source_target_pairs={{0,64},{64,128},{128,192},{192,0},{1,65},{65,129},{129,193},{193,1... | collective-permute-start | bytes 491528 | tf_op jit(solution)/shard_map/ppermute | solution.py:88
  3.1 1.5 %collective-permute-start = (f32[5,64,128]{2,1,0:T(8,128)S(1)}, f32[5,64,128]{2,1,0:T(8,128)S(1)}, u32[]{:S(2)}, u32[]{:S(2)}) collective-permute-start(f32[5,64,128]{2,1,0:T(8,128)S(1)} %get-tuple-element.38), channel_id=1, source_target_pairs={{0,192},{64,0},{128,64},{192,128},{1,193},{65,1},{129,65},{193,129... | collective-permute-start | bytes 491528 | tf_op jit(solution)/shard_map/ppermute | solution.py:88
  4.6 1.1 %shard_map.42 = (f32[8,64,128]{2,1,0:T(8,128)S(1)}, f32[8,64,128]{2,1,0:T(8,128)S(1)}, f32[144,128]{1,0:T(8,128)S(1)}, f32[144,128]{1,0:T(8,128)S(1)}) custom-call(f32[5,64,128]{2,1,0:T(8,128)S(1)} %get-tuple-element.35.after, f32[8,64,128]{2,1,0:T(8,128)} %s.3, f32[8,64,128]{2,1,0:T(8,128)} %c.3), custom_call_target="tpu_custom_call" | custom-call | bytes 3690000 | tf_op jit(solution)/shard_map/pallas_call | solution.py:580
  5.7 1.7 %collective-permute-start.2 = (f32[144,128]{1,0:T(8,128)S(1)}, f32[144,128]{1,0:T(8,128)S(1)}, u32[]{:S(2)}, u32[]{:S(2)}) collective-permute-start(f32[144,128]{1,0:T(8,128)S(1)} %get-tuple-element.39), channel_id=1, source_target_pairs={{0,8},{8,16},{16,24},{24,32},{32,40},{40,48},{48,56},{56,0},{1,9},... | collective-permute-start | bytes 221192 | tf_op jit(solution)/shard_map/ppermute | solution.py:88
  8.2 2.1 %collective-permute-start.4 = (f32[96,128]{1,0:T(8,128)S(1)}, f32[96,128]{1,0:T(8,128)S(1)}, u32[]{:S(2)}, u32[]{:S(2)}) collective-permute-start(f32[96,128]{1,0:T(8,128)S(1)} %get-tuple-element.41), channel_id=1, source_target_pairs={{0,8},{8,16},{16,24},{24,32},{32,40},{40,48},{48,56},{56,0},{1,9},... | collective-permute-start | bytes 147464 | tf_op jit(solution)/shard_map/ppermute | solution.py:88
  10.9 1.1 %collective-permute-done.3.above0 = f32[144,128]{1,0:T(8,128)S(1)} collective-permute-done((f32[144,128]{1,0:T(8,128)S(1)}, f32[144,128]{1,0:T(8,128)S(1)}, u32[]{:S(2)}, u32[]{:S(2)}) %collective-permute-start.3) | collective-permute-done | bytes 73760 | tf_op jit(solution)/shard_map/ppermute | solution.py:88
  12.0 2.5 %collective-permute-done.5.above1 = f32[96,128]{1,0:T(8,128)S(1)} collective-permute-done((f32[96,128]{1,0:T(8,128)S(1)}, f32[96,128]{1,0:T(8,128)S(1)}, u32[]{:S(2)}, u32[]{:S(2)}) %collective-permute-start.5) | collective-permute-done | bytes 49184 | tf_op jit(solution)/shard_map/ppermute | solution.py:88
  14.7 2.9 %collective-permute-start.6 = (f32[2,88,128]{2,1,0:T(8,128)S(1)}, f32[2,88,128]{2,1,0:T(8,128)S(1)}, u32[]{:S(2)}, u32[]{:S(2)}) collective-permute-start(f32[2,88,128]{2,1,0:T(8,128)S(1)} %get-tuple-element.45), channel_id=1, source_target_pairs={{0,1},{1,2},{2,3},{3,4},{4,5},{5,6},{6,7},{7,0},{8,9},{9,10},{10,1... | collective-permute-start | bytes 270344 | tf_op jit(solution)/shard_map/ppermute | solution.py:88
  17.6 1.6 %collective-permute-done.6.below = f32[2,88,128]{2,1,0:T(8,128)S(1)} collective-permute-done((f32[2,88,128]{2,1,0:T(8,128)S(1)}, f32[2,88,128]{2,1,0:T(8,128)S(1)}, u32[]{:S(2)}, u32[]{:S(2)}) %collective-permute-start.6) | collective-permute-done | bytes 90144 | tf_op jit(solution)/shard_map/ppermute | solution.py:88
  19.2 3.6 %collective-permute-done.7.above = f32[2,88,128]{2,1,0:T(8,128)S(1)} collective-permute-done((f32[2,88,128]{2,1,0:T(8,128)S(1)}, f32[2,88,128]{2,1,0:T(8,128)S(1)}, u32[]{:S(2)}, u32[]{:S(2)}) %collective-permute-start.7) | collective-permute-done | bytes 90144 | tf_op jit(solution)/shard_map/ppermute | solution.py:88
  22.8 3.8 %shard_map.46 = (f32[8,64,128]{2,1,0:T(8,128)S(1)}, f32[14,88,256]{2,1,0:T(8,128)S(1)}, f32[14,88,256]{2,1,0:T(8,128)S(1)}, f32[14,88,256]{2,1,0:T(8,128)S(1)}, f32[200,128]{1,0:T(8,128)S(1)}) custom-call(f32[8,64,128]{2,1,0:T(8,128)S(1)} %get-tuple-element.36.s, f32[8,64,128]{2,1,0:T(8,128)S(1)} %get-tuple-element.37.c, ...), custom_call_target="tpu_custom_call" | custom-call | bytes 14760000 | tf_op jit(solution)/shard_map/pallas_call | solution.py:75
  27.6 1.8 %collective-permute-start.10 = (f32[200,128]{1,0:T(8,128)S(1)}, f32[200,128]{1,0:T(8,128)S(1)}, u32[]{:S(2)}, u32[]{:S(2)}) collective-permute-start(f32[200,128]{1,0:T(8,128)S(1)} %get-tuple-element.47.own), channel_id=1, source_target_pairs={{0,192},{64,0},{128,64},{192,128},{1,193},{65,1},{129,65},{193,129... | collective-permute-start | bytes 307208 | tf_op jit(solution)/shard_map/ppermute | solution.py:88
  29.4 1.0 %collective-permute-start.9 = (f32[200,128]{1,0:T(8,128)S(1)}, f32[200,128]{1,0:T(8,128)S(1)}, u32[]{:S(2)}, u32[]{:S(2)}) collective-permute-start(f32[200,128]{1,0:T(8,128)S(1)} %get-tuple-element.47.own), channel_id=1, source_target_pairs={{0,128},{64,192},{128,0},{192,64},{1,129},{65,193},{129,1},{193,65... | collective-permute-start | bytes 307208 | tf_op jit(solution)/shard_map/ppermute | solution.py:88
  30.4 1.3 %collective-permute-done.8.low.after = f32[200,128]{1,0:T(8,128)S(1)} collective-permute-done((f32[200,128]{1,0:T(8,128)S(1)}, f32[200,128]{1,0:T(8,128)S(1)}, u32[]{:S(2)}, u32[]{:S(2)}) %collective-permute-start.8) | collective-permute-done | bytes 102432 | tf_op jit(solution)/shard_map/ppermute | solution.py:88
  32.1 2.7 %collective-permute-start.16 = (f32[360,128]{1,0:T(8,128)S(1)}, f32[360,128]{1,0:T(8,128)S(1)}, u32[]{:S(2)}, u32[]{:S(2)}) collective-permute-start(f32[360,128]{1,0:T(8,128)S(1)} %get-tuple-element.67), channel_id=1, source_target_pairs={{0,192},{64,0},{128,64},{192,128},{1,193},{65,1},{129,65},{193,129... | collective-permute-start | bytes 552968 | tf_op jit(solution)/shard_map/ppermute | solution.py:88
  35.2 1.9 %shard_map.47 = (f32[16,40,128]{2,1,0:T(8,128)S(1)}, f32[16,40,128]{2,1,0:T(8,128)S(1)}, f32[16,40,128]{2,1,0:T(8,128)S(1)}, f32[8,16,128]{2,1,0:T(8,128)S(1)}, ...) custom-call(f32[200,128]{1,0:T(8,128)S(1)} %get-tuple-element.47.own, ...), custom_call_target="tpu_custom_call" | custom-call | bytes 7380000 | tf_op jit(solution)/shard_map/pallas_call | solution.py:75
  37.2 3.0 %collective-permute-start.11 = (f32[96,128]{1,0:T(8,128)S(1)}, f32[96,128]{1,0:T(8,128)S(1)}, u32[]{:S(2)}, u32[]{:S(2)}) collective-permute-start(f32[96,128]{1,0:T(8,128)S(1)} %get-tuple-element.50), channel_id=1, source_target_pairs={{0,8},{8,16},{16,24},{24,32},{32,40},{40,48},{48,56},{56,0},{1,9},... | collective-permute-start | bytes 147464 | tf_op jit(solution)/shard_map/ppermute | solution.py:88
  41.4 1.8 %collective-permute-done.12.above = f32[96,128]{1,0:T(8,128)S(1)} collective-permute-done((f32[96,128]{1,0:T(8,128)S(1)}, f32[96,128]{1,0:T(8,128)S(1)}, u32[]{:S(2)}, u32[]{:S(2)}) %collective-permute-start.12) | collective-permute-done | bytes 49184 | tf_op jit(solution)/shard_map/ppermute | solution.py:88
  43.7 2.9 %collective-permute-start.13 = (f32[80,128]{1,0:T(8,128)S(1)}, f32[80,128]{1,0:T(8,128)S(1)}, u32[]{:S(2)}, u32[]{:S(2)}) collective-permute-start(f32[80,128]{1,0:T(8,128)S(1)} %get-tuple-element.56), channel_id=1, source_target_pairs={{0,1},{1,2},{2,3},{3,4},{4,5},{5,6},{6,7},{7,0},{8,9},{9,10},{10,1... | collective-permute-start | bytes 122888 | tf_op jit(solution)/shard_map/ppermute | solution.py:88
  46.6 1.1 %collective-permute-done.13.left = f32[80,128]{1,0:T(8,128)S(1)} collective-permute-done((f32[80,128]{1,0:T(8,128)S(1)}, f32[80,128]{1,0:T(8,128)S(1)}, u32[]{:S(2)}, u32[]{:S(2)}) %collective-permute-start.13) | collective-permute-done | bytes 40992 | tf_op jit(solution)/shard_map/ppermute | solution.py:88
  47.7 3.5 %collective-permute-done.14.right = f32[80,128]{1,0:T(8,128)S(1)} collective-permute-done((f32[80,128]{1,0:T(8,128)S(1)}, f32[80,128]{1,0:T(8,128)S(1)}, u32[]{:S(2)}, u32[]{:S(2)}) %collective-permute-start.14) | collective-permute-done | bytes 40992 | tf_op jit(solution)/shard_map/ppermute | solution.py:88
  51.9 1.4 %shard_map.51.sol1 = f32[20,48,128]{2,1,0:T(8,128)S(1)} custom-call(f32[8,32,128]{2,1,0:T(8,128)S(1)} %shard_map.50.sol2, f32[16,40,128]{2,1,0:T(8,128)S(1)} %get-tuple-element.52.res, f32[16,40,128]{2,1,0:T(8,128)S(1)} %get-tuple-element.53.sol, f32[16,40,128]{2,1,0:T(8,128)S(1)} %get-tuple-element.58.coef1, f32[96,128]{1,0:T(8,128)S(1)} %collective-permute-done.11.below, ...), custom_call_target="tpu_custom_call" | custom-call | bytes 7380000 | tf_op jit(solution)/shard_map/pallas_call | solution.py:75
  53.3 3.3 %shard_map.53 = (f32[8,64,128]{2,1,0:T(8,128)}, f32[8,64,128]{2,1,0:T(8,128)}) custom-call(f32[20,48,128]{2,1,0:T(8,128)S(1)} %shard_map.51.sol1, f32[8,64,128]{2,1,0:T(8,128)S(1)} %get-tuple-element.59.sol0, f32[8,72,256]{2,1,0:T(8,128)S(1)} %get-tuple-element.63.res_q, f32[14,72,256]{2,1,0:T(8,128)S(1)} %get-tuple-element.64.diag_q, ...), custom_call_target="tpu_custom_call" | custom-call | bytes 3690000 | tf_op jit(solution)/shard_map/pallas_call | solution.py:75
  (23 shorter events, 5.8 us)
Async XLA Ops:
  1.7 6.5 %collective-permute-start.1 = (f32[5,64,128]{2,1,0:T(8,128)S(1)}, f32[5,64,128]{2,1,0:T(8,128)S(1)}, u32[]{:S(2)}, u32[]{:S(2)}) collective-permute-start(f32[5,64,128]{2,1,0:T(8,128)S(1)} %get-tuple-element.35.after), channel_id=1, source_target_pairs={{0,64},{64,128},{128,192},{192,0},{1,65},{65,129},{129,193},{193,1... | collective-permute-start | bytes 491528 | tf_op jit(solution)/shard_map/ppermute | solution.py:88
  3.1 5.1 %collective-permute-start = (f32[5,64,128]{2,1,0:T(8,128)S(1)}, f32[5,64,128]{2,1,0:T(8,128)S(1)}, u32[]{:S(2)}, u32[]{:S(2)}) collective-permute-start(f32[5,64,128]{2,1,0:T(8,128)S(1)} %get-tuple-element.38), channel_id=1, source_target_pairs={{0,192},{64,0},{128,64},{192,128},{1,193},{65,1},{129,65},{193,129... | collective-permute-start | bytes 491528 | tf_op jit(solution)/shard_map/ppermute | solution.py:88
  5.7 5.2 %collective-permute-start.2 = (f32[144,128]{1,0:T(8,128)S(1)}, f32[144,128]{1,0:T(8,128)S(1)}, u32[]{:S(2)}, u32[]{:S(2)}) collective-permute-start(f32[144,128]{1,0:T(8,128)S(1)} %get-tuple-element.39), channel_id=1, source_target_pairs={{0,8},{8,16},{16,24},{24,32},{32,40},{40,48},{48,56},{56,0},{1,9},... | collective-permute-start | bytes 221192 | tf_op jit(solution)/shard_map/ppermute | solution.py:88
  7.4 4.6 %collective-permute-start.3 = (f32[144,128]{1,0:T(8,128)S(1)}, f32[144,128]{1,0:T(8,128)S(1)}, u32[]{:S(2)}, u32[]{:S(2)}) collective-permute-start(f32[144,128]{1,0:T(8,128)S(1)} %get-tuple-element.40), channel_id=1, source_target_pairs={{0,56},{8,0},{16,8},{24,16},{32,24},{40,32},{48,40},{56,48},{1,57}... | collective-permute-start | bytes 221192 | tf_op jit(solution)/shard_map/ppermute | solution.py:88
  8.2 3.8 %collective-permute-start.4 = (f32[96,128]{1,0:T(8,128)S(1)}, f32[96,128]{1,0:T(8,128)S(1)}, u32[]{:S(2)}, u32[]{:S(2)}) collective-permute-start(f32[96,128]{1,0:T(8,128)S(1)} %get-tuple-element.41), channel_id=1, source_target_pairs={{0,8},{8,16},{16,24},{24,32},{32,40},{40,48},{48,56},{56,0},{1,9},... | collective-permute-start | bytes 147464 | tf_op jit(solution)/shard_map/ppermute | solution.py:88
  10.4 4.1 %collective-permute-start.5 = (f32[96,128]{1,0:T(8,128)S(1)}, f32[96,128]{1,0:T(8,128)S(1)}, u32[]{:S(2)}, u32[]{:S(2)}) collective-permute-start(f32[96,128]{1,0:T(8,128)S(1)} %get-tuple-element.42), channel_id=1, source_target_pairs={{0,56},{8,0},{16,8},{24,16},{32,24},{40,32},{48,40},{56,48},{1,57}... | collective-permute-start | bytes 147464 | tf_op jit(solution)/shard_map/ppermute | solution.py:88
  14.7 4.5 %collective-permute-start.6 = (f32[2,88,128]{2,1,0:T(8,128)S(1)}, f32[2,88,128]{2,1,0:T(8,128)S(1)}, u32[]{:S(2)}, u32[]{:S(2)}) collective-permute-start(f32[2,88,128]{2,1,0:T(8,128)S(1)} %get-tuple-element.45), channel_id=1, source_target_pairs={{0,1},{1,2},{2,3},{3,4},{4,5},{5,6},{6,7},{7,0},{8,9},{9,10},{10,1... | collective-permute-start | bytes 270344 | tf_op jit(solution)/shard_map/ppermute | solution.py:88
  17.6 5.2 %collective-permute-start.7 = (f32[2,88,128]{2,1,0:T(8,128)S(1)}, f32[2,88,128]{2,1,0:T(8,128)S(1)}, u32[]{:S(2)}, u32[]{:S(2)}) collective-permute-start(f32[2,88,128]{2,1,0:T(8,128)S(1)} %get-tuple-element.46), channel_id=1, source_target_pairs={{0,7},{1,0},{2,1},{3,2},{4,3},{5,4},{6,5},{7,6},{8,15},{9,8},{10,9... | collective-permute-start | bytes 270344 | tf_op jit(solution)/shard_map/ppermute | solution.py:88
  26.6 5.1 %collective-permute-start.8 = (f32[200,128]{1,0:T(8,128)S(1)}, f32[200,128]{1,0:T(8,128)S(1)}, u32[]{:S(2)}, u32[]{:S(2)}) collective-permute-start(f32[200,128]{1,0:T(8,128)S(1)} %get-tuple-element.47.own), channel_id=1, source_target_pairs={{0,64},{64,128},{128,192},{192,0},{1,65},{65,129},{129,193},{193,1... | collective-permute-start | bytes 307208 | tf_op jit(solution)/shard_map/ppermute | solution.py:88
  27.6 7.1 %collective-permute-start.10 = (f32[200,128]{1,0:T(8,128)S(1)}, f32[200,128]{1,0:T(8,128)S(1)}, u32[]{:S(2)}, u32[]{:S(2)}) collective-permute-start(f32[200,128]{1,0:T(8,128)S(1)} %get-tuple-element.47.own), channel_id=1, source_target_pairs={{0,192},{64,0},{128,64},{192,128},{1,193},{65,1},{129,65},{193,129... | collective-permute-start | bytes 307208 | tf_op jit(solution)/shard_map/ppermute | solution.py:88
  29.4 5.9 %collective-permute-start.9 = (f32[200,128]{1,0:T(8,128)S(1)}, f32[200,128]{1,0:T(8,128)S(1)}, u32[]{:S(2)}, u32[]{:S(2)}) collective-permute-start(f32[200,128]{1,0:T(8,128)S(1)} %get-tuple-element.47.own), channel_id=1, source_target_pairs={{0,128},{64,192},{128,0},{192,64},{1,129},{65,193},{129,1},{193,65... | collective-permute-start | bytes 307208 | tf_op jit(solution)/shard_map/ppermute | solution.py:88
  32.0 21.3 %collective-permute-start.15 = (f32[360,128]{1,0:T(8,128)S(1)}, f32[360,128]{1,0:T(8,128)S(1)}, u32[]{:S(2)}, u32[]{:S(2)}) collective-permute-start(f32[360,128]{1,0:T(8,128)S(1)} %get-tuple-element.66), channel_id=1, source_target_pairs={{0,64},{64,128},{128,192},{192,0},{1,65},{65,129},{129,193},{193,1... | collective-permute-start | bytes 552968 | tf_op jit(solution)/shard_map/ppermute | solution.py:88
  32.1 21.2 %collective-permute-start.16 = (f32[360,128]{1,0:T(8,128)S(1)}, f32[360,128]{1,0:T(8,128)S(1)}, u32[]{:S(2)}, u32[]{:S(2)}) collective-permute-start(f32[360,128]{1,0:T(8,128)S(1)} %get-tuple-element.67), channel_id=1, source_target_pairs={{0,192},{64,0},{128,64},{192,128},{1,193},{65,1},{129,65},{193,129... | collective-permute-start | bytes 552968 | tf_op jit(solution)/shard_map/ppermute | solution.py:88
  37.2 4.2 %collective-permute-start.11 = (f32[96,128]{1,0:T(8,128)S(1)}, f32[96,128]{1,0:T(8,128)S(1)}, u32[]{:S(2)}, u32[]{:S(2)}) collective-permute-start(f32[96,128]{1,0:T(8,128)S(1)} %get-tuple-element.50), channel_id=1, source_target_pairs={{0,8},{8,16},{16,24},{24,32},{32,40},{40,48},{48,56},{56,0},{1,9},... | collective-permute-start | bytes 147464 | tf_op jit(solution)/shard_map/ppermute | solution.py:88
  40.2 2.9 %collective-permute-start.12 = (f32[96,128]{1,0:T(8,128)S(1)}, f32[96,128]{1,0:T(8,128)S(1)}, u32[]{:S(2)}, u32[]{:S(2)}) collective-permute-start(f32[96,128]{1,0:T(8,128)S(1)} %get-tuple-element.51), channel_id=1, source_target_pairs={{0,56},{8,0},{16,8},{24,16},{32,24},{40,32},{48,40},{56,48},{1,57}... | collective-permute-start | bytes 147464 | tf_op jit(solution)/shard_map/ppermute | solution.py:88
  43.7 4.0 %collective-permute-start.13 = (f32[80,128]{1,0:T(8,128)S(1)}, f32[80,128]{1,0:T(8,128)S(1)}, u32[]{:S(2)}, u32[]{:S(2)}) collective-permute-start(f32[80,128]{1,0:T(8,128)S(1)} %get-tuple-element.56), channel_id=1, source_target_pairs={{0,1},{1,2},{2,3},{3,4},{4,5},{5,6},{6,7},{7,0},{8,9},{9,10},{10,1... | collective-permute-start | bytes 122888 | tf_op jit(solution)/shard_map/ppermute | solution.py:88
  46.6 4.6 %collective-permute-start.14 = (f32[80,128]{1,0:T(8,128)S(1)}, f32[80,128]{1,0:T(8,128)S(1)}, u32[]{:S(2)}, u32[]{:S(2)}) collective-permute-start(f32[80,128]{1,0:T(8,128)S(1)} %get-tuple-element.57), channel_id=1, source_target_pairs={{0,7},{1,0},{2,1},{3,2},{4,3},{5,4},{6,5},{7,6},{8,15},{9,8},{10,9... | collective-permute-start | bytes 122888 | tf_op jit(solution)/shard_map/ppermute | solution.py:88
